TPU v7x, 32 devices: a whole 2x2x4 slice. The times are simulated.
32 devices in a mesh: pole: 2 (over x), row: 8 (over z, y), col: 2 (over core).
Axes of the slice: x: 2, y: 2, z: 4, core: 2. Of those that a mesh axis runs over, the one named last changes fastest.
Arguments:
- inverse_pairs: bfloat16 [4, 12288, 12288], P('pole', 'row', 'col'), parts along dimension 0, may hold values from -0.09375 to 0.09375
- factor_rows: bfloat16 [4, 2, 2048, 256], P('pole', None, 'row', 'col'), parts along dimension 0, may hold values from -1.1953125 to 1.1953125
- diag_blocks: bfloat16 [4, 2, 256, 256], P('pole', None, None, 'col'), parts along dimension 0, may hold values from -6 to 6
- row_lists: int32 [2, 16], replicated, may hold values from 0 to 95, as said below
- block_order: int32 [96], replicated, may hold values from 0 to 95, each once
Outputs:
- inv_cols: float32 [4, 2, 12288, 256], P('pole', None, 'row', 'col'), parts along dimension 0
- schur_blocks: float32 [4, 2, 256, 256], P('pole', None, None, 'col'), parts along dimension 0
There are 2 independent parts, one for each index of `pole`. A program takes and returns all parts, laid end to end along the dimension named above; an argument that names none is the same for every part. Nothing has to cross between parts.
Inputs may be any that keep to these rules, and one draw needn't show every extreme that they name: `row_lists`: each of the 2 rows holds 16 different block numbers in increasing order, always including 0 and 95.
All inputs are finite; a program needn't handle non-finite values.
Results may differ from a plain program's by a relative error of at most 0.0003.
Values may be sent and summed in bfloat16 or wider, within the bound.
No kernel may reach another device: no remote copies, remote signals or barrier semaphores. Data moves between devices by JAX's collectives and lax.ppermute only.
A program may use at most 128 MiB of HBM per device.

v0:
```python
import functools
import math

import jax
import jax.numpy as jnp
from jax import lax
from jax.experimental import pallas as pl
from jax.experimental.pallas import tpu as pltpu
from jax.sharding import PartitionSpec as P

BLK = 128
CH = 2
DEPTH = CH * BLK
COL_ENTRY, COL_BLOCK, ROW_ENTRY, ROW_BLOCK, OFFSET, COUNTS = range(6)


def block_at(index, size=BLK):
    return pl.ds(pl.multiple_of(index * size, size), size)


def table_kernel(n_row, entries, sub, col_blocks, row_blocks, lists_ref, order_ref, tab_ref, where_ref):
    half = n_row // 2
    row, core = lax.axis_index("row"), lax.axis_index("col")
    place = jnp.where(lax.rem(row, 2) == 0, lax.div(row, 2), n_row - 1 - lax.div(row, 2))

    def invert(g, carry):
        where_ref[order_ref[g]] = g
        return carry

    lax.fori_loop(0, order_ref.shape[0], invert, 0, unroll=8)
    for k in range(tab_ref.shape[0]):

        def one(i, counts, k=k):
            listed, placed = counts
            chunk, at = lax.div(i, entries), lax.rem(i, entries)
            step = lax.div(chunk + 1, 2)
            step = jnp.where((lax.rem(chunk, 2) == 1) | (chunk == n_row - 1), step, -step)
            source = lax.rem(place - step + 2 * n_row, n_row)
            source = jnp.where(source < half, 2 * source, 2 * (n_row - 1 - source) + 1)
            first = source * (entries * sub) + at * sub
            block = where_ref[lists_ref[k, lax.div(first, BLK)]]
            tab_ref[k, OFFSET, i] = lax.rem(first, BLK)
            col, line = block - core * col_blocks, block - row * row_blocks
            is_col = (col >= 0) & (col < col_blocks)
            is_row = (line >= 0) & (line < row_blocks)

            @pl.when(is_col)
            def _():
                tab_ref[k, COL_ENTRY, listed] = i
                tab_ref[k, COL_BLOCK, listed] = col

            @pl.when(is_row)
            def _():
                tab_ref[k, ROW_ENTRY, placed] = i
                tab_ref[k, ROW_BLOCK, placed] = line

            return listed + is_col.astype(jnp.int32), placed + is_row.astype(jnp.int32)

        listed, placed = lax.fori_loop(0, n_row * entries, one, (jnp.int32(0), jnp.int32(0)), unroll=4)
        tab_ref[k, COUNTS, 0] = listed
        tab_ref[k, COUNTS, 1] = placed
        tab_ref[k, COUNTS, 2] = core


def make_table(n_row, entries, sub, col_blocks, row_blocks, row_lists, block_order):
    smem = pl.BlockSpec(memory_space=pltpu.SMEM)
    return pl.pallas_call(
        functools.partial(table_kernel, n_row, entries, sub, col_blocks, row_blocks),
        out_shape=jax.ShapeDtypeStruct((row_lists.shape[0], 6, max(n_row * entries, 3)), jnp.int32),
        in_specs=[smem] * 2,
        out_specs=smem,
        scratch_shapes=[pltpu.SMEM(block_order.shape, jnp.int32)],
        name="table",
    )(row_lists, block_order)


def start_rows(tab_ref, kind, k, to_ref, sems, halves, entries, early_count, sub):
    def one(at, carry):
        entry = tab_ref[k, kind, at]
        chunk, part = lax.div(entry, entries), lax.rem(entry, entries)
        rows = block_at(at)
        if sub < BLK:
            to_ref[k, rows, :] = jnp.zeros((BLK, to_ref.shape[2]), to_ref.dtype)
            rows = pl.ds(pl.multiple_of(at * BLK + tab_ref[k, OFFSET, entry], sub), sub)

        def copy(stack, chunk, there, p):
            here = stack.at[k, chunk, p, block_at(part, sub), :]
            pltpu.make_async_copy(here, there, sems.at[k]).start()

        for half, stacks in enumerate(halves):
            width = stacks[0].shape[4]
            for p in range(2):
                there = to_ref.at[k, rows, pl.ds((2 * half + p) * width, width)]

                @pl.when(chunk < early_count)
                def _(stacks=stacks, there=there, p=p):
                    copy(stacks[0], chunk, there, p)

                @pl.when(chunk >= early_count)
                def _(stacks=stacks, there=there, p=p):
                    copy(stacks[1], chunk - early_count, there, p)

        return carry

    return one


def wait_rows(k, to_ref, sems, width, sub, halves):
    def one(at, carry):
        there = to_ref.at[k, pl.ds(0, sub), pl.ds(0, 2 * halves * width)]
        pltpu.make_async_copy(there, there, sems.at[k]).wait()
        return carry

    return one


def product(x, w, x_rows, depth):
    width = w.shape[1] // 2
    real, imag = (
        jnp.dot(x[p, x_rows, depth], w[depth, :], preferred_element_type=jnp.float32) for p in range(2)
    )
    return imag[:, width:] - real[:, :width], -(real[:, width:] + imag[:, :width])


def values_kernel(entries, early_count, sub, tile, tab_ref, a_ref, own0, own1, sib0, sib1, *refs):
    mine_ref, theirs_ref, x_ref, w_ref, x_sems, w_sems = refs
    k, step = pl.program_id(0), pl.program_id(1)
    supernodes, tiles = pl.num_programs(0), pl.num_programs(1)
    width = mine_ref.shape[3]
    listed = tab_ref[k, COUNTS, 0]
    now = k * tiles + step

    def start(at):
        which, rows, buffer = lax.div(at, tiles), lax.rem(at, tiles), lax.rem(at, 2)

        def one(slot, carry):
            pltpu.make_async_copy(
                a_ref.at[:, block_at(rows, tile), block_at(tab_ref[which, COL_BLOCK, slot])],
                x_ref.at[buffer, :, :, block_at(slot)],
                x_sems.at[buffer],
            ).start()
            return carry

        lax.fori_loop(0, tab_ref[which, COUNTS, 0], one, 0)

    @pl.when(now == 0)
    def _():
        for which in range(w_ref.shape[0]):
            rows = start_rows(
                tab_ref, COL_ENTRY, which, w_ref, w_sems, ((own0, own1), (sib0, sib1)), entries, early_count, sub
            )
            lax.fori_loop(0, tab_ref[which, COUNTS, 0], rows, 0)
            if which == 0:
                start(now)

    @pl.when(now + 1 < supernodes * tiles)
    def _():
        start(now + 1)

    @pl.when(step == 0)
    def _():
        @pl.when(lax.rem(listed, CH) != 0)
        def _():
            w_ref[k, block_at(listed), :] = jnp.zeros((BLK, w_ref.shape[2]), w_ref.dtype)

        lax.fori_loop(0, listed, wait_rows(k, w_ref, w_sems, width, sub, 2), 0)

    buffer = lax.rem(now, 2)

    @pl.when(lax.rem(listed, CH) != 0)
    def _():
        x_ref[buffer, :, :, block_at(listed)] = jnp.zeros((2, tile, BLK), x_ref.dtype)

    def arrived(slot, carry):
        there = x_ref.at[buffer, :, :, block_at(slot)]
        pltpu.make_async_copy(there, there, x_sems.at[buffer]).wait()
        return carry

    lax.fori_loop(0, listed, arrived, 0)
    steps = lax.div(listed + (CH - 1), CH)

    @pl.when(steps == 0)
    def _():
        mine_ref[...] = jnp.zeros_like(mine_ref)
        theirs_ref[...] = jnp.zeros_like(theirs_ref)

    for count in range(1, w_ref.shape[1] // DEPTH + 1):

        @pl.when(steps == count)
        def _(count=count):
            for half, out_ref in enumerate((mine_ref, theirs_ref)):
                columns = w_ref.at[k, :, pl.ds(2 * half * width, 2 * width)]
                parts = product(x_ref.at[buffer], columns, pl.ds(0, tile), pl.ds(0, count * DEPTH))
                for q in range(2):
                    out_ref[0, q] = parts[q]


def gram_kernel(entries, early_count, sub, tab_ref, a_ref, own0, own1, sib0, sib1, *refs):
    mine_ref, theirs_ref, x_ref, w_ref, l_ref, v_ref, r_ref, acc_ref, x_sems, w_sems, l_sems = refs
    k = pl.program_id(0)
    own, sib = (own0, own1), (sib0, sib1)
    width = mine_ref.shape[4]
    chunk_rows = mine_ref.shape[3]
    listed, placed = tab_ref[k, COUNTS, 0], tab_ref[k, COUNTS, 1]

    def start_pair(which, pair):
        def one_place(place, carry):
            rows = block_at(tab_ref[which, ROW_BLOCK, place])

            def one(slot, inner):
                pltpu.make_async_copy(
                    a_ref.at[:, rows, block_at(tab_ref[which, COL_BLOCK, slot])],
                    x_ref.at[which, lax.rem(pair, 2), :, block_at(place - 2 * pair), block_at(slot)],
                    x_sems.at[which, lax.rem(pair, 2)],
                ).start()
                return inner

            return lax.fori_loop(0, tab_ref[which, COUNTS, 0], one, carry)

        lax.fori_loop(2 * pair, jnp.minimum(2 * pair + 2, tab_ref[which, COUNTS, 1]), one_place, 0)

    @pl.when(k == 0)
    def _():
        for which in range(x_ref.shape[0]):
            stacks = ((own, sib), entries, early_count, sub)
            there = tab_ref[which, COUNTS, 1]
            lax.fori_loop(0, there, start_rows(tab_ref, ROW_ENTRY, which, l_ref, l_sems, *stacks), 0)

            @pl.when(there > 0)
            def _(which=which, stacks=stacks):
                lax.fori_loop(
                    0, tab_ref[which, COUNTS, 0], start_rows(tab_ref, COL_ENTRY, which, w_ref, w_sems, *stacks), 0
                )

            start_pair(which, 0)

    acc_ref[...] = jnp.zeros_like(acc_ref)
    odd = lax.rem(listed, CH) != 0
    steps = lax.div(listed + (CH - 1), CH)
    lax.fori_loop(0, placed, wait_rows(k, l_ref, l_sems, width, sub, 2), 0)

    @pl.when(placed > 0)
    def _():
        lax.fori_loop(0, listed, wait_rows(k, w_ref, w_sems, width, sub, 2), 0)

    def one_pair(pair, carry):
        start_pair(k, pair + 1)
        buffer = lax.rem(pair, 2)

        @pl.when(odd)
        def _():
            x_ref[k, buffer, :, :, block_at(listed)] = jnp.zeros((2, 2 * BLK, BLK), x_ref.dtype)

        def one_place(place, inner):
            def arrived(slot, innermost):
                there = x_ref.at[k, buffer, :, block_at(place - 2 * pair), block_at(slot)]
                pltpu.make_async_copy(there, there, x_sems.at[k, buffer]).wait()
                return innermost

            return lax.fori_loop(0, listed, arrived, inner)

        lax.fori_loop(2 * pair, jnp.minimum(2 * pair + 2, placed), one_place, 0)
        for count in range(1, w_ref.shape[1] // DEPTH + 1):

            @pl.when(steps == count)
            def _(count=count):
                for half in range(2):
                    columns = w_ref.at[k, :, pl.ds(2 * half * width, 2 * width)]
                    parts = product(x_ref.at[k, buffer], columns, pl.ds(0, 2 * BLK), pl.ds(0, count * DEPTH))
                    for q in range(2):
                        v_ref[:, pl.ds((2 * half + q) * width, width)] = parts[q]

        @pl.when(2 * pair + 1 >= placed)
        def _():
            v_ref[pl.ds(BLK, BLK), :] = jnp.zeros((BLK, v_ref.shape[1]), v_ref.dtype)
            l_ref[k, block_at(2 * pair + 1), :] = jnp.zeros((BLK, l_ref.shape[2]), l_ref.dtype)

        left = l_ref[k, block_at(pair, 2 * BLK), :]
        rest = v_ref[...]
        for piece in range(3):
            kept = rest.astype(jnp.bfloat16)
            r_ref[pl.ds(piece * 2 * BLK, 2 * BLK), :] = kept
            rest = rest - kept.astype(jnp.float32)
        for p in range(2):
            turned = jnp.concatenate(
                [left[:, (2 * h + p) * width : (2 * h + p + 1) * width].T for h in range(2)], axis=0
            )
            turned = jnp.concatenate([turned] * 3, axis=1)
            acc_ref[p] += jnp.dot(turned, r_ref[...], preferred_element_type=jnp.float32)
        return carry

    @pl.when((listed > 0) & (placed > 0))
    def _():
        @pl.when(odd)
        def _():
            w_ref[k, block_at(listed), :] = jnp.zeros((BLK, w_ref.shape[2]), w_ref.dtype)

        lax.fori_loop(0, lax.div(placed + 1, 2), one_pair, 0)

    core = tab_ref[0, COUNTS, 2]
    per_half = width // chunk_rows
    for half in range(2):
        first = (core if half == 0 else 1 - core) * per_half
        for i in range(per_half):
            rows = pl.ds(half * width + i * chunk_rows, chunk_rows)
            for out_ref, at in ((mine_ref, 0), (theirs_ref, 2 * width)):
                real, imag = pl.ds(at, width), pl.ds(width + at, width)
                out_ref[first + i, 0, 0] = acc_ref[0, rows, real] - acc_ref[1, rows, imag]
                out_ref[first + i, 0, 1] = acc_ref[0, rows, imag] + acc_ref[1, rows, real]


def vmem_limit(scratch, blocks):
    held = [x for x in scratch if x.dtype in (jnp.bfloat16, jnp.float32)]
    size = sum(math.prod(x.shape) * jnp.dtype(x.dtype).itemsize for x in held)
    return size + 2 * sum(math.prod(shape) * 4 for shape in blocks) + 8 * 2**20


def make_values(tab, a, stacks, entries, sub):
    supernodes, early_count = stacks[0].shape[:2]
    rows, width = a.shape[1], stacks[0].shape[4]
    slots = tab.shape[2] + tab.shape[2] % CH
    tile = max(t for t in range(BLK, min(rows, 768) + 1, BLK) if rows % t == 0)
    out_spec = pl.BlockSpec((1, 2, tile, width), lambda k, m, _: (k, 0, m, 0))
    out = jax.ShapeDtypeStruct((supernodes, 2, rows, width), jnp.float32)
    scratch = [
        pltpu.VMEM((2, 2, tile, slots * BLK), jnp.bfloat16),
        pltpu.VMEM((supernodes, slots * BLK, 4 * width), jnp.bfloat16),
        pltpu.SemaphoreType.DMA((2,)),
        pltpu.SemaphoreType.DMA((supernodes,)),
    ]
    return pl.pallas_call(
        functools.partial(values_kernel, entries, early_count, sub, tile),
        out_shape=(out, out),
        grid_spec=pltpu.PrefetchScalarGridSpec(
            num_scalar_prefetch=1,
            grid=(supernodes, rows // tile),
            in_specs=[pl.BlockSpec(memory_space=pl.ANY)] * 5,
            out_specs=(out_spec, out_spec),
            scratch_shapes=scratch,
        ),
        compiler_params=pltpu.CompilerParams(vmem_limit_bytes=vmem_limit(scratch, [(2, tile, width)] * 2)),
        cost_estimate=pl.CostEstimate(
            flops=2 * supernodes * rows * slots * BLK * 4 * width, bytes_accessed=16 * 2**20, transcendentals=0
        ),
        name="values",
    )(tab, a, *stacks)


def make_gram(tab, a, stacks, entries, sub, shares):
    supernodes, early_count = stacks[0].shape[:2]
    rows, width = a.shape[1], stacks[0].shape[4]
    slots = tab.shape[2] + tab.shape[2] % CH
    places = min(slots, (rows // BLK) * (BLK // sub))
    places += places % 2
    out = jax.ShapeDtypeStruct((shares, supernodes, 2, 2 * width // shares, width), jnp.float32)
    out_spec = pl.BlockSpec((shares, 1) + out.shape[2:], lambda k, _: (0, k, 0, 0, 0))
    scratch = [
        pltpu.VMEM((supernodes, 2, 2, 2 * BLK, slots * BLK), jnp.bfloat16),
        pltpu.VMEM((supernodes, slots * BLK, 4 * width), jnp.bfloat16),
        pltpu.VMEM((supernodes, places * BLK, 4 * width), jnp.bfloat16),
        pltpu.VMEM((2 * BLK, 4 * width), jnp.float32),
        pltpu.VMEM((3 * 2 * BLK, 4 * width), jnp.bfloat16),
        pltpu.VMEM((2, 2 * width, 4 * width), jnp.float32),
        pltpu.SemaphoreType.DMA((supernodes, 2)),
        pltpu.SemaphoreType.DMA((supernodes,)),
        pltpu.SemaphoreType.DMA((supernodes,)),
    ]
    return pl.pallas_call(
        functools.partial(gram_kernel, entries, early_count, sub),
        out_shape=(out, out),
        grid_spec=pltpu.PrefetchScalarGridSpec(
            num_scalar_prefetch=1,
            grid=(supernodes,),
            in_specs=[pl.BlockSpec(memory_space=pl.ANY)] * 5,
            out_specs=(out_spec, out_spec),
            scratch_shapes=scratch,
        ),
        compiler_params=pltpu.CompilerParams(vmem_limit_bytes=vmem_limit(scratch, [out.shape] * 2)),
        cost_estimate=pl.CostEstimate(
            flops=supernodes * 2 * BLK * slots * 2 * BLK * 4 * width, bytes_accessed=8 * 2**20, transcendentals=0
        ),
        name="gram",
    )(tab, a, *stacks)


def scatter_sum(total, n_row, beside):
    half = n_row // 2
    row = lax.axis_index("row")
    level, odd = row // 2, row % 2
    pairs = total.reshape((half, 2) + total.shape[1:])
    came = []
    for d in range(1, half):
        route = [(i, (i + 2 * d) % n_row) for i in range(n_row)]
        sent = lax.dynamic_index_in_dim(pairs, (level + d) % half, 0, keepdims=False)
        came.append(lax.ppermute(sent, "row", route))
    *came, beside = lax.optimization_barrier((*came, beside))
    kept = lax.dynamic_index_in_dim(pairs, level, 0, keepdims=False)
    for x in came:
        kept = kept + x
    route = [(i, i ^ 1) for i in range(n_row)]
    sent = lax.dynamic_index_in_dim(kept, 1 - odd, 0, keepdims=False)
    last, beside = lax.optimization_barrier((lax.ppermute(sent, "row", route), beside))
    return lax.dynamic_index_in_dim(kept, odd, 0, keepdims=False) + last, beside


def local(n_row, inverse_pairs, factor_rows, diag_blocks, row_lists, block_order):
    supernodes = row_lists.shape[0]
    local_rows, local_cols = inverse_pairs.shape[1:]
    per_chip = factor_rows.shape[2]
    sub = min(BLK, per_chip)
    entries = per_chip // sub
    half = n_row // 2
    cycle = list(range(0, n_row, 2)) + list(range(n_row - 1, 0, -2))
    ahead = [(cycle[i], cycle[(i + 1) % n_row]) for i in range(n_row)]
    behind = [(b, a) for a, b in ahead]
    swap = [(0, 1), (1, 0)]

    tab = make_table(n_row, entries, sub, local_cols // BLK, local_rows // BLK, row_lists, block_order)

    chunks = [[factor_rows[k]] for k in range(supernodes)]
    up = [factor_rows[k] for k in range(supernodes)]
    down = list(up)
    for d in range(1, half):
        for k in range(supernodes):
            up[k] = lax.ppermute(up[k], "row", ahead)
            down[k] = lax.ppermute(down[k], "row", behind)
            chunks[k] += [up[k], down[k]]
        if d == 1:
            up[0], tab = lax.optimization_barrier((up[0], tab))
    for k in range(supernodes):
        last = [lax.ppermute(up[k][0:1], "row", ahead), lax.ppermute(down[k][1:2], "row", behind)]
        chunks[k].append(jnp.concatenate(last, axis=0))
    early = max(1, n_row - 3)
    own = [
        jnp.stack([jnp.stack(chunks[k][:early]) for k in range(supernodes)]),
        jnp.stack([jnp.stack(chunks[k][early:]) for k in range(supernodes)]),
    ]
    stacks = own + [lax.ppermute(x, "col", swap) for x in own]

    mine, theirs = make_gram(tab, inverse_pairs, stacks, entries, sub, n_row)
    total = mine + lax.ppermute(theirs, "col", swap)
    total, tab = lax.optimization_barrier((total, tab))
    mine, theirs = make_values(tab, inverse_pairs, stacks, entries, sub)
    share, theirs = scatter_sum(total, n_row, theirs)
    values = mine + lax.ppermute(theirs, "col", swap)
    shares = lax.all_to_all(jnp.broadcast_to(share[None], total.shape), "row", 0, 0, tiled=True)
    gram = jnp.moveaxis(shares, 0, 2).reshape(diag_blocks.shape)
    return (values, diag_blocks.astype(jnp.float32) - gram)


def solution(mesh):
    in_specs = (
        P("pole", "row", "col"),
        P("pole", None, "row", "col"),
        P("pole", None, None, "col"),
        P(),
        P(),
    )
    out_specs = (P("pole", None, "row", "col"), P("pole", None, None, "col"))
    body = functools.partial(local, mesh.shape["row"])
    return jax.shard_map(body, mesh=mesh, in_specs=in_specs, out_specs=out_specs, check_vma=False)
```

profile of v0, /device:TPU:0, one launch (start us, length us, event | category | flops | bytes accessed | tf_op | source)
XLA Modules:
  0.0 97.9 jit_solution(15446090967945254245)
XLA Ops:
  1.7 3.1 %collective-permute-start = (bf16[2,256,128]{2,1,0:T(8,128)(2,1)S(1)}, bf16[2,256,128]{2,1,0:T(8,128)(2,1)S(1)}, u32[]{:S(2)}, u32[]{:S(2)}) collective-permute-start(bf16[2,256,128]{2,1,0:T(8,128)(2,1)S(1)} %get-tuple-element.36), channel_id=1, source_target_pairs={{0,4},{4,8},{8,12},{12,14},{14,10},{10,6},{6,2},{2,0},{1,5},{5,9},... | collective-permute-start | bytes 393224 | tf_op jit(solution)/shard_map/ppermute | solution.py:425
  4.7 1.6 %collective-permute-start.4 = (bf16[2,256,128]{2,1,0:T(8,128)(2,1)S(1)}, bf16[2,256,128]{2,1,0:T(8,128)(2,1)S(1)}, u32[]{:S(2)}, u32[]{:S(2)}) collective-permute-start(bf16[2,256,128]{2,1,0:T(8,128)(2,1)S(1)} %get-tuple-element.35), channel_id=1, source_target_pairs={{0,4},{4,8},{8,12},{12,14},{14,10},{10,6},{6,2},{2,0},{1,5},{5,9},... | collective-permute-start | bytes 393224 | tf_op jit(solution)/shard_map/ppermute | solution.py:425
  6.8 2.4 %table.1.tab_ref = s32[2,6,16]{2,1,0:T(8,128)} custom-call(s32[2,16]{1,0:T(2,128)} %lists_ref.1, s32[96]{0:T(128)} %order_ref.1), custom_call_target="tpu_custom_call" | custom-call | tf_op jit(solution)/shard_map/table/pallas_call | solution.py:67
  9.2 2.0 %collective-permute-start.2 = (bf16[2,256,128]{2,1,0:T(8,128)(2,1)S(1)}, bf16[2,256,128]{2,1,0:T(8,128)(2,1)S(1)}, u32[]{:S(2)}, u32[]{:S(2)}) collective-permute-start(bf16[2,256,128]{2,1,0:T(8,128)(2,1)S(1)} %collective-permute-done), channel_id=1, source_target_pairs={{0,4},{4,8},{8,12},{12,14},{14,10},{10,6},{6,2},{2,0},{1,5},{5,9},... | collective-permute-start | bytes 393224 | tf_op jit(solution)/shard_map/ppermute | solution.py:425
  11.2 1.7 %collective-permute-start.6 = (bf16[2,256,128]{2,1,0:T(8,128)(2,1)S(1)}, bf16[2,256,128]{2,1,0:T(8,128)(2,1)S(1)}, u32[]{:S(2)}, u32[]{:S(2)}) collective-permute-start(bf16[2,256,128]{2,1,0:T(8,128)(2,1)S(1)} %collective-permute-done.4), channel_id=1, source_target_pairs={{0,4},{4,8},{8,12},{12,14},{14,10},{10,6},{6,2},{2,0},{1,5},{5,9},... | collective-permute-start | bytes 393224 | tf_op jit(solution)/shard_map/ppermute | solution.py:425
  13.8 1.3 %collective-permute-start.3 = (bf16[2,256,128]{2,1,0:T(8,128)(2,1)S(1)}, bf16[2,256,128]{2,1,0:T(8,128)(2,1)S(1)}, u32[]{:S(2)}, u32[]{:S(2)}) collective-permute-start(bf16[2,256,128]{2,1,0:T(8,128)(2,1)S(1)} %collective-permute-done.1), channel_id=1, source_target_pairs={{4,0},{8,4},{12,8},{14,12},{10,14},{6,10},{2,6},{0,2},{5,1},{9,5},... | collective-permute-start | bytes 393224 | tf_op jit(solution)/shard_map/ppermute | solution.py:426
  15.1 1.9 %collective-permute-done.6 = bf16[2,256,128]{2,1,0:T(8,128)(2,1)S(1)} collective-permute-done((bf16[2,256,128]{2,1,0:T(8,128)(2,1)S(1)}, bf16[2,256,128]{2,1,0:T(8,128)(2,1)S(1)}, u32[]{:S(2)}, u32[]{:S(2)}) %collective-permute-start.6) | collective-permute-done | bytes 131104 | tf_op jit(solution)/shard_map/ppermute | solution.py:425
  17.0 1.5 %collective-permute-start.12 = (bf16[2,256,128]{2,1,0:T(8,128)(2,1)S(1)}, bf16[2,256,128]{2,1,0:T(8,128)(2,1)S(1)}, u32[]{:S(2)}, u32[]{:S(2)}) collective-permute-start(bf16[2,256,128]{2,1,0:T(8,128)(2,1)S(1)} %collective-permute-done.6), channel_id=1, source_target_pairs={{0,4},{4,8},{8,12},{12,14},{14,10},{10,6},{6,2},{2,0},{1,5},{5,9},... | collective-permute-start | bytes 393224 | tf_op jit(solution)/shard_map/ppermute | solution.py:425
  19.2 1.6 %collective-permute-start.8 = (bf16[2,256,128]{2,1,0:T(8,128)(2,1)S(1)}, bf16[2,256,128]{2,1,0:T(8,128)(2,1)S(1)}, u32[]{:S(2)}, u32[]{:S(2)}) collective-permute-start(bf16[2,256,128]{2,1,0:T(8,128)(2,1)S(1)} %collective-permute-done.2), channel_id=1, source_target_pairs={{0,4},{4,8},{8,12},{12,14},{14,10},{10,6},{6,2},{2,0},{1,5},{5,9},... | collective-permute-start | bytes 393224 | tf_op jit(solution)/shard_map/ppermute | solution.py:425
  21.4 2.6 %collective-permute-done.13 = bf16[2,256,128]{2,1,0:T(8,128)(2,1)S(1)} collective-permute-done((bf16[2,256,128]{2,1,0:T(8,128)(2,1)S(1)}, bf16[2,256,128]{2,1,0:T(8,128)(2,1)S(1)}, u32[]{:S(2)}, u32[]{:S(2)}) %collective-permute-start.13) | collective-permute-done | bytes 131104 | tf_op jit(solution)/shard_map/ppermute | solution.py:426
  26.3 1.1 %collective-permute-start.11 = (bf16[1,256,128]{2,1,0:T(8,128)(2,1)S(1)}, bf16[1,256,128]{2,1,0:T(8,128)(2,1)S(1)}, u32[]{:S(2)}, u32[]{:S(2)}) collective-permute-start(bf16[1,256,128]{2,1,0:T(8,128)(2,1)S(1)} %slice.27), channel_id=1, source_target_pairs={{4,0},{8,4},{12,8},{14,12},{10,14},{6,10},{2,6},{0,2},{5,1},{9,5},... | collective-permute-start | bytes 196616 | tf_op jit(solution)/shard_map/ppermute | solution.py:431
  29.4 1.4 %collective-permute-done.11 = bf16[1,256,128]{2,1,0:T(8,128)(2,1)S(1)} collective-permute-done((bf16[1,256,128]{2,1,0:T(8,128)(2,1)S(1)}, bf16[1,256,128]{2,1,0:T(8,128)(2,1)S(1)}, u32[]{:S(2)}, u32[]{:S(2)}) %collective-permute-start.11) | collective-permute-done | bytes 65568 | tf_op jit(solution)/shard_map/ppermute | solution.py:431
  32.1 2.3 %collective-permute-done.17.sib1 = bf16[2,3,2,256,128]{4,3,2,1,0:T(8,128)(2,1)S(1)} collective-permute-done((bf16[2,3,2,256,128]{4,3,2,1,0:T(8,128)(2,1)S(1)}, bf16[2,3,2,256,128]{4,3,2,1,0:T(8,128)(2,1)S(1)}, u32[]{:S(2)}, u32[]{:S(2)}) %collective-permute-start.17) | collective-permute-done | bytes 786464 | tf_op jit(solution)/shard_map/ppermute | solution.py:438
  34.4 9.7 %gram.1 = (f32[8,2,2,32,128]{4,3,2,1,0:T(8,128)S(1)}, f32[8,2,2,32,128]{4,3,2,1,0:T(8,128)}) custom-call(s32[2,6,16]{2,1,0:T(8,128)S(1)} %copy-done.5, bf16[2,1536,6144]{2,1,0:T(8,128)(2,1)} %a_ref.3, bf16[2,5,2,256,128]{4,3,2,1,0:T(8,128)(2,1)S(1)} %pad_maximum_fusion.own0, bf16[2,3,2,256,128]{4,3,2,1,0:T(8,128)(2,1)S(1)} %pad_maximum_fusion.1.own1, ...), custom_call_target="tpu_custom_call" | custom-call | flops 1073741824 | bytes 8388608 | tf_op jit(solution)/shard_map/gram/pallas_call | solution.py:368
  44.9 2.2 %collective-permute-done.18 = f32[8,2,2,32,128]{4,3,2,1,0:T(8,128)} collective-permute-done((f32[8,2,2,32,128]{4,3,2,1,0:T(8,128)}, f32[8,2,2,32,128]{4,3,2,1,0:T(8,128)}, u32[]{:S(2)}, u32[]{:S(2)}) %collective-permute-start.18) | collective-permute-done | bytes 524320 | tf_op jit(solution)/shard_map/ppermute | solution.py:441
  47.1 1.3 %add.62 = f32[8,2,2,32,128]{4,3,2,1,0:T(8,128)S(1)} add(f32[8,2,2,32,128]{4,3,2,1,0:T(8,128)} %copy-done.4, f32[8,2,2,32,128]{4,3,2,1,0:T(8,128)} %collective-permute-done.18) | non-fusion elementwise | flops 131072 | bytes 1572864 | tf_op jit(solution)/shard_map/add | solution.py:441
  49.5 2.8 %collective-permute-start.21 = (f32[2,2,2,32,128]{4,3,2,1,0:T(8,128)S(1)}, f32[2,2,2,32,128]{4,3,2,1,0:T(8,128)S(1)}, u32[]{:S(2)}, u32[]{:S(2)}) collective-permute-start(f32[2,2,2,32,128]{4,3,2,1,0:T(8,128)S(1)} %get-tuple-element.30), channel_id=1, source_target_pairs={{0,12},{2,14},{4,0},{6,2},{8,4},{10,6},{12,8},{14,10},{1,13},{3,15... | collective-permute-start | bytes 393224 | tf_op jit(solution)/shard_map/ppermute | solution.py:395
  52.3 1.1 %copy-done.3 = bf16[2,3,2,256,128]{4,3,2,1,0:T(8,128)(2,1)S(1)} copy-done((bf16[2,3,2,256,128]{4,3,2,1,0:T(8,128)(2,1)S(1)}, bf16[2,3,2,256,128]{4,3,2,1,0:T(8,128)(2,1)}, u32[]{:S(2)}) %copy-start.3) | copy-done | bytes 786456
  53.5 13.4 %values.1 = (f32[2,2,1536,128]{3,2,1,0:T(8,128)S(1)}, f32[2,2,1536,128]{3,2,1,0:T(8,128)}) custom-call(s32[2,6,16]{2,1,0:T(8,128)S(1)} %copy-done.5, bf16[2,1536,6144]{2,1,0:T(8,128)(2,1)} %a_ref.3, bf16[2,5,2,256,128]{4,3,2,1,0:T(8,128)(2,1)S(1)} %pad_maximum_fusion.own0, bf16[2,3,2,256,128]{4,3,2,1,0:T(8,128)(2,1)S(1)} %pad_maximum_fusion.1.own1, ...), custom_call_target="tpu_custom_call" | custom-call | flops 6442450944 | bytes 16777216 | tf_op jit(solution)/shard_map/values/pallas_call | solution.py:331
  66.8 1.6 %copy-done = f32[2,2,1536,128]{3,2,1,0:T(8,128)} copy-done((f32[2,2,1536,128]{3,2,1,0:T(8,128)}, f32[2,2,1536,128]{3,2,1,0:T(8,128)S(1)}, u32[]{:S(2)}) %copy-start) | copy-done | bytes 3145752
  68.6 3.0 %collective-permute-start.22 = (f32[2,2,32,128]{3,2,1,0:T(8,128)S(1)}, f32[2,2,32,128]{3,2,1,0:T(8,128)}, u32[]{:S(2)}, u32[]{:S(2)}) collective-permute-start(f32[2,2,32,128]{3,2,1,0:T(8,128)S(1)} %dynamic-slice_bitcast_fusion.3), channel_id=1, source_target_pairs={{0,2},{2,0},{4,6},{6,4},{8,10},{10,8},{12,14},{14,12},{1,3},{3,1},... | collective-permute-start | bytes 196616 | tf_op jit(solution)/shard_map/ppermute | solution.py:402
  71.5 2.4 %collective-permute-done.22 = f32[2,2,32,128]{3,2,1,0:T(8,128)} collective-permute-done((f32[2,2,32,128]{3,2,1,0:T(8,128)S(1)}, f32[2,2,32,128]{3,2,1,0:T(8,128)}, u32[]{:S(2)}, u32[]{:S(2)}) %collective-permute-start.22) | collective-permute-done | bytes 65568 | tf_op jit(solution)/shard_map/ppermute | solution.py:402
  74.8 18.3 %all_to_all.5 = f32[8,2,2,32,128]{4,3,2,1,0:T(8,128)S(1)} all-to-all(f32[8,2,2,32,128]{4,3,2,1,0:T(8,128)S(1)} %broadcast_in_dim.2), channel_id=1, replica_groups=mesh['pole'=2,'row'=8,'col'=2] {'row'}, dimensions={0} | all-to-all | bytes 1048576 | tf_op jit(solution)/shard_map/all_to_all | solution.py:446
  94.0 3.9 %add.78 = f32[2,2,1536,128]{3,2,1,0:T(8,128)} add(f32[2,2,1536,128]{3,2,1,0:T(8,128)S(1)} %copy-done.1, f32[2,2,1536,128]{3,2,1,0:T(8,128)} %collective-permute-done.23) | non-fusion elementwise | flops 786432 | bytes 9437184 | tf_op jit(solution)/shard_map/add | solution.py:445
  (70 shorter events, 12.8 us)
Async XLA Ops:
  1.7 7.5 %collective-permute-start = (bf16[2,256,128]{2,1,0:T(8,128)(2,1)S(1)}, bf16[2,256,128]{2,1,0:T(8,128)(2,1)S(1)}, u32[]{:S(2)}, u32[]{:S(2)}) collective-permute-start(bf16[2,256,128]{2,1,0:T(8,128)(2,1)S(1)} %get-tuple-element.36), channel_id=1, source_target_pairs={{0,4},{4,8},{8,12},{12,14},{14,10},{10,6},{6,2},{2,0},{1,5},{5,9},... | collective-permute-start | bytes 393224 | tf_op jit(solution)/shard_map/ppermute | solution.py:425
  4.7 6.5 %collective-permute-start.4 = (bf16[2,256,128]{2,1,0:T(8,128)(2,1)S(1)}, bf16[2,256,128]{2,1,0:T(8,128)(2,1)S(1)}, u32[]{:S(2)}, u32[]{:S(2)}) collective-permute-start(bf16[2,256,128]{2,1,0:T(8,128)(2,1)S(1)} %get-tuple-element.35), channel_id=1, source_target_pairs={{0,4},{4,8},{8,12},{12,14},{14,10},{10,6},{6,2},{2,0},{1,5},{5,9},... | collective-permute-start | bytes 393224 | tf_op jit(solution)/shard_map/ppermute | solution.py:425
  6.3 6.7 %collective-permute-start.5 = (bf16[2,256,128]{2,1,0:T(8,128)(2,1)S(1)}, bf16[2,256,128]{2,1,0:T(8,128)(2,1)S(1)}, u32[]{:S(2)}, u32[]{:S(2)}) collective-permute-start(bf16[2,256,128]{2,1,0:T(8,128)(2,1)S(1)} %get-tuple-element.35), channel_id=1, source_target_pairs={{4,0},{8,4},{12,8},{14,12},{10,14},{6,10},{2,6},{0,2},{5,1},{9,5},... | collective-permute-start | bytes 393224 | tf_op jit(solution)/shard_map/ppermute | solution.py:426
  6.8 7.0 %collective-permute-start.1 = (bf16[2,256,128]{2,1,0:T(8,128)(2,1)S(1)}, bf16[2,256,128]{2,1,0:T(8,128)(2,1)S(1)}, u32[]{:S(2)}, u32[]{:S(2)}) collective-permute-start(bf16[2,256,128]{2,1,0:T(8,128)(2,1)S(1)} %get-tuple-element.36), channel_id=1, source_target_pairs={{4,0},{8,4},{12,8},{14,12},{10,14},{6,10},{2,6},{0,2},{5,1},{9,5},... | collective-permute-start | bytes 393224 | tf_op jit(solution)/shard_map/ppermute | solution.py:426
  9.2 10.0 %collective-permute-start.2 = (bf16[2,256,128]{2,1,0:T(8,128)(2,1)S(1)}, bf16[2,256,128]{2,1,0:T(8,128)(2,1)S(1)}, u32[]{:S(2)}, u32[]{:S(2)}) collective-permute-start(bf16[2,256,128]{2,1,0:T(8,128)(2,1)S(1)} %collective-permute-done), channel_id=1, source_target_pairs={{0,4},{4,8},{8,12},{12,14},{14,10},{10,6},{6,2},{2,0},{1,5},{5,9},... | collective-permute-start | bytes 393224 | tf_op jit(solution)/shard_map/ppermute | solution.py:425
  11.2 5.8 %collective-permute-start.6 = (bf16[2,256,128]{2,1,0:T(8,128)(2,1)S(1)}, bf16[2,256,128]{2,1,0:T(8,128)(2,1)S(1)}, u32[]{:S(2)}, u32[]{:S(2)}) collective-permute-start(bf16[2,256,128]{2,1,0:T(8,128)(2,1)S(1)} %collective-permute-done.4), channel_id=1, source_target_pairs={{0,4},{4,8},{8,12},{12,14},{14,10},{10,6},{6,2},{2,0},{1,5},{5,9},... | collective-permute-start | bytes 393224 | tf_op jit(solution)/shard_map/ppermute | solution.py:425
  13.0 5.6 %collective-permute-start.7 = (bf16[2,256,128]{2,1,0:T(8,128)(2,1)S(1)}, bf16[2,256,128]{2,1,0:T(8,128)(2,1)S(1)}, u32[]{:S(2)}, u32[]{:S(2)}) collective-permute-start(bf16[2,256,128]{2,1,0:T(8,128)(2,1)S(1)} %collective-permute-done.5), channel_id=1, source_target_pairs={{4,0},{8,4},{12,8},{14,12},{10,14},{6,10},{2,6},{0,2},{5,1},{9,5},... | collective-permute-start | bytes 393224 | tf_op jit(solution)/shard_map/ppermute | solution.py:426
  13.8 7.0 %collective-permute-start.3 = (bf16[2,256,128]{2,1,0:T(8,128)(2,1)S(1)}, bf16[2,256,128]{2,1,0:T(8,128)(2,1)S(1)}, u32[]{:S(2)}, u32[]{:S(2)}) collective-permute-start(bf16[2,256,128]{2,1,0:T(8,128)(2,1)S(1)} %collective-permute-done.1), channel_id=1, source_target_pairs={{4,0},{8,4},{12,8},{14,12},{10,14},{6,10},{2,6},{0,2},{5,1},{9,5},... | collective-permute-start | bytes 393224 | tf_op jit(solution)/shard_map/ppermute | solution.py:426
  17.0 8.1 %collective-permute-start.12 = (bf16[2,256,128]{2,1,0:T(8,128)(2,1)S(1)}, bf16[2,256,128]{2,1,0:T(8,128)(2,1)S(1)}, u32[]{:S(2)}, u32[]{:S(2)}) collective-permute-start(bf16[2,256,128]{2,1,0:T(8,128)(2,1)S(1)} %collective-permute-done.6), channel_id=1, source_target_pairs={{0,4},{4,8},{8,12},{12,14},{14,10},{10,6},{6,2},{2,0},{1,5},{5,9},... | collective-permute-start | bytes 393224 | tf_op jit(solution)/shard_map/ppermute | solution.py:425
  18.6 5.4 %collective-permute-start.13 = (bf16[2,256,128]{2,1,0:T(8,128)(2,1)S(1)}, bf16[2,256,128]{2,1,0:T(8,128)(2,1)S(1)}, u32[]{:S(2)}, u32[]{:S(2)}) collective-permute-start(bf16[2,256,128]{2,1,0:T(8,128)(2,1)S(1)} %collective-permute-done.7), channel_id=1, source_target_pairs={{4,0},{8,4},{12,8},{14,12},{10,14},{6,10},{2,6},{0,2},{5,1},{9,5},... | collective-permute-start | bytes 393224 | tf_op jit(solution)/shard_map/ppermute | solution.py:426
  19.2 8.3 %collective-permute-start.8 = (bf16[2,256,128]{2,1,0:T(8,128)(2,1)S(1)}, bf16[2,256,128]{2,1,0:T(8,128)(2,1)S(1)}, u32[]{:S(2)}, u32[]{:S(2)}) collective-permute-start(bf16[2,256,128]{2,1,0:T(8,128)(2,1)S(1)} %collective-permute-done.2), channel_id=1, source_target_pairs={{0,4},{4,8},{8,12},{12,14},{14,10},{10,6},{6,2},{2,0},{1,5},{5,9},... | collective-permute-start | bytes 393224 | tf_op jit(solution)/shard_map/ppermute | solution.py:425
  20.8 5.5 %collective-permute-start.9 = (bf16[2,256,128]{2,1,0:T(8,128)(2,1)S(1)}, bf16[2,256,128]{2,1,0:T(8,128)(2,1)S(1)}, u32[]{:S(2)}, u32[]{:S(2)}) collective-permute-start(bf16[2,256,128]{2,1,0:T(8,128)(2,1)S(1)} %collective-permute-done.3), channel_id=1, source_target_pairs={{4,0},{8,4},{12,8},{14,12},{10,14},{6,10},{2,6},{0,2},{5,1},{9,5},... | collective-permute-start | bytes 393224 | tf_op jit(solution)/shard_map/ppermute | solution.py:426
  24.0 4.5 %collective-permute-start.15 = (bf16[1,256,128]{2,1,0:T(8,128)(2,1)S(1)}, bf16[1,256,128]{2,1,0:T(8,128)(2,1)S(1)}, u32[]{:S(2)}, u32[]{:S(2)}) collective-permute-start(bf16[1,256,128]{2,1,0:T(8,128)(2,1)S(1)} %slice.29), channel_id=1, source_target_pairs={{4,0},{8,4},{12,8},{14,12},{10,14},{6,10},{2,6},{0,2},{5,1},{9,5},... | collective-permute-start | bytes 196616 | tf_op jit(solution)/shard_map/ppermute | solution.py:431
  25.1 4.3 %collective-permute-start.14 = (bf16[1,256,128]{2,1,0:T(8,128)(2,1)S(1)}, bf16[1,256,128]{2,1,0:T(8,128)(2,1)S(1)}, u32[]{:S(2)}, u32[]{:S(2)}) collective-permute-start(bf16[1,256,128]{2,1,0:T(8,128)(2,1)S(1)} %slice.28), channel_id=1, source_target_pairs={{0,4},{4,8},{8,12},{12,14},{14,10},{10,6},{6,2},{2,0},{1,5},{5,9},... | collective-permute-start | bytes 196616 | tf_op jit(solution)/shard_map/ppermute | solution.py:431
  26.2 8.1 %collective-permute-start.16 = (bf16[2,5,2,256,128]{4,3,2,1,0:T(8,128)(2,1)S(1)}, bf16[2,5,2,256,128]{4,3,2,1,0:T(8,128)(2,1)S(1)}, u32[]{:S(2)}, u32[]{:S(2)}) collective-permute-start(bf16[2,5,2,256,128]{4,3,2,1,0:T(8,128)(2,1)S(1)} %pad_maximum_fusion.own0), channel_id=1, source_target_pairs={{0,1},{1,0},{2,3},{3,2},{4,5},{5,4},{6,7},{7,6},{8,9},{9,8},{10,11... | collective-permute-start | bytes 3932168 | tf_op jit(solution)/shard_map/ppermute | solution.py:438
  26.3 4.5 %collective-permute-start.11 = (bf16[1,256,128]{2,1,0:T(8,128)(2,1)S(1)}, bf16[1,256,128]{2,1,0:T(8,128)(2,1)S(1)}, u32[]{:S(2)}, u32[]{:S(2)}) collective-permute-start(bf16[1,256,128]{2,1,0:T(8,128)(2,1)S(1)} %slice.27), channel_id=1, source_target_pairs={{4,0},{8,4},{12,8},{14,12},{10,14},{6,10},{2,6},{0,2},{5,1},{9,5},... | collective-permute-start | bytes 196616 | tf_op jit(solution)/shard_map/ppermute | solution.py:431
  27.5 4.3 %collective-permute-start.10 = (bf16[1,256,128]{2,1,0:T(8,128)(2,1)S(1)}, bf16[1,256,128]{2,1,0:T(8,128)(2,1)S(1)}, u32[]{:S(2)}, u32[]{:S(2)}) collective-permute-start(bf16[1,256,128]{2,1,0:T(8,128)(2,1)S(1)} %slice.26), channel_id=1, source_target_pairs={{0,4},{4,8},{8,12},{12,14},{14,10},{10,6},{6,2},{2,0},{1,5},{5,9},... | collective-permute-start | bytes 196616 | tf_op jit(solution)/shard_map/ppermute | solution.py:431
  32.0 2.4 %collective-permute-start.17 = (bf16[2,3,2,256,128]{4,3,2,1,0:T(8,128)(2,1)S(1)}, bf16[2,3,2,256,128]{4,3,2,1,0:T(8,128)(2,1)S(1)}, u32[]{:S(2)}, u32[]{:S(2)}) collective-permute-start(bf16[2,3,2,256,128]{4,3,2,1,0:T(8,128)(2,1)S(1)} %pad_maximum_fusion.1.own1), channel_id=1, source_target_pairs={{0,1},{1,0},{2,3},{3,2},{4,5},{5,4},{6,7},{7,6},{8,9},{9,8},{10,11... | collective-permute-start | bytes 2359304 | tf_op jit(solution)/shard_map/ppermute | solution.py:438
  44.9 2.3 %collective-permute-start.18 = (f32[8,2,2,32,128]{4,3,2,1,0:T(8,128)}, f32[8,2,2,32,128]{4,3,2,1,0:T(8,128)}, u32[]{:S(2)}, u32[]{:S(2)}) collective-permute-start(f32[8,2,2,32,128]{4,3,2,1,0:T(8,128)} %get-tuple-element.19), channel_id=1, source_target_pairs={{0,1},{1,0},{2,3},{3,2},{4,5},{5,4},{6,7},{7,6},{8,9},{9,8},{10,11... | collective-permute-start | bytes 1572872 | tf_op jit(solution)/shard_map/ppermute | solution.py:441
  48.4 20.0 %collective-permute-start.19 = (f32[2,2,2,32,128]{4,3,2,1,0:T(8,128)S(1)}, f32[2,2,2,32,128]{4,3,2,1,0:T(8,128)S(1)}, u32[]{:S(2)}, u32[]{:S(2)}) collective-permute-start(f32[2,2,2,32,128]{4,3,2,1,0:T(8,128)S(1)} %get-tuple-element.32), channel_id=1, source_target_pairs={{0,4},{2,6},{4,8},{6,10},{8,12},{10,14},{12,0},{14,2},{1,5},{3,7},... | collective-permute-start | bytes 393224 | tf_op jit(solution)/shard_map/ppermute | solution.py:395
  48.5 20.0 %collective-permute-start.20 = (f32[2,2,2,32,128]{4,3,2,1,0:T(8,128)S(1)}, f32[2,2,2,32,128]{4,3,2,1,0:T(8,128)S(1)}, u32[]{:S(2)}, u32[]{:S(2)}) collective-permute-start(f32[2,2,2,32,128]{4,3,2,1,0:T(8,128)S(1)} %get-tuple-element.31), channel_id=1, source_target_pairs={{0,8},{2,10},{4,12},{6,14},{8,0},{10,2},{12,4},{14,6},{1,9},{3,11}... | collective-permute-start | bytes 393224 | tf_op jit(solution)/shard_map/ppermute | solution.py:395
  49.5 19.0 %collective-permute-start.21 = (f32[2,2,2,32,128]{4,3,2,1,0:T(8,128)S(1)}, f32[2,2,2,32,128]{4,3,2,1,0:T(8,128)S(1)}, u32[]{:S(2)}, u32[]{:S(2)}) collective-permute-start(f32[2,2,2,32,128]{4,3,2,1,0:T(8,128)S(1)} %get-tuple-element.30), channel_id=1, source_target_pairs={{0,12},{2,14},{4,0},{6,2},{8,4},{10,6},{12,8},{14,10},{1,13},{3,15... | collective-permute-start | bytes 393224 | tf_op jit(solution)/shard_map/ppermute | solution.py:395
  68.6 5.3 %collective-permute-start.22 = (f32[2,2,32,128]{3,2,1,0:T(8,128)S(1)}, f32[2,2,32,128]{3,2,1,0:T(8,128)}, u32[]{:S(2)}, u32[]{:S(2)}) collective-permute-start(f32[2,2,32,128]{3,2,1,0:T(8,128)S(1)} %dynamic-slice_bitcast_fusion.3), channel_id=1, source_target_pairs={{0,2},{2,0},{4,6},{6,4},{8,10},{10,8},{12,14},{14,12},{1,3},{3,1},... | collective-permute-start | bytes 196616 | tf_op jit(solution)/shard_map/ppermute | solution.py:402
  73.9 20.1 %collective-permute-start.23 = (f32[2,2,1536,128]{3,2,1,0:T(8,128)}, f32[2,2,1536,128]{3,2,1,0:T(8,128)}, u32[]{:S(2)}, u32[]{:S(2)}) collective-permute-start(f32[2,2,1536,128]{3,2,1,0:T(8,128)} %get-tuple-element.28), channel_id=1, source_target_pairs={{0,1},{1,0},{2,3},{3,2},{4,5},{5,4},{6,7},{7,6},{8,9},{9,8},{10,11... | collective-permute-start | bytes 9437192 | tf_op jit(solution)/shard_map/ppermute | solution.py:445
  (7 other events, 71.8 us)
where the time goes:
time: 99.4 us; the launch traced here: 97.9 us
  starting transfers between devices  26 us (26%)
  Pallas kernels  25.4 us (26%)
  blocking collectives  18.3 us (18%)
  waiting for transfers between devices  15.1 us (15%)
  other arithmetic  7.21 us (7%)
  local copies, waits for them, and re-layouts  4.91 us (5%)
    all_to_all x1, blocking collectives, local(): lax.all_to_all(jnp.broadcast_to(share[None], total.shape), 'row', 0, 0, t...  18.3 us
    pallas_call x1, Pallas kernels, make_values(): pl.pallas_call(functools.partial(values_kernel, entries, early_count, sub...  13.4 us
    ppermute x6, starting transfers between devices, local(): up[k] = lax.ppermute(up[k], 'row', ahead)  11.5 us
    pallas_call x1, Pallas kernels, make_gram(): pl.pallas_call(functools.partial(gram_kernel, entries, early_count, sub),...  9.69 us
    unnamed x21, local copies, waits for them, and re-layouts  4.72 us
    ppermute x3, starting transfers between devices, scatter_sum(): came.append(lax.ppermute(sent, 'row', route))  3.87 us
    add x1, other arithmetic, local(): values = mine + lax.ppermute(theirs, 'col', swap)  3.86 us
    ppermute x6, starting transfers between devices, local(): down[k] = lax.ppermute(down[k], 'row', behind)  3.32 us
  transfers between devices with their start and end apart: 24, of which 9 were waited for; matrix products, arithmetic and copies ran while one was open for 2% of the time, Pallas kernels for 16%

commit v1 on v0

--- a/solution.py
+++ b/solution.py
@@ -312,14 +312,14 @@
 def vmem_limit(scratch, blocks):
     held = [x for x in scratch if x.dtype in (jnp.bfloat16, jnp.float32)]
     size = sum(math.prod(x.shape) * jnp.dtype(x.dtype).itemsize for x in held)
-    return size + 2 * sum(math.prod(shape) * 4 for shape in blocks) + 8 * 2**20
+    return size + 2 * sum(math.prod(shape) * 4 for shape in blocks) + 5 * 2**20
 
 
 def make_values(tab, a, stacks, entries, sub):
     supernodes, early_count = stacks[0].shape[:2]
     rows, width = a.shape[1], stacks[0].shape[4]
     slots = tab.shape[2] + tab.shape[2] % CH
-    tile = max(t for t in range(BLK, min(rows, 768) + 1, BLK) if rows % t == 0)
+    tile = max(t for t in range(BLK, min(rows, 512) + 1, BLK) if rows % t == 0)
     out_spec = pl.BlockSpec((1, 2, tile, width), lambda k, m, _: (k, 0, m, 0))
     out = jax.ShapeDtypeStruct((supernodes, 2, rows, width), jnp.float32)
     scratch = [
@@ -403,6 +403,37 @@
     return lax.dynamic_index_in_dim(kept, odd, 0, keepdims=False) + last, beside
 
 
+def place_kernel(n_row, diag_ref, *refs):
+    *own, other, out_ref = refs
+    half = n_row // 2
+    row = lax.axis_index("row")
+    level, odd = lax.div(row, 2), lax.rem(row, 2)
+    size = own[0].shape[2]
+    out_ref[...] = diag_ref[...].astype(jnp.float32)
+    for d in range(half):
+        base = 2 * lax.rem(level - d + half, half)
+        out_ref[:, :, block_at(base + odd, size), :] -= own[d][...]
+        out_ref[:, :, block_at(base + 1 - odd, size), :] -= other[d]
+
+
+def gather_shares(diag_blocks, share, n_row, beside):
+    half = n_row // 2
+    own = [share]
+    for d in range(1, half):
+        own.append(lax.ppermute(share, "row", [(i, (i + 2 * d) % n_row) for i in range(n_row)]))
+    other = lax.ppermute(jnp.stack(own), "row", [(i, i ^ 1) for i in range(n_row)])
+    other, beside = lax.optimization_barrier((other, beside))
+    vmem = pl.BlockSpec(memory_space=pltpu.VMEM)
+    schur = pl.pallas_call(
+        functools.partial(place_kernel, n_row),
+        out_shape=jax.ShapeDtypeStruct(diag_blocks.shape, jnp.float32),
+        in_specs=[vmem] * (half + 2),
+        out_specs=vmem,
+        name="place",
+    )(diag_blocks, *own, other)
+    return schur, beside
+
+
 def local(n_row, inverse_pairs, factor_rows, diag_blocks, row_lists, block_order):
     supernodes = row_lists.shape[0]
     local_rows, local_cols = inverse_pairs.shape[1:]
@@ -443,9 +474,8 @@
     mine, theirs = make_values(tab, inverse_pairs, stacks, entries, sub)
     share, theirs = scatter_sum(total, n_row, theirs)
     values = mine + lax.ppermute(theirs, "col", swap)
-    shares = lax.all_to_all(jnp.broadcast_to(share[None], total.shape), "row", 0, 0, tiled=True)
-    gram = jnp.moveaxis(shares, 0, 2).reshape(diag_blocks.shape)
-    return (values, diag_blocks.astype(jnp.float32) - gram)
+    schur, values = gather_shares(diag_blocks, share, n_row, values)
+    return (values, schur)
 
 
 def solution(mesh):

time: 99.4 us -> 96.2 us (0.968); the launches traced: 97.9 us -> 97.1 us
  blocking collectives: 18.3 us -> 0 us
  waiting for transfers between devices: 15.1 us -> 23.8 us
  Pallas kernels: 25.4 us -> 30.9 us
  starting transfers between devices: 26 us -> 29.4 us
    all_to_all x1 -> x0, blocking collectives: 18.3 us -> none  [local(): lax.all_to_all(jnp.broadcast_to(share[None], total.shape), 'row', 0, 0, t...]
    ppermute x0 -> x4, waiting for transfers between devices: none -> 7.49 us  [the longest x3 4.85 us: gather_shares(): lax.ppermute(share, 'row', [(i, (i + 2 * d) % n_row) for i in range(n_row)])]
    ppermute x0 -> x4, starting transfers between devices: none -> 3.94 us  [the longest x3 3.87 us: gather_shares(): lax.ppermute(share, 'row', [(i, (i + 2 * d) % n_row) for i in range(n_row)])]
    ppermute x3, starting transfers between devices: 3.87 us -> 7.62 us  [scatter_sum(): came.append(lax.ppermute(sent, 'row', route))]
    ppermute x6, waiting for transfers between devices: 3.04 us -> 0.02 us  [local(): down[k] = lax.ppermute(down[k], 'row', behind)]
    ppermute x1, starting transfers between devices: 2.98 us -> 0.07 us  [scatter_sum(): lax.ppermute(sent, 'row', route)]
    ppermute x6, starting transfers between devices: 3.32 us -> 0.58 us  [local(): down[k] = lax.ppermute(down[k], 'row', behind)]
    pallas_call x1, Pallas kernels: 13.4 us -> 16 us  [make_values(): pl.pallas_call(functools.partial(values_kernel, entries, early_count, sub...]
  transfers between devices with their start and end apart: 24 -> 28, of which waited for: 9 -> 12; matrix products, arithmetic and copies ran while one was open for 2% -> 6% of each run, Pallas kernels for 16% -> 19%
where the time goes in v1:
time: 96.2 us; the launch traced here: 97.1 us
  Pallas kernels  30.9 us (32%)
  starting transfers between devices  29.4 us (31%)
  waiting for transfers between devices  23.8 us (25%)
  other arithmetic  6.49 us (7%)
  local copies, waits for them, and re-layouts  5.54 us (6%)
    pallas_call x1, Pallas kernels, make_values(): pl.pallas_call(functools.partial(values_kernel, entries, early_count, sub...  16 us
    ppermute x6, starting transfers between devices, local(): up[k] = lax.ppermute(up[k], 'row', ahead)  12.8 us
    pallas_call x1, Pallas kernels, make_gram(): pl.pallas_call(functools.partial(gram_kernel, entries, early_count, sub),...  10.4 us
    ppermute x3, starting transfers between devices, scatter_sum(): came.append(lax.ppermute(sent, 'row', route))  7.62 us
    unnamed x27, local copies, waits for them, and re-layouts  5.42 us
    ppermute x3, waiting for transfers between devices, gather_shares(): lax.ppermute(share, 'row', [(i, (i + 2 * d) % n_row) for i in range(n_row)])  4.85 us
    add x1, other arithmetic, local(): values = mine + lax.ppermute(theirs, 'col', swap)  4.82 us
    ppermute x1, waiting for transfers between devices, scatter_sum(): lax.ppermute(sent, 'row', route)  4.25 us
  transfers between devices with their start and end apart: 28, of which 12 were waited for; matrix products, arithmetic and copies ran while one was open for 6% of the time, Pallas kernels for 19%

profile of v1, /device:TPU:0, one launch (start us, length us, event | category | flops | bytes accessed | tf_op | source)
XLA Modules:
  0.0 97.1 jit_solution(12735701793487844806)
XLA Ops:
  1.7 3.1 %collective-permute-start = (bf16[2,256,128]{2,1,0:T(8,128)(2,1)S(1)}, bf16[2,256,128]{2,1,0:T(8,128)(2,1)S(1)}, u32[]{:S(2)}, u32[]{:S(2)}) collective-permute-start(bf16[2,256,128]{2,1,0:T(8,128)(2,1)S(1)} %get-tuple-element.40), channel_id=1, source_target_pairs={{0,4},{4,8},{8,12},{12,14},{14,10},{10,6},{6,2},{2,0},{1,5},{5,9},... | collective-permute-start | bytes 393224 | tf_op jit(solution)/shard_map/ppermute | solution.py:456
  4.8 2.0 %collective-permute-start.4 = (bf16[2,256,128]{2,1,0:T(8,128)(2,1)S(1)}, bf16[2,256,128]{2,1,0:T(8,128)(2,1)S(1)}, u32[]{:S(2)}, u32[]{:S(2)}) collective-permute-start(bf16[2,256,128]{2,1,0:T(8,128)(2,1)S(1)} %get-tuple-element.39), channel_id=1, source_target_pairs={{0,4},{4,8},{8,12},{12,14},{14,10},{10,6},{6,2},{2,0},{1,5},{5,9},... | collective-permute-start | bytes 393224 | tf_op jit(solution)/shard_map/ppermute | solution.py:456
  6.8 2.4 %table.1.tab_ref = s32[2,6,16]{2,1,0:T(8,128)} custom-call(s32[2,16]{1,0:T(2,128)} %lists_ref.1, s32[96]{0:T(128)} %order_ref.1), custom_call_target="tpu_custom_call" | custom-call | tf_op jit(solution)/shard_map/table/pallas_call | solution.py:67
  9.2 2.1 %collective-permute-start.2 = (bf16[2,256,128]{2,1,0:T(8,128)(2,1)S(1)}, bf16[2,256,128]{2,1,0:T(8,128)(2,1)S(1)}, u32[]{:S(2)}, u32[]{:S(2)}) collective-permute-start(bf16[2,256,128]{2,1,0:T(8,128)(2,1)S(1)} %collective-permute-done), channel_id=1, source_target_pairs={{0,4},{4,8},{8,12},{12,14},{14,10},{10,6},{6,2},{2,0},{1,5},{5,9},... | collective-permute-start | bytes 393224 | tf_op jit(solution)/shard_map/ppermute | solution.py:456
  11.3 2.0 %collective-permute-start.6 = (bf16[2,256,128]{2,1,0:T(8,128)(2,1)S(1)}, bf16[2,256,128]{2,1,0:T(8,128)(2,1)S(1)}, u32[]{:S(2)}, u32[]{:S(2)}) collective-permute-start(bf16[2,256,128]{2,1,0:T(8,128)(2,1)S(1)} %collective-permute-done.4), channel_id=1, source_target_pairs={{0,4},{4,8},{8,12},{12,14},{14,10},{10,6},{6,2},{2,0},{1,5},{5,9},... | collective-permute-start | bytes 393224 | tf_op jit(solution)/shard_map/ppermute | solution.py:456
  13.4 2.1 %collective-permute-done.2 = bf16[2,256,128]{2,1,0:T(8,128)(2,1)S(1)} collective-permute-done((bf16[2,256,128]{2,1,0:T(8,128)(2,1)S(1)}, bf16[2,256,128]{2,1,0:T(8,128)(2,1)S(1)}, u32[]{:S(2)}, u32[]{:S(2)}) %collective-permute-start.2) | collective-permute-done | bytes 131104 | tf_op jit(solution)/shard_map/ppermute | solution.py:456
  15.5 1.8 %collective-permute-start.8 = (bf16[2,256,128]{2,1,0:T(8,128)(2,1)S(1)}, bf16[2,256,128]{2,1,0:T(8,128)(2,1)S(1)}, u32[]{:S(2)}, u32[]{:S(2)}) collective-permute-start(bf16[2,256,128]{2,1,0:T(8,128)(2,1)S(1)} %collective-permute-done.2), channel_id=1, source_target_pairs={{0,4},{4,8},{8,12},{12,14},{14,10},{10,6},{6,2},{2,0},{1,5},{5,9},... | collective-permute-start | bytes 393224 | tf_op jit(solution)/shard_map/ppermute | solution.py:456
  18.3 1.8 %collective-permute-start.12 = (bf16[2,256,128]{2,1,0:T(8,128)(2,1)S(1)}, bf16[2,256,128]{2,1,0:T(8,128)(2,1)S(1)}, u32[]{:S(2)}, u32[]{:S(2)}) collective-permute-start(bf16[2,256,128]{2,1,0:T(8,128)(2,1)S(1)} %collective-permute-done.6), channel_id=1, source_target_pairs={{0,4},{4,8},{8,12},{12,14},{14,10},{10,6},{6,2},{2,0},{1,5},{5,9},... | collective-permute-start | bytes 393224 | tf_op jit(solution)/shard_map/ppermute | solution.py:456
  21.3 1.7 %collective-permute-start.10 = (bf16[1,256,128]{2,1,0:T(8,128)(2,1)S(1)}, bf16[1,256,128]{2,1,0:T(8,128)(2,1)S(1)}, u32[]{:S(2)}, u32[]{:S(2)}) collective-permute-start(bf16[1,256,128]{2,1,0:T(8,128)(2,1)S(1)} %slice.26), channel_id=1, source_target_pairs={{0,4},{4,8},{8,12},{12,14},{14,10},{10,6},{6,2},{2,0},{1,5},{5,9},... | collective-permute-start | bytes 196616 | tf_op jit(solution)/shard_map/ppermute | solution.py:462
  23.6 1.8 %collective-permute-start.14 = (bf16[1,256,128]{2,1,0:T(8,128)(2,1)S(1)}, bf16[1,256,128]{2,1,0:T(8,128)(2,1)S(1)}, u32[]{:S(2)}, u32[]{:S(2)}) collective-permute-start(bf16[1,256,128]{2,1,0:T(8,128)(2,1)S(1)} %slice.28), channel_id=1, source_target_pairs={{0,4},{4,8},{8,12},{12,14},{14,10},{10,6},{6,2},{2,0},{1,5},{5,9},... | collective-permute-start | bytes 196616 | tf_op jit(solution)/shard_map/ppermute | solution.py:462
  30.0 2.3 %collective-permute-done.17.sib1 = bf16[2,3,2,256,128]{4,3,2,1,0:T(8,128)(2,1)S(1)} collective-permute-done((bf16[2,3,2,256,128]{4,3,2,1,0:T(8,128)(2,1)S(1)}, bf16[2,3,2,256,128]{4,3,2,1,0:T(8,128)(2,1)S(1)}, u32[]{:S(2)}, u32[]{:S(2)}) %collective-permute-start.17) | collective-permute-done | bytes 786464 | tf_op jit(solution)/shard_map/ppermute | solution.py:469
  32.3 10.4 %gram.1 = (f32[8,2,2,32,128]{4,3,2,1,0:T(8,128)S(1)}, f32[8,2,2,32,128]{4,3,2,1,0:T(8,128)}) custom-call(s32[2,6,16]{2,1,0:T(8,128)S(1)} %copy-done.4, bf16[2,1536,6144]{2,1,0:T(8,128)(2,1)} %a_ref.3, bf16[2,5,2,256,128]{4,3,2,1,0:T(8,128)(2,1)S(1)} %pad_maximum_fusion.own0, bf16[2,3,2,256,128]{4,3,2,1,0:T(8,128)(2,1)S(1)} %pad_maximum_fusion.1.own1, ...), custom_call_target="tpu_custom_call" | custom-call | flops 1073741824 | bytes 8388608 | tf_op jit(solution)/shard_map/gram/pallas_call | solution.py:368
  43.5 2.2 %collective-permute-done.18 = f32[8,2,2,32,128]{4,3,2,1,0:T(8,128)} collective-permute-done((f32[8,2,2,32,128]{4,3,2,1,0:T(8,128)}, f32[8,2,2,32,128]{4,3,2,1,0:T(8,128)}, u32[]{:S(2)}, u32[]{:S(2)}) %collective-permute-start.18) | collective-permute-done | bytes 524320 | tf_op jit(solution)/shard_map/ppermute | solution.py:472
  47.1 5.2 %collective-permute-start.19 = (f32[2,2,2,32,128]{4,3,2,1,0:T(8,128)S(1)}, f32[2,2,2,32,128]{4,3,2,1,0:T(8,128)S(1)}, u32[]{:S(2)}, u32[]{:S(2)}) collective-permute-start(f32[2,2,2,32,128]{4,3,2,1,0:T(8,128)S(1)} %get-tuple-element.36), channel_id=1, source_target_pairs={{0,4},{2,6},{4,8},{6,10},{8,12},{10,14},{12,0},{14,2},{1,5},{3,7},... | collective-permute-start | bytes 393224 | tf_op jit(solution)/shard_map/ppermute | solution.py:395
  52.3 2.4 %collective-permute-start.21 = (f32[2,2,2,32,128]{4,3,2,1,0:T(8,128)S(1)}, f32[2,2,2,32,128]{4,3,2,1,0:T(8,128)S(1)}, u32[]{:S(2)}, u32[]{:S(2)}) collective-permute-start(f32[2,2,2,32,128]{4,3,2,1,0:T(8,128)S(1)} %get-tuple-element.34), channel_id=1, source_target_pairs={{0,12},{2,14},{4,0},{6,2},{8,4},{10,6},{12,8},{14,10},{1,13},{3,15... | collective-permute-start | bytes 393224 | tf_op jit(solution)/shard_map/ppermute | solution.py:395
  55.8 16.0 %values.1 = (f32[2,2,1536,128]{3,2,1,0:T(8,128)S(1)}, f32[2,2,1536,128]{3,2,1,0:T(8,128)}) custom-call(s32[2,6,16]{2,1,0:T(8,128)S(1)} %copy-done.4, bf16[2,1536,6144]{2,1,0:T(8,128)(2,1)} %a_ref.3, bf16[2,5,2,256,128]{4,3,2,1,0:T(8,128)(2,1)S(1)} %pad_maximum_fusion.own0, bf16[2,3,2,256,128]{4,3,2,1,0:T(8,128)(2,1)S(1)} %pad_maximum_fusion.1.own1, ...), custom_call_target="tpu_custom_call" | custom-call | flops 6442450944 | bytes 16777216 | tf_op jit(solution)/shard_map/values/pallas_call | solution.py:331
  71.9 1.6 %copy-done = f32[2,2,1536,128]{3,2,1,0:T(8,128)} copy-done((f32[2,2,1536,128]{3,2,1,0:T(8,128)}, f32[2,2,1536,128]{3,2,1,0:T(8,128)S(1)}, u32[]{:S(2)}) %copy-start) | copy-done | bytes 3145752
  73.7 4.3 %collective-permute-done.22 = f32[2,2,32,128]{3,2,1,0:T(8,128)S(1)} collective-permute-done((f32[2,2,32,128]{3,2,1,0:T(8,128)S(1)}, f32[2,2,32,128]{3,2,1,0:T(8,128)S(1)}, u32[]{:S(2)}, u32[]{:S(2)}) %collective-permute-start.22) | collective-permute-done | bytes 65568 | tf_op jit(solution)/shard_map/ppermute | solution.py:402
  78.0 2.5 %collective-permute-start.24 = (f32[2,2,32,128]{3,2,1,0:T(8,128)S(1)}, f32[2,2,32,128]{3,2,1,0:T(8,128)S(1)}, u32[]{:S(2)}, u32[]{:S(2)}) collective-permute-start(f32[2,2,32,128]{3,2,1,0:T(8,128)S(1)} %bitcast_add_fusion.1.refs_0_), channel_id=1, source_target_pairs={{0,8},{2,10},{4,12},{6,14},{8,0},{10,2},{12,4},{14,6},{1,9},{3,11}... | collective-permute-start | bytes 196616 | tf_op jit(solution)/shard_map/ppermute | solution.py:423
  81.8 3.0 %collective-permute-done.23.refs_1_ = f32[2,2,32,128]{3,2,1,0:T(8,128)S(1)} collective-permute-done((f32[2,2,32,128]{3,2,1,0:T(8,128)S(1)}, f32[2,2,32,128]{3,2,1,0:T(8,128)S(1)}, u32[]{:S(2)}, u32[]{:S(2)}) %collective-permute-start.23) | collective-permute-done | bytes 65568 | tf_op jit(solution)/shard_map/ppermute | solution.py:423
  84.8 1.9 %collective-permute-done.24.refs_2_ = f32[2,2,32,128]{3,2,1,0:T(8,128)S(1)} collective-permute-done((f32[2,2,32,128]{3,2,1,0:T(8,128)S(1)}, f32[2,2,32,128]{3,2,1,0:T(8,128)S(1)}, u32[]{:S(2)}, u32[]{:S(2)}) %collective-permute-start.24) | collective-permute-done | bytes 65568 | tf_op jit(solution)/shard_map/ppermute | solution.py:423
  86.8 4.8 %add.80 = f32[2,2,1536,128]{3,2,1,0:T(8,128)} add(f32[2,2,1536,128]{3,2,1,0:T(8,128)} %copy-done, f32[2,2,1536,128]{3,2,1,0:T(8,128)} %collective-permute-done.27) | non-fusion elementwise | flops 786432 | bytes 9437184 | tf_op jit(solution)/shard_map/add | solution.py:476
  91.7 2.6 %collective-permute-done.26.refs_4_ = f32[4,2,2,32,128]{4,3,2,1,0:T(8,128)S(1)} collective-permute-done((f32[4,2,2,32,128]{4,3,2,1,0:T(8,128)S(1)}, f32[4,2,2,32,128]{4,3,2,1,0:T(8,128)S(1)}, u32[]{:S(2)}, u32[]{:S(2)}) %collective-permute-start.26) | collective-permute-done | bytes 262176 | tf_op jit(solution)/shard_map/ppermute | solution.py:424
  95.0 2.1 %place.1 = f32[2,2,256,128]{3,2,1,0:T(8,128)} custom-call(bf16[2,2,256,128]{3,2,1,0:T(8,128)(2,1)} %diag_ref.1, f32[2,2,32,128]{3,2,1,0:T(8,128)} %copy-done.5, f32[2,2,32,128]{3,2,1,0:T(8,128)} %copy-done.7, f32[2,2,32,128]{3,2,1,0:T(8,128)} %copy-done.8, f32[2,2,32,128]{3,2,1,0:T(8,128)} %copy-done.9, f32[4,2,2,32,128]{4,3,2,1,0:T(8,128)} %copy-done.6), custom_call_target="tpu_custom_call" | custom-call | tf_op jit(solution)/shard_map/place/pallas_call | solution.py:427
  (82 shorter events, 14.0 us)
Async XLA Ops:
  1.7 7.5 %collective-permute-start = (bf16[2,256,128]{2,1,0:T(8,128)(2,1)S(1)}, bf16[2,256,128]{2,1,0:T(8,128)(2,1)S(1)}, u32[]{:S(2)}, u32[]{:S(2)}) collective-permute-start(bf16[2,256,128]{2,1,0:T(8,128)(2,1)S(1)} %get-tuple-element.40), channel_id=1, source_target_pairs={{0,4},{4,8},{8,12},{12,14},{14,10},{10,6},{6,2},{2,0},{1,5},{5,9},... | collective-permute-start | bytes 393224 | tf_op jit(solution)/shard_map/ppermute | solution.py:456
  4.7 6.5 %collective-permute-start.1 = (bf16[2,256,128]{2,1,0:T(8,128)(2,1)S(1)}, bf16[2,256,128]{2,1,0:T(8,128)(2,1)S(1)}, u32[]{:S(2)}, u32[]{:S(2)}) collective-permute-start(bf16[2,256,128]{2,1,0:T(8,128)(2,1)S(1)} %get-tuple-element.40), channel_id=1, source_target_pairs={{4,0},{8,4},{12,8},{14,12},{10,14},{6,10},{2,6},{0,2},{5,1},{9,5},... | collective-permute-start | bytes 393224 | tf_op jit(solution)/shard_map/ppermute | solution.py:457
  4.8 6.5 %collective-permute-start.4 = (bf16[2,256,128]{2,1,0:T(8,128)(2,1)S(1)}, bf16[2,256,128]{2,1,0:T(8,128)(2,1)S(1)}, u32[]{:S(2)}, u32[]{:S(2)}) collective-permute-start(bf16[2,256,128]{2,1,0:T(8,128)(2,1)S(1)} %get-tuple-element.39), channel_id=1, source_target_pairs={{0,4},{4,8},{8,12},{12,14},{14,10},{10,6},{6,2},{2,0},{1,5},{5,9},... | collective-permute-start | bytes 393224 | tf_op jit(solution)/shard_map/ppermute | solution.py:456
  6.8 6.5 %collective-permute-start.5 = (bf16[2,256,128]{2,1,0:T(8,128)(2,1)S(1)}, bf16[2,256,128]{2,1,0:T(8,128)(2,1)S(1)}, u32[]{:S(2)}, u32[]{:S(2)}) collective-permute-start(bf16[2,256,128]{2,1,0:T(8,128)(2,1)S(1)} %get-tuple-element.39), channel_id=1, source_target_pairs={{4,0},{8,4},{12,8},{14,12},{10,14},{6,10},{2,6},{0,2},{5,1},{9,5},... | collective-permute-start | bytes 393224 | tf_op jit(solution)/shard_map/ppermute | solution.py:457
  9.2 6.3 %collective-permute-start.2 = (bf16[2,256,128]{2,1,0:T(8,128)(2,1)S(1)}, bf16[2,256,128]{2,1,0:T(8,128)(2,1)S(1)}, u32[]{:S(2)}, u32[]{:S(2)}) collective-permute-start(bf16[2,256,128]{2,1,0:T(8,128)(2,1)S(1)} %collective-permute-done), channel_id=1, source_target_pairs={{0,4},{4,8},{8,12},{12,14},{14,10},{10,6},{6,2},{2,0},{1,5},{5,9},... | collective-permute-start | bytes 393224 | tf_op jit(solution)/shard_map/ppermute | solution.py:456
  11.2 6.1 %collective-permute-start.3 = (bf16[2,256,128]{2,1,0:T(8,128)(2,1)S(1)}, bf16[2,256,128]{2,1,0:T(8,128)(2,1)S(1)}, u32[]{:S(2)}, u32[]{:S(2)}) collective-permute-start(bf16[2,256,128]{2,1,0:T(8,128)(2,1)S(1)} %collective-permute-done.1), channel_id=1, source_target_pairs={{4,0},{8,4},{12,8},{14,12},{10,14},{6,10},{2,6},{0,2},{5,1},{9,5},... | collective-permute-start | bytes 393224 | tf_op jit(solution)/shard_map/ppermute | solution.py:457
  11.3 7.1 %collective-permute-start.6 = (bf16[2,256,128]{2,1,0:T(8,128)(2,1)S(1)}, bf16[2,256,128]{2,1,0:T(8,128)(2,1)S(1)}, u32[]{:S(2)}, u32[]{:S(2)}) collective-permute-start(bf16[2,256,128]{2,1,0:T(8,128)(2,1)S(1)} %collective-permute-done.4), channel_id=1, source_target_pairs={{0,4},{4,8},{8,12},{12,14},{14,10},{10,6},{6,2},{2,0},{1,5},{5,9},... | collective-permute-start | bytes 393224 | tf_op jit(solution)/shard_map/ppermute | solution.py:456
  13.3 6.9 %collective-permute-start.7 = (bf16[2,256,128]{2,1,0:T(8,128)(2,1)S(1)}, bf16[2,256,128]{2,1,0:T(8,128)(2,1)S(1)}, u32[]{:S(2)}, u32[]{:S(2)}) collective-permute-start(bf16[2,256,128]{2,1,0:T(8,128)(2,1)S(1)} %collective-permute-done.5), channel_id=1, source_target_pairs={{4,0},{8,4},{12,8},{14,12},{10,14},{6,10},{2,6},{0,2},{5,1},{9,5},... | collective-permute-start | bytes 393224 | tf_op jit(solution)/shard_map/ppermute | solution.py:457
  15.5 5.7 %collective-permute-start.8 = (bf16[2,256,128]{2,1,0:T(8,128)(2,1)S(1)}, bf16[2,256,128]{2,1,0:T(8,128)(2,1)S(1)}, u32[]{:S(2)}, u32[]{:S(2)}) collective-permute-start(bf16[2,256,128]{2,1,0:T(8,128)(2,1)S(1)} %collective-permute-done.2), channel_id=1, source_target_pairs={{0,4},{4,8},{8,12},{12,14},{14,10},{10,6},{6,2},{2,0},{1,5},{5,9},... | collective-permute-start | bytes 393224 | tf_op jit(solution)/shard_map/ppermute | solution.py:456
  17.3 5.7 %collective-permute-start.9 = (bf16[2,256,128]{2,1,0:T(8,128)(2,1)S(1)}, bf16[2,256,128]{2,1,0:T(8,128)(2,1)S(1)}, u32[]{:S(2)}, u32[]{:S(2)}) collective-permute-start(bf16[2,256,128]{2,1,0:T(8,128)(2,1)S(1)} %collective-permute-done.3), channel_id=1, source_target_pairs={{4,0},{8,4},{12,8},{14,12},{10,14},{6,10},{2,6},{0,2},{5,1},{9,5},... | collective-permute-start | bytes 393224 | tf_op jit(solution)/shard_map/ppermute | solution.py:457
  18.3 5.2 %collective-permute-start.12 = (bf16[2,256,128]{2,1,0:T(8,128)(2,1)S(1)}, bf16[2,256,128]{2,1,0:T(8,128)(2,1)S(1)}, u32[]{:S(2)}, u32[]{:S(2)}) collective-permute-start(bf16[2,256,128]{2,1,0:T(8,128)(2,1)S(1)} %collective-permute-done.6), channel_id=1, source_target_pairs={{0,4},{4,8},{8,12},{12,14},{14,10},{10,6},{6,2},{2,0},{1,5},{5,9},... | collective-permute-start | bytes 393224 | tf_op jit(solution)/shard_map/ppermute | solution.py:456
  20.2 5.2 %collective-permute-start.13 = (bf16[2,256,128]{2,1,0:T(8,128)(2,1)S(1)}, bf16[2,256,128]{2,1,0:T(8,128)(2,1)S(1)}, u32[]{:S(2)}, u32[]{:S(2)}) collective-permute-start(bf16[2,256,128]{2,1,0:T(8,128)(2,1)S(1)} %collective-permute-done.7), channel_id=1, source_target_pairs={{4,0},{8,4},{12,8},{14,12},{10,14},{6,10},{2,6},{0,2},{5,1},{9,5},... | collective-permute-start | bytes 393224 | tf_op jit(solution)/shard_map/ppermute | solution.py:457
  21.3 4.5 %collective-permute-start.10 = (bf16[1,256,128]{2,1,0:T(8,128)(2,1)S(1)}, bf16[1,256,128]{2,1,0:T(8,128)(2,1)S(1)}, u32[]{:S(2)}, u32[]{:S(2)}) collective-permute-start(bf16[1,256,128]{2,1,0:T(8,128)(2,1)S(1)} %slice.26), channel_id=1, source_target_pairs={{0,4},{4,8},{8,12},{12,14},{14,10},{10,6},{6,2},{2,0},{1,5},{5,9},... | collective-permute-start | bytes 196616 | tf_op jit(solution)/shard_map/ppermute | solution.py:462
  23.5 8.8 %collective-permute-start.16 = (bf16[2,5,2,256,128]{4,3,2,1,0:T(8,128)(2,1)S(1)}, bf16[2,5,2,256,128]{4,3,2,1,0:T(8,128)(2,1)S(1)}, u32[]{:S(2)}, u32[]{:S(2)}) collective-permute-start(bf16[2,5,2,256,128]{4,3,2,1,0:T(8,128)(2,1)S(1)} %pad_maximum_fusion.own0), channel_id=1, source_target_pairs={{0,1},{1,0},{2,3},{3,2},{4,5},{5,4},{6,7},{7,6},{8,9},{9,8},{10,11... | collective-permute-start | bytes 3932168 | tf_op jit(solution)/shard_map/ppermute | solution.py:469
  23.6 4.7 %collective-permute-start.14 = (bf16[1,256,128]{2,1,0:T(8,128)(2,1)S(1)}, bf16[1,256,128]{2,1,0:T(8,128)(2,1)S(1)}, u32[]{:S(2)}, u32[]{:S(2)}) collective-permute-start(bf16[1,256,128]{2,1,0:T(8,128)(2,1)S(1)} %slice.28), channel_id=1, source_target_pairs={{0,4},{4,8},{8,12},{12,14},{14,10},{10,6},{6,2},{2,0},{1,5},{5,9},... | collective-permute-start | bytes 196616 | tf_op jit(solution)/shard_map/ppermute | solution.py:462
  47.1 26.4 %collective-permute-start.19 = (f32[2,2,2,32,128]{4,3,2,1,0:T(8,128)S(1)}, f32[2,2,2,32,128]{4,3,2,1,0:T(8,128)S(1)}, u32[]{:S(2)}, u32[]{:S(2)}) collective-permute-start(f32[2,2,2,32,128]{4,3,2,1,0:T(8,128)S(1)} %get-tuple-element.36), channel_id=1, source_target_pairs={{0,4},{2,6},{4,8},{6,10},{8,12},{10,14},{12,0},{14,2},{1,5},{3,7},... | collective-permute-start | bytes 393224 | tf_op jit(solution)/shard_map/ppermute | solution.py:395
  52.3 21.3 %collective-permute-start.20 = (f32[2,2,2,32,128]{4,3,2,1,0:T(8,128)S(1)}, f32[2,2,2,32,128]{4,3,2,1,0:T(8,128)S(1)}, u32[]{:S(2)}, u32[]{:S(2)}) collective-permute-start(f32[2,2,2,32,128]{4,3,2,1,0:T(8,128)S(1)} %get-tuple-element.35), channel_id=1, source_target_pairs={{0,8},{2,10},{4,12},{6,14},{8,0},{10,2},{12,4},{14,6},{1,9},{3,11}... | collective-permute-start | bytes 393224 | tf_op jit(solution)/shard_map/ppermute | solution.py:395
  52.3 21.3 %collective-permute-start.21 = (f32[2,2,2,32,128]{4,3,2,1,0:T(8,128)S(1)}, f32[2,2,2,32,128]{4,3,2,1,0:T(8,128)S(1)}, u32[]{:S(2)}, u32[]{:S(2)}) collective-permute-start(f32[2,2,2,32,128]{4,3,2,1,0:T(8,128)S(1)} %get-tuple-element.34), channel_id=1, source_target_pairs={{0,12},{2,14},{4,0},{6,2},{8,4},{10,6},{12,8},{14,10},{1,13},{3,15... | collective-permute-start | bytes 393224 | tf_op jit(solution)/shard_map/ppermute | solution.py:395
  73.6 4.3 %collective-permute-start.22 = (f32[2,2,32,128]{3,2,1,0:T(8,128)S(1)}, f32[2,2,32,128]{3,2,1,0:T(8,128)S(1)}, u32[]{:S(2)}, u32[]{:S(2)}) collective-permute-start(f32[2,2,32,128]{3,2,1,0:T(8,128)S(1)} %dynamic-slice_bitcast_fusion.3), channel_id=1, source_target_pairs={{0,2},{2,0},{4,6},{6,4},{8,10},{10,8},{12,14},{14,12},{1,3},{3,1},... | collective-permute-start | bytes 196616 | tf_op jit(solution)/shard_map/ppermute | solution.py:402
  77.9 8.9 %collective-permute-start.27 = (f32[2,2,1536,128]{3,2,1,0:T(8,128)}, f32[2,2,1536,128]{3,2,1,0:T(8,128)}, u32[]{:S(2)}, u32[]{:S(2)}) collective-permute-start(f32[2,2,1536,128]{3,2,1,0:T(8,128)} %get-tuple-element.31), channel_id=1, source_target_pairs={{0,1},{1,0},{2,3},{3,2},{4,5},{5,4},{6,7},{7,6},{8,9},{9,8},{10,11... | collective-permute-start | bytes 9437192 | tf_op jit(solution)/shard_map/ppermute | solution.py:476
  78.0 6.8 %collective-permute-start.23 = (f32[2,2,32,128]{3,2,1,0:T(8,128)S(1)}, f32[2,2,32,128]{3,2,1,0:T(8,128)S(1)}, u32[]{:S(2)}, u32[]{:S(2)}) collective-permute-start(f32[2,2,32,128]{3,2,1,0:T(8,128)S(1)} %bitcast_add_fusion.1.refs_0_), channel_id=1, source_target_pairs={{0,4},{2,6},{4,8},{6,10},{8,12},{10,14},{12,0},{14,2},{1,5},{3,7},... | collective-permute-start | bytes 196616 | tf_op jit(solution)/shard_map/ppermute | solution.py:423
  78.0 8.7 %collective-permute-start.24 = (f32[2,2,32,128]{3,2,1,0:T(8,128)S(1)}, f32[2,2,32,128]{3,2,1,0:T(8,128)S(1)}, u32[]{:S(2)}, u32[]{:S(2)}) collective-permute-start(f32[2,2,32,128]{3,2,1,0:T(8,128)S(1)} %bitcast_add_fusion.1.refs_0_), channel_id=1, source_target_pairs={{0,8},{2,10},{4,12},{6,14},{8,0},{10,2},{12,4},{14,6},{1,9},{3,11}... | collective-permute-start | bytes 196616 | tf_op jit(solution)/shard_map/ppermute | solution.py:423
  80.5 6.2 %collective-permute-start.25 = (f32[2,2,32,128]{3,2,1,0:T(8,128)S(1)}, f32[2,2,32,128]{3,2,1,0:T(8,128)S(1)}, u32[]{:S(2)}, u32[]{:S(2)}) collective-permute-start(f32[2,2,32,128]{3,2,1,0:T(8,128)S(1)} %bitcast_add_fusion.1.refs_0_), channel_id=1, source_target_pairs={{0,12},{2,14},{4,0},{6,2},{8,4},{10,6},{12,8},{14,10},{1,13},{3,15... | collective-permute-start | bytes 196616 | tf_op jit(solution)/shard_map/ppermute | solution.py:423
  86.7 7.6 %collective-permute-start.26 = (f32[4,2,2,32,128]{4,3,2,1,0:T(8,128)S(1)}, f32[4,2,2,32,128]{4,3,2,1,0:T(8,128)S(1)}, u32[]{:S(2)}, u32[]{:S(2)}) collective-permute-start(f32[4,2,2,32,128]{4,3,2,1,0:T(8,128)S(1)} %pad_maximum_fusion.2), channel_id=1, source_target_pairs={{0,2},{2,0},{4,6},{6,4},{8,10},{10,8},{12,14},{14,12},{1,3},{3,1},... | collective-permute-start | bytes 786440 | tf_op jit(solution)/shard_map/ppermute | solution.py:424
  (14 other events, 67.3 us)

commit v2 on v1

--- a/solution.py
+++ b/solution.py
@@ -143,19 +143,25 @@
 
         lax.fori_loop(0, tab_ref[which, COUNTS, 0], one, 0)
 
+    def start_weights(which):
+        halves = ((own0, own1), (sib0, sib1))
+        rows = start_rows(tab_ref, COL_ENTRY, which, w_ref, w_sems, halves, entries, early_count, sub)
+        lax.fori_loop(0, tab_ref[which, COUNTS, 0], rows, 0)
+
     @pl.when(now == 0)
     def _():
-        for which in range(w_ref.shape[0]):
-            rows = start_rows(
-                tab_ref, COL_ENTRY, which, w_ref, w_sems, ((own0, own1), (sib0, sib1)), entries, early_count, sub
-            )
-            lax.fori_loop(0, tab_ref[which, COUNTS, 0], rows, 0)
-            if which == 0:
-                start(now)
+        start(now)
+        start_weights(0)
 
     @pl.when(now + 1 < supernodes * tiles)
     def _():
         start(now + 1)
+
+    for which in range(1, w_ref.shape[0]):
+
+        @pl.when(now == which * tiles - 1)
+        def _(which=which):
+            start_weights(which)
 
     @pl.when(step == 0)
     def _():
@@ -224,7 +230,7 @@
         for which in range(x_ref.shape[0]):
             stacks = ((own, sib), entries, early_count, sub)
             there = tab_ref[which, COUNTS, 1]
-            lax.fori_loop(0, there, start_rows(tab_ref, ROW_ENTRY, which, l_ref, l_sems, *stacks), 0)
+            start_pair(which, 0)
 
             @pl.when(there > 0)
             def _(which=which, stacks=stacks):
@@ -232,7 +238,7 @@
                     0, tab_ref[which, COUNTS, 0], start_rows(tab_ref, COL_ENTRY, which, w_ref, w_sems, *stacks), 0
                 )
 
-            start_pair(which, 0)
+            lax.fori_loop(0, there, start_rows(tab_ref, ROW_ENTRY, which, l_ref, l_sems, *stacks), 0)
 
     acc_ref[...] = jnp.zeros_like(acc_ref)
     odd = lax.rem(listed, CH) != 0
@@ -243,50 +249,43 @@
     def _():
         lax.fori_loop(0, listed, wait_rows(k, w_ref, w_sems, width, sub, 2), 0)
 
-    def one_pair(pair, carry):
+    def one_group(places, pair, carry):
         start_pair(k, pair + 1)
-        buffer = lax.rem(pair, 2)
+        buffer, rows = lax.rem(pair, 2), places * BLK
 
         @pl.when(odd)
         def _():
-            x_ref[k, buffer, :, :, block_at(listed)] = jnp.zeros((2, 2 * BLK, BLK), x_ref.dtype)
-
-        def one_place(place, inner):
-            def arrived(slot, innermost):
-                there = x_ref.at[k, buffer, :, block_at(place - 2 * pair), block_at(slot)]
+            x_ref[k, buffer, :, pl.ds(0, rows), block_at(listed)] = jnp.zeros((2, rows, BLK), x_ref.dtype)
+
+        def arrived(slot, inner):
+            for place in range(places):
+                there = x_ref.at[k, buffer, :, pl.ds(place * BLK, BLK), block_at(slot)]
                 pltpu.make_async_copy(there, there, x_sems.at[k, buffer]).wait()
-                return innermost
-
-            return lax.fori_loop(0, listed, arrived, inner)
-
-        lax.fori_loop(2 * pair, jnp.minimum(2 * pair + 2, placed), one_place, 0)
+            return inner
+
+        lax.fori_loop(0, listed, arrived, 0)
         for count in range(1, w_ref.shape[1] // DEPTH + 1):
 
             @pl.when(steps == count)
             def _(count=count):
                 for half in range(2):
                     columns = w_ref.at[k, :, pl.ds(2 * half * width, 2 * width)]
-                    parts = product(x_ref.at[k, buffer], columns, pl.ds(0, 2 * BLK), pl.ds(0, count * DEPTH))
+                    parts = product(x_ref.at[k, buffer], columns, pl.ds(0, rows), pl.ds(0, count * DEPTH))
                     for q in range(2):
-                        v_ref[:, pl.ds((2 * half + q) * width, width)] = parts[q]
-
-        @pl.when(2 * pair + 1 >= placed)
-        def _():
-            v_ref[pl.ds(BLK, BLK), :] = jnp.zeros((BLK, v_ref.shape[1]), v_ref.dtype)
-            l_ref[k, block_at(2 * pair + 1), :] = jnp.zeros((BLK, l_ref.shape[2]), l_ref.dtype)
-
-        left = l_ref[k, block_at(pair, 2 * BLK), :]
-        rest = v_ref[...]
+                        v_ref[pl.ds(0, rows), pl.ds((2 * half + q) * width, width)] = parts[q]
+
+        rest = v_ref[pl.ds(0, rows), :]
         for piece in range(3):
             kept = rest.astype(jnp.bfloat16)
-            r_ref[pl.ds(piece * 2 * BLK, 2 * BLK), :] = kept
+            r_ref[pl.ds(piece * rows, rows), :] = kept
             rest = rest - kept.astype(jnp.float32)
+        left = l_ref[k, pl.ds(pl.multiple_of(pair * 2 * BLK, 2 * BLK), rows), :]
         for p in range(2):
             turned = jnp.concatenate(
                 [left[:, (2 * h + p) * width : (2 * h + p + 1) * width].T for h in range(2)], axis=0
             )
             turned = jnp.concatenate([turned] * 3, axis=1)
-            acc_ref[p] += jnp.dot(turned, r_ref[...], preferred_element_type=jnp.float32)
+            acc_ref[p] += jnp.dot(turned, r_ref[pl.ds(0, 3 * rows), :], preferred_element_type=jnp.float32)
         return carry
 
     @pl.when((listed > 0) & (placed > 0))
@@ -295,7 +294,12 @@
         def _():
             w_ref[k, block_at(listed), :] = jnp.zeros((BLK, w_ref.shape[2]), w_ref.dtype)
 
-        lax.fori_loop(0, lax.div(placed + 1, 2), one_pair, 0)
+        pairs = lax.div(placed, 2)
+        lax.fori_loop(0, pairs, functools.partial(one_group, 2), 0)
+
+        @pl.when(lax.rem(placed, 2) != 0)
+        def _():
+            one_group(1, pairs, 0)
 
     core = tab_ref[0, COUNTS, 2]
     per_half = width // chunk_rows
@@ -312,16 +316,16 @@
 def vmem_limit(scratch, blocks):
     held = [x for x in scratch if x.dtype in (jnp.bfloat16, jnp.float32)]
     size = sum(math.prod(x.shape) * jnp.dtype(x.dtype).itemsize for x in held)
-    return size + 2 * sum(math.prod(shape) * 4 for shape in blocks) + 5 * 2**20
+    return size + 2 * sum(math.prod(shape) * 4 for shape in blocks) + 2 * 2**20
 
 
 def make_values(tab, a, stacks, entries, sub):
     supernodes, early_count = stacks[0].shape[:2]
     rows, width = a.shape[1], stacks[0].shape[4]
     slots = tab.shape[2] + tab.shape[2] % CH
-    tile = max(t for t in range(BLK, min(rows, 512) + 1, BLK) if rows % t == 0)
+    tile = max(t for t in range(BLK, min(rows, 768) + 1, BLK) if rows % t == 0)
     out_spec = pl.BlockSpec((1, 2, tile, width), lambda k, m, _: (k, 0, m, 0))
-    out = jax.ShapeDtypeStruct((supernodes, 2, rows, width), jnp.float32)
+    out = pltpu.HBM((supernodes, 2, rows, width), jnp.float32)
     scratch = [
         pltpu.VMEM((2, 2, tile, slots * BLK), jnp.bfloat16),
         pltpu.VMEM((supernodes, slots * BLK, 4 * width), jnp.bfloat16),

time: 96.2 us -> 89.7 us (0.932); the launches traced: 97.1 us -> 88.3 us
  Pallas kernels: 30.9 us -> 22.7 us
  starting transfers between devices: 29.4 us -> 34.6 us
  waiting for transfers between devices: 23.8 us -> 19.7 us
  local copies, waits for them, and re-layouts: 5.54 us -> 3.93 us
    pallas_call x1, Pallas kernels: 16 us -> 11.5 us  [make_values(): pl.pallas_call(functools.partial(values_kernel, entries, early_count, sub...]
    pallas_call x1, Pallas kernels: 10.4 us -> 6.71 us  [make_gram(): pl.pallas_call(functools.partial(gram_kernel, entries, early_count, sub),...]
    ppermute x1, waiting for transfers between devices: 2.64 us -> 0.45 us  [gather_shares(): lax.ppermute(jnp.stack(own), 'row', [(i, i ^ 1) for i in range(n_row)])]
    ppermute x1, starting transfers between devices: 0.01 us -> 1.62 us  [local(): values = mine + lax.ppermute(theirs, 'col', swap)]
    unnamed x27 -> x25, local copies, waits for them, and re-layouts: 5.42 us -> 3.82 us
    ppermute x1, starting transfers between devices: 0.07 us -> 1.47 us  [gather_shares(): lax.ppermute(jnp.stack(own), 'row', [(i, i ^ 1) for i in range(n_row)])]
    ppermute x1, starting transfers between devices: 0.07 us -> 1.47 us  [scatter_sum(): lax.ppermute(sent, 'row', route)]
    ppermute x1, waiting for transfers between devices: 4.25 us -> 2.86 us  [scatter_sum(): lax.ppermute(sent, 'row', route)]
  transfers between devices with their start and end apart: 28 -> 28, of which waited for: 12 -> 12; matrix products, arithmetic and copies ran while one was open for 6% -> 6% of each run, Pallas kernels for 19% -> 16%
where the time goes in v2:
time: 89.7 us; the launch traced here: 88.3 us
  starting transfers between devices  34.6 us (39%)
  Pallas kernels  22.7 us (25%)
  waiting for transfers between devices  19.7 us (22%)
  other arithmetic  6.49 us (7%)
  local copies, waits for them, and re-layouts  3.93 us (4%)
  between operations  0.92 us (1%)
    ppermute x6, starting transfers between devices, local(): up[k] = lax.ppermute(up[k], 'row', ahead)  12.8 us
    pallas_call x1, Pallas kernels, make_values(): pl.pallas_call(functools.partial(values_kernel, entries, early_count, sub...  11.5 us
    ppermute x3, starting transfers between devices, scatter_sum(): came.append(lax.ppermute(sent, 'row', route))  7.07 us
    pallas_call x1, Pallas kernels, make_gram(): pl.pallas_call(functools.partial(gram_kernel, entries, early_count, sub),...  6.71 us
    add x1, other arithmetic, local(): values = mine + lax.ppermute(theirs, 'col', swap)  4.82 us
    ppermute x3, waiting for transfers between devices, gather_shares(): lax.ppermute(share, 'row', [(i, (i + 2 * d) % n_row) for i in range(n_row)])  4.68 us
    ppermute x3, starting transfers between devices, gather_shares(): lax.ppermute(share, 'row', [(i, (i + 2 * d) % n_row) for i in range(n_row)])  3.87 us
    unnamed x25, local copies, waits for them, and re-layouts  3.82 us
  transfers between devices with their start and end apart: 28, of which 12 were waited for; matrix products, arithmetic and copies ran while one was open for 6% of the time, Pallas kernels for 16%

profile of v2, /device:TPU:0, one launch (start us, length us, event | category | flops | bytes accessed | tf_op | source)
XLA Modules:
  0.0 88.3 jit_solution(12963943130259792195)
XLA Ops:
  1.7 3.1 %collective-permute-start = (bf16[2,256,128]{2,1,0:T(8,128)(2,1)S(1)}, bf16[2,256,128]{2,1,0:T(8,128)(2,1)S(1)}, u32[]{:S(2)}, u32[]{:S(2)}) collective-permute-start(bf16[2,256,128]{2,1,0:T(8,128)(2,1)S(1)} %get-tuple-element.40), channel_id=1, source_target_pairs={{0,4},{4,8},{8,12},{12,14},{14,10},{10,6},{6,2},{2,0},{1,5},{5,9},... | collective-permute-start | bytes 393224 | tf_op jit(solution)/shard_map/ppermute | solution.py:460
  4.8 2.0 %collective-permute-start.4 = (bf16[2,256,128]{2,1,0:T(8,128)(2,1)S(1)}, bf16[2,256,128]{2,1,0:T(8,128)(2,1)S(1)}, u32[]{:S(2)}, u32[]{:S(2)}) collective-permute-start(bf16[2,256,128]{2,1,0:T(8,128)(2,1)S(1)} %get-tuple-element.39), channel_id=1, source_target_pairs={{0,4},{4,8},{8,12},{12,14},{14,10},{10,6},{6,2},{2,0},{1,5},{5,9},... | collective-permute-start | bytes 393224 | tf_op jit(solution)/shard_map/ppermute | solution.py:460
  6.8 2.4 %table.1.tab_ref = s32[2,6,16]{2,1,0:T(8,128)} custom-call(s32[2,16]{1,0:T(2,128)} %lists_ref.1, s32[96]{0:T(128)} %order_ref.1), custom_call_target="tpu_custom_call" | custom-call | tf_op jit(solution)/shard_map/table/pallas_call | solution.py:67
  9.2 2.1 %collective-permute-start.2 = (bf16[2,256,128]{2,1,0:T(8,128)(2,1)S(1)}, bf16[2,256,128]{2,1,0:T(8,128)(2,1)S(1)}, u32[]{:S(2)}, u32[]{:S(2)}) collective-permute-start(bf16[2,256,128]{2,1,0:T(8,128)(2,1)S(1)} %collective-permute-done), channel_id=1, source_target_pairs={{0,4},{4,8},{8,12},{12,14},{14,10},{10,6},{6,2},{2,0},{1,5},{5,9},... | collective-permute-start | bytes 393224 | tf_op jit(solution)/shard_map/ppermute | solution.py:460
  11.3 2.0 %collective-permute-start.6 = (bf16[2,256,128]{2,1,0:T(8,128)(2,1)S(1)}, bf16[2,256,128]{2,1,0:T(8,128)(2,1)S(1)}, u32[]{:S(2)}, u32[]{:S(2)}) collective-permute-start(bf16[2,256,128]{2,1,0:T(8,128)(2,1)S(1)} %collective-permute-done.4), channel_id=1, source_target_pairs={{0,4},{4,8},{8,12},{12,14},{14,10},{10,6},{6,2},{2,0},{1,5},{5,9},... | collective-permute-start | bytes 393224 | tf_op jit(solution)/shard_map/ppermute | solution.py:460
  13.4 2.1 %collective-permute-done.2 = bf16[2,256,128]{2,1,0:T(8,128)(2,1)S(1)} collective-permute-done((bf16[2,256,128]{2,1,0:T(8,128)(2,1)S(1)}, bf16[2,256,128]{2,1,0:T(8,128)(2,1)S(1)}, u32[]{:S(2)}, u32[]{:S(2)}) %collective-permute-start.2) | collective-permute-done | bytes 131104 | tf_op jit(solution)/shard_map/ppermute | solution.py:460
  15.5 1.8 %collective-permute-start.8 = (bf16[2,256,128]{2,1,0:T(8,128)(2,1)S(1)}, bf16[2,256,128]{2,1,0:T(8,128)(2,1)S(1)}, u32[]{:S(2)}, u32[]{:S(2)}) collective-permute-start(bf16[2,256,128]{2,1,0:T(8,128)(2,1)S(1)} %collective-permute-done.2), channel_id=1, source_target_pairs={{0,4},{4,8},{8,12},{12,14},{14,10},{10,6},{6,2},{2,0},{1,5},{5,9},... | collective-permute-start | bytes 393224 | tf_op jit(solution)/shard_map/ppermute | solution.py:460
  18.3 1.8 %collective-permute-start.12 = (bf16[2,256,128]{2,1,0:T(8,128)(2,1)S(1)}, bf16[2,256,128]{2,1,0:T(8,128)(2,1)S(1)}, u32[]{:S(2)}, u32[]{:S(2)}) collective-permute-start(bf16[2,256,128]{2,1,0:T(8,128)(2,1)S(1)} %collective-permute-done.6), channel_id=1, source_target_pairs={{0,4},{4,8},{8,12},{12,14},{14,10},{10,6},{6,2},{2,0},{1,5},{5,9},... | collective-permute-start | bytes 393224 | tf_op jit(solution)/shard_map/ppermute | solution.py:460
  21.3 1.7 %collective-permute-start.10 = (bf16[1,256,128]{2,1,0:T(8,128)(2,1)S(1)}, bf16[1,256,128]{2,1,0:T(8,128)(2,1)S(1)}, u32[]{:S(2)}, u32[]{:S(2)}) collective-permute-start(bf16[1,256,128]{2,1,0:T(8,128)(2,1)S(1)} %slice.26), channel_id=1, source_target_pairs={{0,4},{4,8},{8,12},{12,14},{14,10},{10,6},{6,2},{2,0},{1,5},{5,9},... | collective-permute-start | bytes 196616 | tf_op jit(solution)/shard_map/ppermute | solution.py:466
  23.6 1.8 %collective-permute-start.14 = (bf16[1,256,128]{2,1,0:T(8,128)(2,1)S(1)}, bf16[1,256,128]{2,1,0:T(8,128)(2,1)S(1)}, u32[]{:S(2)}, u32[]{:S(2)}) collective-permute-start(bf16[1,256,128]{2,1,0:T(8,128)(2,1)S(1)} %slice.28), channel_id=1, source_target_pairs={{0,4},{4,8},{8,12},{12,14},{14,10},{10,6},{6,2},{2,0},{1,5},{5,9},... | collective-permute-start | bytes 196616 | tf_op jit(solution)/shard_map/ppermute | solution.py:466
  30.0 2.3 %collective-permute-done.17.sib1 = bf16[2,3,2,256,128]{4,3,2,1,0:T(8,128)(2,1)S(1)} collective-permute-done((bf16[2,3,2,256,128]{4,3,2,1,0:T(8,128)(2,1)S(1)}, bf16[2,3,2,256,128]{4,3,2,1,0:T(8,128)(2,1)S(1)}, u32[]{:S(2)}, u32[]{:S(2)}) %collective-permute-start.17) | collective-permute-done | bytes 786464 | tf_op jit(solution)/shard_map/ppermute | solution.py:473
  32.3 6.7 %gram.1 = (f32[8,2,2,32,128]{4,3,2,1,0:T(8,128)S(1)}, f32[8,2,2,32,128]{4,3,2,1,0:T(8,128)}) custom-call(s32[2,6,16]{2,1,0:T(8,128)S(1)} %copy-done.3, bf16[2,1536,6144]{2,1,0:T(8,128)(2,1)} %a_ref.3, bf16[2,5,2,256,128]{4,3,2,1,0:T(8,128)(2,1)S(1)} %pad_maximum_fusion.own0, bf16[2,3,2,256,128]{4,3,2,1,0:T(8,128)(2,1)S(1)} %pad_maximum_fusion.1.own1, ...), custom_call_target="tpu_custom_call" | custom-call | flops 1073741824 | bytes 8388608 | tf_op jit(solution)/shard_map/gram/pallas_call | solution.py:372
  41.1 1.9 %collective-permute-done.18 = f32[8,2,2,32,128]{4,3,2,1,0:T(8,128)} collective-permute-done((f32[8,2,2,32,128]{4,3,2,1,0:T(8,128)}, f32[8,2,2,32,128]{4,3,2,1,0:T(8,128)}, u32[]{:S(2)}, u32[]{:S(2)}) %collective-permute-start.18) | collective-permute-done | bytes 524320 | tf_op jit(solution)/shard_map/ppermute | solution.py:476
  44.3 2.4 %collective-permute-start.19 = (f32[2,2,2,32,128]{4,3,2,1,0:T(8,128)S(1)}, f32[2,2,2,32,128]{4,3,2,1,0:T(8,128)S(1)}, u32[]{:S(2)}, u32[]{:S(2)}) collective-permute-start(f32[2,2,2,32,128]{4,3,2,1,0:T(8,128)S(1)} %get-tuple-element.36), channel_id=1, source_target_pairs={{0,4},{2,6},{4,8},{6,10},{8,12},{10,14},{12,0},{14,2},{1,5},{3,7},... | collective-permute-start | bytes 393224 | tf_op jit(solution)/shard_map/ppermute | solution.py:399
  46.7 1.9 %collective-permute-start.20 = (f32[2,2,2,32,128]{4,3,2,1,0:T(8,128)S(1)}, f32[2,2,2,32,128]{4,3,2,1,0:T(8,128)S(1)}, u32[]{:S(2)}, u32[]{:S(2)}) collective-permute-start(f32[2,2,2,32,128]{4,3,2,1,0:T(8,128)S(1)} %get-tuple-element.35), channel_id=1, source_target_pairs={{0,8},{2,10},{4,12},{6,14},{8,0},{10,2},{12,4},{14,6},{1,9},{3,11}... | collective-permute-start | bytes 393224 | tf_op jit(solution)/shard_map/ppermute | solution.py:399
  48.6 2.8 %collective-permute-start.21 = (f32[2,2,2,32,128]{4,3,2,1,0:T(8,128)S(1)}, f32[2,2,2,32,128]{4,3,2,1,0:T(8,128)S(1)}, u32[]{:S(2)}, u32[]{:S(2)}) collective-permute-start(f32[2,2,2,32,128]{4,3,2,1,0:T(8,128)S(1)} %get-tuple-element.34), channel_id=1, source_target_pairs={{0,12},{2,14},{4,0},{6,2},{8,4},{10,6},{12,8},{14,10},{1,13},{3,15... | collective-permute-start | bytes 393224 | tf_op jit(solution)/shard_map/ppermute | solution.py:399
  52.6 11.5 %values.1 = (f32[2,2,1536,128]{3,2,1,0:T(8,128)}, f32[2,2,1536,128]{3,2,1,0:T(8,128)}) custom-call(s32[2,6,16]{2,1,0:T(8,128)S(1)} %copy-done.3, bf16[2,1536,6144]{2,1,0:T(8,128)(2,1)} %a_ref.3, bf16[2,5,2,256,128]{4,3,2,1,0:T(8,128)(2,1)S(1)} %pad_maximum_fusion.own0, bf16[2,3,2,256,128]{4,3,2,1,0:T(8,128)(2,1)S(1)} %pad_maximum_fusion.1.own1, ...), custom_call_target="tpu_custom_call" | custom-call | flops 6442450944 | bytes 16777216 | tf_op jit(solution)/shard_map/values/pallas_call | solution.py:335
  65.6 2.9 %collective-permute-done.22 = f32[2,2,32,128]{3,2,1,0:T(8,128)S(1)} collective-permute-done((f32[2,2,32,128]{3,2,1,0:T(8,128)S(1)}, f32[2,2,32,128]{3,2,1,0:T(8,128)S(1)}, u32[]{:S(2)}, u32[]{:S(2)}) %collective-permute-start.22) | collective-permute-done | bytes 65568 | tf_op jit(solution)/shard_map/ppermute | solution.py:406
  68.5 1.6 %collective-permute-start.27 = (f32[2,2,1536,128]{3,2,1,0:T(8,128)}, f32[2,2,1536,128]{3,2,1,0:T(8,128)}, u32[]{:S(2)}, u32[]{:S(2)}) collective-permute-start(f32[2,2,1536,128]{3,2,1,0:T(8,128)} %get-tuple-element.31), channel_id=1, source_target_pairs={{0,1},{1,0},{2,3},{3,2},{4,5},{5,4},{6,7},{7,6},{8,9},{9,8},{10,11... | collective-permute-start | bytes 9437192 | tf_op jit(solution)/shard_map/ppermute | solution.py:480
  71.0 3.0 %collective-permute-start.25 = (f32[2,2,32,128]{3,2,1,0:T(8,128)S(1)}, f32[2,2,32,128]{3,2,1,0:T(8,128)S(1)}, u32[]{:S(2)}, u32[]{:S(2)}) collective-permute-start(f32[2,2,32,128]{3,2,1,0:T(8,128)S(1)} %bitcast_add_fusion.1.refs_0_), channel_id=1, source_target_pairs={{0,12},{2,14},{4,0},{6,2},{8,4},{10,6},{12,8},{14,10},{1,13},{3,15... | collective-permute-start | bytes 196616 | tf_op jit(solution)/shard_map/ppermute | solution.py:427
  74.0 3.0 %collective-permute-done.23.refs_1_ = f32[2,2,32,128]{3,2,1,0:T(8,128)S(1)} collective-permute-done((f32[2,2,32,128]{3,2,1,0:T(8,128)S(1)}, f32[2,2,32,128]{3,2,1,0:T(8,128)S(1)}, u32[]{:S(2)}, u32[]{:S(2)}) %collective-permute-start.23) | collective-permute-done | bytes 65568 | tf_op jit(solution)/shard_map/ppermute | solution.py:427
  77.0 1.7 %collective-permute-done.24.refs_2_ = f32[2,2,32,128]{3,2,1,0:T(8,128)S(1)} collective-permute-done((f32[2,2,32,128]{3,2,1,0:T(8,128)S(1)}, f32[2,2,32,128]{3,2,1,0:T(8,128)S(1)}, u32[]{:S(2)}, u32[]{:S(2)}) %collective-permute-start.24) | collective-permute-done | bytes 65568 | tf_op jit(solution)/shard_map/ppermute | solution.py:427
  80.2 4.8 %add.80 = f32[2,2,1536,128]{3,2,1,0:T(8,128)} add(f32[2,2,1536,128]{3,2,1,0:T(8,128)} %get-tuple-element.30, f32[2,2,1536,128]{3,2,1,0:T(8,128)} %collective-permute-done.27) | non-fusion elementwise | flops 786432 | bytes 9437184 | tf_op jit(solution)/shard_map/add | solution.py:480
  86.2 2.1 %place.1 = f32[2,2,256,128]{3,2,1,0:T(8,128)} custom-call(bf16[2,2,256,128]{3,2,1,0:T(8,128)(2,1)} %diag_ref.1, f32[2,2,32,128]{3,2,1,0:T(8,128)} %copy-done.4, f32[2,2,32,128]{3,2,1,0:T(8,128)} %copy-done.6, f32[2,2,32,128]{3,2,1,0:T(8,128)} %copy-done.7, f32[2,2,32,128]{3,2,1,0:T(8,128)} %copy-done.8, f32[4,2,2,32,128]{4,3,2,1,0:T(8,128)} %copy-done.5), custom_call_target="tpu_custom_call" | custom-call | tf_op jit(solution)/shard_map/place/pallas_call | solution.py:431
  (80 shorter events, 18.1 us)
Async XLA Ops:
  1.7 7.5 %collective-permute-start = (bf16[2,256,128]{2,1,0:T(8,128)(2,1)S(1)}, bf16[2,256,128]{2,1,0:T(8,128)(2,1)S(1)}, u32[]{:S(2)}, u32[]{:S(2)}) collective-permute-start(bf16[2,256,128]{2,1,0:T(8,128)(2,1)S(1)} %get-tuple-element.40), channel_id=1, source_target_pairs={{0,4},{4,8},{8,12},{12,14},{14,10},{10,6},{6,2},{2,0},{1,5},{5,9},... | collective-permute-start | bytes 393224 | tf_op jit(solution)/shard_map/ppermute | solution.py:460
  4.7 6.5 %collective-permute-start.1 = (bf16[2,256,128]{2,1,0:T(8,128)(2,1)S(1)}, bf16[2,256,128]{2,1,0:T(8,128)(2,1)S(1)}, u32[]{:S(2)}, u32[]{:S(2)}) collective-permute-start(bf16[2,256,128]{2,1,0:T(8,128)(2,1)S(1)} %get-tuple-element.40), channel_id=1, source_target_pairs={{4,0},{8,4},{12,8},{14,12},{10,14},{6,10},{2,6},{0,2},{5,1},{9,5},... | collective-permute-start | bytes 393224 | tf_op jit(solution)/shard_map/ppermute | solution.py:461
  4.8 6.5 %collective-permute-start.4 = (bf16[2,256,128]{2,1,0:T(8,128)(2,1)S(1)}, bf16[2,256,128]{2,1,0:T(8,128)(2,1)S(1)}, u32[]{:S(2)}, u32[]{:S(2)}) collective-permute-start(bf16[2,256,128]{2,1,0:T(8,128)(2,1)S(1)} %get-tuple-element.39), channel_id=1, source_target_pairs={{0,4},{4,8},{8,12},{12,14},{14,10},{10,6},{6,2},{2,0},{1,5},{5,9},... | collective-permute-start | bytes 393224 | tf_op jit(solution)/shard_map/ppermute | solution.py:460
  6.8 6.5 %collective-permute-start.5 = (bf16[2,256,128]{2,1,0:T(8,128)(2,1)S(1)}, bf16[2,256,128]{2,1,0:T(8,128)(2,1)S(1)}, u32[]{:S(2)}, u32[]{:S(2)}) collective-permute-start(bf16[2,256,128]{2,1,0:T(8,128)(2,1)S(1)} %get-tuple-element.39), channel_id=1, source_target_pairs={{4,0},{8,4},{12,8},{14,12},{10,14},{6,10},{2,6},{0,2},{5,1},{9,5},... | collective-permute-start | bytes 393224 | tf_op jit(solution)/shard_map/ppermute | solution.py:461
  9.2 6.3 %collective-permute-start.2 = (bf16[2,256,128]{2,1,0:T(8,128)(2,1)S(1)}, bf16[2,256,128]{2,1,0:T(8,128)(2,1)S(1)}, u32[]{:S(2)}, u32[]{:S(2)}) collective-permute-start(bf16[2,256,128]{2,1,0:T(8,128)(2,1)S(1)} %collective-permute-done), channel_id=1, source_target_pairs={{0,4},{4,8},{8,12},{12,14},{14,10},{10,6},{6,2},{2,0},{1,5},{5,9},... | collective-permute-start | bytes 393224 | tf_op jit(solution)/shard_map/ppermute | solution.py:460
  11.2 6.1 %collective-permute-start.3 = (bf16[2,256,128]{2,1,0:T(8,128)(2,1)S(1)}, bf16[2,256,128]{2,1,0:T(8,128)(2,1)S(1)}, u32[]{:S(2)}, u32[]{:S(2)}) collective-permute-start(bf16[2,256,128]{2,1,0:T(8,128)(2,1)S(1)} %collective-permute-done.1), channel_id=1, source_target_pairs={{4,0},{8,4},{12,8},{14,12},{10,14},{6,10},{2,6},{0,2},{5,1},{9,5},... | collective-permute-start | bytes 393224 | tf_op jit(solution)/shard_map/ppermute | solution.py:461
  11.3 7.1 %collective-permute-start.6 = (bf16[2,256,128]{2,1,0:T(8,128)(2,1)S(1)}, bf16[2,256,128]{2,1,0:T(8,128)(2,1)S(1)}, u32[]{:S(2)}, u32[]{:S(2)}) collective-permute-start(bf16[2,256,128]{2,1,0:T(8,128)(2,1)S(1)} %collective-permute-done.4), channel_id=1, source_target_pairs={{0,4},{4,8},{8,12},{12,14},{14,10},{10,6},{6,2},{2,0},{1,5},{5,9},... | collective-permute-start | bytes 393224 | tf_op jit(solution)/shard_map/ppermute | solution.py:460
  13.3 6.9 %collective-permute-start.7 = (bf16[2,256,128]{2,1,0:T(8,128)(2,1)S(1)}, bf16[2,256,128]{2,1,0:T(8,128)(2,1)S(1)}, u32[]{:S(2)}, u32[]{:S(2)}) collective-permute-start(bf16[2,256,128]{2,1,0:T(8,128)(2,1)S(1)} %collective-permute-done.5), channel_id=1, source_target_pairs={{4,0},{8,4},{12,8},{14,12},{10,14},{6,10},{2,6},{0,2},{5,1},{9,5},... | collective-permute-start | bytes 393224 | tf_op jit(solution)/shard_map/ppermute | solution.py:461
  15.5 5.7 %collective-permute-start.8 = (bf16[2,256,128]{2,1,0:T(8,128)(2,1)S(1)}, bf16[2,256,128]{2,1,0:T(8,128)(2,1)S(1)}, u32[]{:S(2)}, u32[]{:S(2)}) collective-permute-start(bf16[2,256,128]{2,1,0:T(8,128)(2,1)S(1)} %collective-permute-done.2), channel_id=1, source_target_pairs={{0,4},{4,8},{8,12},{12,14},{14,10},{10,6},{6,2},{2,0},{1,5},{5,9},... | collective-permute-start | bytes 393224 | tf_op jit(solution)/shard_map/ppermute | solution.py:460
  17.3 5.7 %collective-permute-start.9 = (bf16[2,256,128]{2,1,0:T(8,128)(2,1)S(1)}, bf16[2,256,128]{2,1,0:T(8,128)(2,1)S(1)}, u32[]{:S(2)}, u32[]{:S(2)}) collective-permute-start(bf16[2,256,128]{2,1,0:T(8,128)(2,1)S(1)} %collective-permute-done.3), channel_id=1, source_target_pairs={{4,0},{8,4},{12,8},{14,12},{10,14},{6,10},{2,6},{0,2},{5,1},{9,5},... | collective-permute-start | bytes 393224 | tf_op jit(solution)/shard_map/ppermute | solution.py:461
  18.3 5.2 %collective-permute-start.12 = (bf16[2,256,128]{2,1,0:T(8,128)(2,1)S(1)}, bf16[2,256,128]{2,1,0:T(8,128)(2,1)S(1)}, u32[]{:S(2)}, u32[]{:S(2)}) collective-permute-start(bf16[2,256,128]{2,1,0:T(8,128)(2,1)S(1)} %collective-permute-done.6), channel_id=1, source_target_pairs={{0,4},{4,8},{8,12},{12,14},{14,10},{10,6},{6,2},{2,0},{1,5},{5,9},... | collective-permute-start | bytes 393224 | tf_op jit(solution)/shard_map/ppermute | solution.py:460
  20.2 5.2 %collective-permute-start.13 = (bf16[2,256,128]{2,1,0:T(8,128)(2,1)S(1)}, bf16[2,256,128]{2,1,0:T(8,128)(2,1)S(1)}, u32[]{:S(2)}, u32[]{:S(2)}) collective-permute-start(bf16[2,256,128]{2,1,0:T(8,128)(2,1)S(1)} %collective-permute-done.7), channel_id=1, source_target_pairs={{4,0},{8,4},{12,8},{14,12},{10,14},{6,10},{2,6},{0,2},{5,1},{9,5},... | collective-permute-start | bytes 393224 | tf_op jit(solution)/shard_map/ppermute | solution.py:461
  21.3 4.5 %collective-permute-start.10 = (bf16[1,256,128]{2,1,0:T(8,128)(2,1)S(1)}, bf16[1,256,128]{2,1,0:T(8,128)(2,1)S(1)}, u32[]{:S(2)}, u32[]{:S(2)}) collective-permute-start(bf16[1,256,128]{2,1,0:T(8,128)(2,1)S(1)} %slice.26), channel_id=1, source_target_pairs={{0,4},{4,8},{8,12},{12,14},{14,10},{10,6},{6,2},{2,0},{1,5},{5,9},... | collective-permute-start | bytes 196616 | tf_op jit(solution)/shard_map/ppermute | solution.py:466
  23.5 8.8 %collective-permute-start.16 = (bf16[2,5,2,256,128]{4,3,2,1,0:T(8,128)(2,1)S(1)}, bf16[2,5,2,256,128]{4,3,2,1,0:T(8,128)(2,1)S(1)}, u32[]{:S(2)}, u32[]{:S(2)}) collective-permute-start(bf16[2,5,2,256,128]{4,3,2,1,0:T(8,128)(2,1)S(1)} %pad_maximum_fusion.own0), channel_id=1, source_target_pairs={{0,1},{1,0},{2,3},{3,2},{4,5},{5,4},{6,7},{7,6},{8,9},{9,8},{10,11... | collective-permute-start | bytes 3932168 | tf_op jit(solution)/shard_map/ppermute | solution.py:473
  23.6 4.7 %collective-permute-start.14 = (bf16[1,256,128]{2,1,0:T(8,128)(2,1)S(1)}, bf16[1,256,128]{2,1,0:T(8,128)(2,1)S(1)}, u32[]{:S(2)}, u32[]{:S(2)}) collective-permute-start(bf16[1,256,128]{2,1,0:T(8,128)(2,1)S(1)} %slice.28), channel_id=1, source_target_pairs={{0,4},{4,8},{8,12},{12,14},{14,10},{10,6},{6,2},{2,0},{1,5},{5,9},... | collective-permute-start | bytes 196616 | tf_op jit(solution)/shard_map/ppermute | solution.py:466
  44.3 19.7 %collective-permute-start.19 = (f32[2,2,2,32,128]{4,3,2,1,0:T(8,128)S(1)}, f32[2,2,2,32,128]{4,3,2,1,0:T(8,128)S(1)}, u32[]{:S(2)}, u32[]{:S(2)}) collective-permute-start(f32[2,2,2,32,128]{4,3,2,1,0:T(8,128)S(1)} %get-tuple-element.36), channel_id=1, source_target_pairs={{0,4},{2,6},{4,8},{6,10},{8,12},{10,14},{12,0},{14,2},{1,5},{3,7},... | collective-permute-start | bytes 393224 | tf_op jit(solution)/shard_map/ppermute | solution.py:399
  46.7 17.4 %collective-permute-start.20 = (f32[2,2,2,32,128]{4,3,2,1,0:T(8,128)S(1)}, f32[2,2,2,32,128]{4,3,2,1,0:T(8,128)S(1)}, u32[]{:S(2)}, u32[]{:S(2)}) collective-permute-start(f32[2,2,2,32,128]{4,3,2,1,0:T(8,128)S(1)} %get-tuple-element.35), channel_id=1, source_target_pairs={{0,8},{2,10},{4,12},{6,14},{8,0},{10,2},{12,4},{14,6},{1,9},{3,11}... | collective-permute-start | bytes 393224 | tf_op jit(solution)/shard_map/ppermute | solution.py:399
  48.6 15.5 %collective-permute-start.21 = (f32[2,2,2,32,128]{4,3,2,1,0:T(8,128)S(1)}, f32[2,2,2,32,128]{4,3,2,1,0:T(8,128)S(1)}, u32[]{:S(2)}, u32[]{:S(2)}) collective-permute-start(f32[2,2,2,32,128]{4,3,2,1,0:T(8,128)S(1)} %get-tuple-element.34), channel_id=1, source_target_pairs={{0,12},{2,14},{4,0},{6,2},{8,4},{10,6},{12,8},{14,10},{1,13},{3,15... | collective-permute-start | bytes 393224 | tf_op jit(solution)/shard_map/ppermute | solution.py:399
  64.2 4.3 %collective-permute-start.22 = (f32[2,2,32,128]{3,2,1,0:T(8,128)S(1)}, f32[2,2,32,128]{3,2,1,0:T(8,128)S(1)}, u32[]{:S(2)}, u32[]{:S(2)}) collective-permute-start(f32[2,2,32,128]{3,2,1,0:T(8,128)S(1)} %dynamic-slice_bitcast_fusion.3), channel_id=1, source_target_pairs={{0,2},{2,0},{4,6},{6,4},{8,10},{10,8},{12,14},{14,12},{1,3},{3,1},... | collective-permute-start | bytes 196616 | tf_op jit(solution)/shard_map/ppermute | solution.py:406
  68.5 11.7 %collective-permute-start.27 = (f32[2,2,1536,128]{3,2,1,0:T(8,128)}, f32[2,2,1536,128]{3,2,1,0:T(8,128)}, u32[]{:S(2)}, u32[]{:S(2)}) collective-permute-start(f32[2,2,1536,128]{3,2,1,0:T(8,128)} %get-tuple-element.31), channel_id=1, source_target_pairs={{0,1},{1,0},{2,3},{3,2},{4,5},{5,4},{6,7},{7,6},{8,9},{9,8},{10,11... | collective-permute-start | bytes 9437192 | tf_op jit(solution)/shard_map/ppermute | solution.py:480
  70.2 6.8 %collective-permute-start.23 = (f32[2,2,32,128]{3,2,1,0:T(8,128)S(1)}, f32[2,2,32,128]{3,2,1,0:T(8,128)S(1)}, u32[]{:S(2)}, u32[]{:S(2)}) collective-permute-start(f32[2,2,32,128]{3,2,1,0:T(8,128)S(1)} %bitcast_add_fusion.1.refs_0_), channel_id=1, source_target_pairs={{0,4},{2,6},{4,8},{6,10},{8,12},{10,14},{12,0},{14,2},{1,5},{3,7},... | collective-permute-start | bytes 196616 | tf_op jit(solution)/shard_map/ppermute | solution.py:427
  70.2 8.5 %collective-permute-start.24 = (f32[2,2,32,128]{3,2,1,0:T(8,128)S(1)}, f32[2,2,32,128]{3,2,1,0:T(8,128)S(1)}, u32[]{:S(2)}, u32[]{:S(2)}) collective-permute-start(f32[2,2,32,128]{3,2,1,0:T(8,128)S(1)} %bitcast_add_fusion.1.refs_0_), channel_id=1, source_target_pairs={{0,8},{2,10},{4,12},{6,14},{8,0},{10,2},{12,4},{14,6},{1,9},{3,11}... | collective-permute-start | bytes 196616 | tf_op jit(solution)/shard_map/ppermute | solution.py:427
  71.0 7.7 %collective-permute-start.25 = (f32[2,2,32,128]{3,2,1,0:T(8,128)S(1)}, f32[2,2,32,128]{3,2,1,0:T(8,128)S(1)}, u32[]{:S(2)}, u32[]{:S(2)}) collective-permute-start(f32[2,2,32,128]{3,2,1,0:T(8,128)S(1)} %bitcast_add_fusion.1.refs_0_), channel_id=1, source_target_pairs={{0,12},{2,14},{4,0},{6,2},{8,4},{10,6},{12,8},{14,10},{1,13},{3,15... | collective-permute-start | bytes 196616 | tf_op jit(solution)/shard_map/ppermute | solution.py:427
  78.7 6.8 %collective-permute-start.26 = (f32[4,2,2,32,128]{4,3,2,1,0:T(8,128)S(1)}, f32[4,2,2,32,128]{4,3,2,1,0:T(8,128)S(1)}, u32[]{:S(2)}, u32[]{:S(2)}) collective-permute-start(f32[4,2,2,32,128]{4,3,2,1,0:T(8,128)S(1)} %pad_maximum_fusion.2), channel_id=1, source_target_pairs={{0,2},{2,0},{4,6},{6,4},{8,10},{10,8},{12,14},{14,12},{1,3},{3,1},... | collective-permute-start | bytes 786440 | tf_op jit(solution)/shard_map/ppermute | solution.py:428
  (13 other events, 68.1 us)

commit v3 on v2

--- a/solution.py
+++ b/solution.py
@@ -122,8 +122,7 @@
     return imag[:, width:] - real[:, :width], -(real[:, width:] + imag[:, :width])
 
 
-def values_kernel(entries, early_count, sub, tile, tab_ref, a_ref, own0, own1, sib0, sib1, *refs):
-    mine_ref, theirs_ref, x_ref, w_ref, x_sems, w_sems = refs
+def values_kernel(tile, tab_ref, a_ref, rows_ref, mine_ref, theirs_ref, x_ref, w_ref, x_sems, w_sems):
     k, step = pl.program_id(0), pl.program_id(1)
     supernodes, tiles = pl.num_programs(0), pl.num_programs(1)
     width = mine_ref.shape[3]
@@ -143,33 +142,22 @@
 
         lax.fori_loop(0, tab_ref[which, COUNTS, 0], one, 0)
 
-    def start_weights(which):
-        halves = ((own0, own1), (sib0, sib1))
-        rows = start_rows(tab_ref, COL_ENTRY, which, w_ref, w_sems, halves, entries, early_count, sub)
-        lax.fori_loop(0, tab_ref[which, COUNTS, 0], rows, 0)
+    def weights(which):
+        return pltpu.make_async_copy(rows_ref.at[which], w_ref.at[which], w_sems.at[which])
 
     @pl.when(now == 0)
     def _():
         start(now)
-        start_weights(0)
+        for which in range(w_ref.shape[0]):
+            weights(which).start()
 
     @pl.when(now + 1 < supernodes * tiles)
     def _():
         start(now + 1)
 
-    for which in range(1, w_ref.shape[0]):
-
-        @pl.when(now == which * tiles - 1)
-        def _(which=which):
-            start_weights(which)
-
     @pl.when(step == 0)
     def _():
-        @pl.when(lax.rem(listed, CH) != 0)
-        def _():
-            w_ref[k, block_at(listed), :] = jnp.zeros((BLK, w_ref.shape[2]), w_ref.dtype)
-
-        lax.fori_loop(0, listed, wait_rows(k, w_ref, w_sems, width, sub, 2), 0)
+        weights(k).wait()
 
     buffer = lax.rem(now, 2)
 
@@ -202,7 +190,7 @@
 
 
 def gram_kernel(entries, early_count, sub, tab_ref, a_ref, own0, own1, sib0, sib1, *refs):
-    mine_ref, theirs_ref, x_ref, w_ref, l_ref, v_ref, r_ref, acc_ref, x_sems, w_sems, l_sems = refs
+    mine_ref, theirs_ref, rows_ref, x_ref, w_ref, l_ref, v_ref, r_ref, acc_ref, x_sems, w_sems, l_sems, out_sem = refs
     k = pl.program_id(0)
     own, sib = (own0, own1), (sib0, sib1)
     width = mine_ref.shape[4]
@@ -231,23 +219,23 @@
             stacks = ((own, sib), entries, early_count, sub)
             there = tab_ref[which, COUNTS, 1]
             start_pair(which, 0)
-
-            @pl.when(there > 0)
-            def _(which=which, stacks=stacks):
-                lax.fori_loop(
-                    0, tab_ref[which, COUNTS, 0], start_rows(tab_ref, COL_ENTRY, which, w_ref, w_sems, *stacks), 0
-                )
-
+            lax.fori_loop(
+                0, tab_ref[which, COUNTS, 0], start_rows(tab_ref, COL_ENTRY, which, w_ref, w_sems, *stacks), 0
+            )
             lax.fori_loop(0, there, start_rows(tab_ref, ROW_ENTRY, which, l_ref, l_sems, *stacks), 0)
 
     acc_ref[...] = jnp.zeros_like(acc_ref)
     odd = lax.rem(listed, CH) != 0
     steps = lax.div(listed + (CH - 1), CH)
+    lax.fori_loop(0, listed, wait_rows(k, w_ref, w_sems, width, sub, 2), 0)
+
+    @pl.when(odd)
+    def _():
+        w_ref[k, block_at(listed), :] = jnp.zeros((BLK, w_ref.shape[2]), w_ref.dtype)
+
+    handed = pltpu.make_async_copy(w_ref.at[k], rows_ref.at[k], out_sem)
+    handed.start()
     lax.fori_loop(0, placed, wait_rows(k, l_ref, l_sems, width, sub, 2), 0)
-
-    @pl.when(placed > 0)
-    def _():
-        lax.fori_loop(0, listed, wait_rows(k, w_ref, w_sems, width, sub, 2), 0)
 
     def one_group(places, pair, carry):
         start_pair(k, pair + 1)
@@ -290,10 +278,6 @@
 
     @pl.when((listed > 0) & (placed > 0))
     def _():
-        @pl.when(odd)
-        def _():
-            w_ref[k, block_at(listed), :] = jnp.zeros((BLK, w_ref.shape[2]), w_ref.dtype)
-
         pairs = lax.div(placed, 2)
         lax.fori_loop(0, pairs, functools.partial(one_group, 2), 0)
 
@@ -311,6 +295,7 @@
                 real, imag = pl.ds(at, width), pl.ds(width + at, width)
                 out_ref[first + i, 0, 0] = acc_ref[0, rows, real] - acc_ref[1, rows, imag]
                 out_ref[first + i, 0, 1] = acc_ref[0, rows, imag] + acc_ref[1, rows, real]
+    handed.wait()
 
 
 def vmem_limit(scratch, blocks):
@@ -319,26 +304,25 @@
     return size + 2 * sum(math.prod(shape) * 4 for shape in blocks) + 2 * 2**20
 
 
-def make_values(tab, a, stacks, entries, sub):
-    supernodes, early_count = stacks[0].shape[:2]
-    rows, width = a.shape[1], stacks[0].shape[4]
+def make_values(tab, a, gathered):
+    supernodes, rows, width = gathered.shape[0], a.shape[1], gathered.shape[2] // 4
     slots = tab.shape[2] + tab.shape[2] % CH
     tile = max(t for t in range(BLK, min(rows, 768) + 1, BLK) if rows % t == 0)
     out_spec = pl.BlockSpec((1, 2, tile, width), lambda k, m, _: (k, 0, m, 0))
     out = pltpu.HBM((supernodes, 2, rows, width), jnp.float32)
     scratch = [
         pltpu.VMEM((2, 2, tile, slots * BLK), jnp.bfloat16),
-        pltpu.VMEM((supernodes, slots * BLK, 4 * width), jnp.bfloat16),
+        pltpu.VMEM(gathered.shape, jnp.bfloat16),
         pltpu.SemaphoreType.DMA((2,)),
         pltpu.SemaphoreType.DMA((supernodes,)),
     ]
     return pl.pallas_call(
-        functools.partial(values_kernel, entries, early_count, sub, tile),
+        functools.partial(values_kernel, tile),
         out_shape=(out, out),
         grid_spec=pltpu.PrefetchScalarGridSpec(
             num_scalar_prefetch=1,
             grid=(supernodes, rows // tile),
-            in_specs=[pl.BlockSpec(memory_space=pl.ANY)] * 5,
+            in_specs=[pl.BlockSpec(memory_space=pl.ANY)] * 2,
             out_specs=(out_spec, out_spec),
             scratch_shapes=scratch,
         ),
@@ -347,7 +331,7 @@
             flops=2 * supernodes * rows * slots * BLK * 4 * width, bytes_accessed=16 * 2**20, transcendentals=0
         ),
         name="values",
-    )(tab, a, *stacks)
+    )(tab, a, gathered)
 
 
 def make_gram(tab, a, stacks, entries, sub, shares):
@@ -368,15 +352,16 @@
         pltpu.SemaphoreType.DMA((supernodes, 2)),
         pltpu.SemaphoreType.DMA((supernodes,)),
         pltpu.SemaphoreType.DMA((supernodes,)),
+        pltpu.SemaphoreType.DMA,
     ]
     return pl.pallas_call(
         functools.partial(gram_kernel, entries, early_count, sub),
-        out_shape=(out, out),
+        out_shape=(out, out, pltpu.HBM((supernodes, slots * BLK, 4 * width), jnp.bfloat16)),
         grid_spec=pltpu.PrefetchScalarGridSpec(
             num_scalar_prefetch=1,
             grid=(supernodes,),
             in_specs=[pl.BlockSpec(memory_space=pl.ANY)] * 5,
-            out_specs=(out_spec, out_spec),
+            out_specs=(out_spec, out_spec, pl.BlockSpec(memory_space=pl.ANY)),
             scratch_shapes=scratch,
         ),
         compiler_params=pltpu.CompilerParams(vmem_limit_bytes=vmem_limit(scratch, [out.shape] * 2)),
@@ -472,10 +457,10 @@
     ]
     stacks = own + [lax.ppermute(x, "col", swap) for x in own]
 
-    mine, theirs = make_gram(tab, inverse_pairs, stacks, entries, sub, n_row)
+    mine, theirs, gathered = make_gram(tab, inverse_pairs, stacks, entries, sub, n_row)
     total = mine + lax.ppermute(theirs, "col", swap)
     total, tab = lax.optimization_barrier((total, tab))
-    mine, theirs = make_values(tab, inverse_pairs, stacks, entries, sub)
+    mine, theirs = make_values(tab, inverse_pairs, gathered)
     share, theirs = scatter_sum(total, n_row, theirs)
     values = mine + lax.ppermute(theirs, "col", swap)
     schur, values = gather_shares(diag_blocks, share, n_row, values)

time: 89.7 us -> 90.2 us (level)
  waiting for transfers between devices: 19.7 us -> 24.3 us
  starting transfers between devices: 34.6 us -> 30.2 us
  other arithmetic: 6.49 us -> 4.34 us
  Pallas kernels: 22.7 us -> 23.9 us
    ppermute x1, waiting for transfers between devices: 0.45 us -> 3.62 us  [gather_shares(): lax.ppermute(jnp.stack(own), 'row', [(i, i ^ 1) for i in range(n_row)])]
    ppermute x1, starting transfers between devices: 1.62 us -> 0.01 us  [local(): values = mine + lax.ppermute(theirs, 'col', swap)]
    pallas_call x1, Pallas kernels: 11.5 us -> 13.1 us  [make_values(): pl.pallas_call(functools.partial(values_kernel, tile), out_shape=(out, ou...]
    ppermute x1, starting transfers between devices: 1.47 us -> 0.07 us  [gather_shares(): lax.ppermute(jnp.stack(own), 'row', [(i, i ^ 1) for i in range(n_row)])]
    ppermute x1, starting transfers between devices: 1.47 us -> 0.07 us  [scatter_sum(): lax.ppermute(sent, 'row', route)]
    ppermute x1, waiting for transfers between devices: 2.86 us -> 4.25 us  [scatter_sum(): lax.ppermute(sent, 'row', route)]
    ppermute x3, starting transfers between devices: 7.07 us -> 8.35 us  [scatter_sum(): came.append(lax.ppermute(sent, 'row', route))]
    ppermute x1, starting transfers between devices: 1.33 us -> 0.07 us  [local(): total = mine + lax.ppermute(theirs, 'col', swap)]
  transfers between devices with their start and end apart: 28 -> 28, of which waited for: 12 -> 12; matrix products, arithmetic and copies ran while one was open for 6% -> 5% of each run, Pallas kernels for 16% -> 17%
where the time goes in v3:
time: 90.2 us; the launch traced here: 88.6 us
  starting transfers between devices  30.2 us (33%)
  waiting for transfers between devices  24.3 us (27%)
  Pallas kernels  23.9 us (26%)
  local copies, waits for them, and re-layouts  4.81 us (5%)
  other arithmetic  4.34 us (5%)
  between operations  1.01 us (1%)
    pallas_call x1, Pallas kernels, make_values(): pl.pallas_call(functools.partial(values_kernel, tile), out_shape=(out, ou...  13.1 us
    ppermute x6, starting transfers between devices, local(): up[k] = lax.ppermute(up[k], 'row', ahead)  12.8 us
    ppermute x3, starting transfers between devices, scatter_sum(): came.append(lax.ppermute(sent, 'row', route))  8.35 us
    pallas_call x1, Pallas kernels, make_gram(): pl.pallas_call(functools.partial(gram_kernel, entries, early_count, sub),...  6.35 us
    ppermute x3, waiting for transfers between devices, gather_shares(): lax.ppermute(share, 'row', [(i, (i + 2 * d) % n_row) for i in range(n_row)])  4.85 us
    unnamed x21, local copies, waits for them, and re-layouts  4.7 us
    ppermute x1, waiting for transfers between devices, scatter_sum(): lax.ppermute(sent, 'row', route)  4.25 us
    ppermute x3, starting transfers between devices, gather_shares(): lax.ppermute(share, 'row', [(i, (i + 2 * d) % n_row) for i in range(n_row)])  3.87 us
  transfers between devices with their start and end apart: 28, of which 12 were waited for; matrix products, arithmetic and copies ran while one was open for 5% of the time, Pallas kernels for 17%

profile of v3, /device:TPU:0, one launch (start us, length us, event | category | flops | bytes accessed | tf_op | source)
XLA Modules:
  0.0 88.6 jit_solution(9737471785983924430)
XLA Ops:
  1.7 3.1 %collective-permute-start = (bf16[2,256,128]{2,1,0:T(8,128)(2,1)S(1)}, bf16[2,256,128]{2,1,0:T(8,128)(2,1)S(1)}, u32[]{:S(2)}, u32[]{:S(2)}) collective-permute-start(bf16[2,256,128]{2,1,0:T(8,128)(2,1)S(1)} %get-tuple-element.42), channel_id=1, source_target_pairs={{0,4},{4,8},{8,12},{12,14},{14,10},{10,6},{6,2},{2,0},{1,5},{5,9},... | collective-permute-start | bytes 393224 | tf_op jit(solution)/shard_map/ppermute | solution.py:445
  4.8 2.0 %collective-permute-start.4 = (bf16[2,256,128]{2,1,0:T(8,128)(2,1)S(1)}, bf16[2,256,128]{2,1,0:T(8,128)(2,1)S(1)}, u32[]{:S(2)}, u32[]{:S(2)}) collective-permute-start(bf16[2,256,128]{2,1,0:T(8,128)(2,1)S(1)} %get-tuple-element.41), channel_id=1, source_target_pairs={{0,4},{4,8},{8,12},{12,14},{14,10},{10,6},{6,2},{2,0},{1,5},{5,9},... | collective-permute-start | bytes 393224 | tf_op jit(solution)/shard_map/ppermute | solution.py:445
  6.8 2.4 %table.1.tab_ref = s32[2,6,16]{2,1,0:T(8,128)} custom-call(s32[2,16]{1,0:T(2,128)} %lists_ref.1, s32[96]{0:T(128)} %order_ref.1), custom_call_target="tpu_custom_call" | custom-call | tf_op jit(solution)/shard_map/table/pallas_call | solution.py:67
  9.2 2.1 %collective-permute-start.2 = (bf16[2,256,128]{2,1,0:T(8,128)(2,1)S(1)}, bf16[2,256,128]{2,1,0:T(8,128)(2,1)S(1)}, u32[]{:S(2)}, u32[]{:S(2)}) collective-permute-start(bf16[2,256,128]{2,1,0:T(8,128)(2,1)S(1)} %collective-permute-done), channel_id=1, source_target_pairs={{0,4},{4,8},{8,12},{12,14},{14,10},{10,6},{6,2},{2,0},{1,5},{5,9},... | collective-permute-start | bytes 393224 | tf_op jit(solution)/shard_map/ppermute | solution.py:445
  11.3 2.0 %collective-permute-start.6 = (bf16[2,256,128]{2,1,0:T(8,128)(2,1)S(1)}, bf16[2,256,128]{2,1,0:T(8,128)(2,1)S(1)}, u32[]{:S(2)}, u32[]{:S(2)}) collective-permute-start(bf16[2,256,128]{2,1,0:T(8,128)(2,1)S(1)} %collective-permute-done.4), channel_id=1, source_target_pairs={{0,4},{4,8},{8,12},{12,14},{14,10},{10,6},{6,2},{2,0},{1,5},{5,9},... | collective-permute-start | bytes 393224 | tf_op jit(solution)/shard_map/ppermute | solution.py:445
  13.4 2.1 %collective-permute-done.2 = bf16[2,256,128]{2,1,0:T(8,128)(2,1)S(1)} collective-permute-done((bf16[2,256,128]{2,1,0:T(8,128)(2,1)S(1)}, bf16[2,256,128]{2,1,0:T(8,128)(2,1)S(1)}, u32[]{:S(2)}, u32[]{:S(2)}) %collective-permute-start.2) | collective-permute-done | bytes 131104 | tf_op jit(solution)/shard_map/ppermute | solution.py:445
  15.5 1.8 %collective-permute-start.8 = (bf16[2,256,128]{2,1,0:T(8,128)(2,1)S(1)}, bf16[2,256,128]{2,1,0:T(8,128)(2,1)S(1)}, u32[]{:S(2)}, u32[]{:S(2)}) collective-permute-start(bf16[2,256,128]{2,1,0:T(8,128)(2,1)S(1)} %collective-permute-done.2), channel_id=1, source_target_pairs={{0,4},{4,8},{8,12},{12,14},{14,10},{10,6},{6,2},{2,0},{1,5},{5,9},... | collective-permute-start | bytes 393224 | tf_op jit(solution)/shard_map/ppermute | solution.py:445
  18.3 1.8 %collective-permute-start.12 = (bf16[2,256,128]{2,1,0:T(8,128)(2,1)S(1)}, bf16[2,256,128]{2,1,0:T(8,128)(2,1)S(1)}, u32[]{:S(2)}, u32[]{:S(2)}) collective-permute-start(bf16[2,256,128]{2,1,0:T(8,128)(2,1)S(1)} %collective-permute-done.6), channel_id=1, source_target_pairs={{0,4},{4,8},{8,12},{12,14},{14,10},{10,6},{6,2},{2,0},{1,5},{5,9},... | collective-permute-start | bytes 393224 | tf_op jit(solution)/shard_map/ppermute | solution.py:445
  23.6 1.8 %collective-permute-start.14 = (bf16[1,256,128]{2,1,0:T(8,128)(2,1)S(1)}, bf16[1,256,128]{2,1,0:T(8,128)(2,1)S(1)}, u32[]{:S(2)}, u32[]{:S(2)}) collective-permute-start(bf16[1,256,128]{2,1,0:T(8,128)(2,1)S(1)} %slice.28), channel_id=1, source_target_pairs={{0,4},{4,8},{8,12},{12,14},{14,10},{10,6},{6,2},{2,0},{1,5},{5,9},... | collective-permute-start | bytes 196616 | tf_op jit(solution)/shard_map/ppermute | solution.py:451
  30.0 2.3 %collective-permute-done.17.sib1 = bf16[2,3,2,256,128]{4,3,2,1,0:T(8,128)(2,1)S(1)} collective-permute-done((bf16[2,3,2,256,128]{4,3,2,1,0:T(8,128)(2,1)S(1)}, bf16[2,3,2,256,128]{4,3,2,1,0:T(8,128)(2,1)S(1)}, u32[]{:S(2)}, u32[]{:S(2)}) %collective-permute-start.17) | collective-permute-done | bytes 786464 | tf_op jit(solution)/shard_map/ppermute | solution.py:458
  32.3 6.3 %gram.1 = (f32[8,2,2,32,128]{4,3,2,1,0:T(8,128)S(1)}, f32[8,2,2,32,128]{4,3,2,1,0:T(8,128)S(1)}, bf16[2,2048,512]{2,1,0:T(8,128)(2,1)}) custom-call(s32[2,6,16]{2,1,0:T(8,128)S(1)} %copy-done.1, bf16[2,1536,6144]{2,1,0:T(8,128)(2,1)} %a_ref.3, bf16[2,5,2,256,128]{4,3,2,1,0:T(8,128)(2,1)S(1)} %pad_maximum_fusion.own0, ...), custom_call_target="tpu_custom_call" | custom-call | flops 1073741824 | bytes 8388608 | tf_op jit(solution)/shard_map/gram/pallas_call | solution.py:357
  38.8 1.8 %collective-permute-done.18 = f32[8,2,2,32,128]{4,3,2,1,0:T(8,128)S(1)} collective-permute-done((f32[8,2,2,32,128]{4,3,2,1,0:T(8,128)S(1)}, f32[8,2,2,32,128]{4,3,2,1,0:T(8,128)S(1)}, u32[]{:S(2)}, u32[]{:S(2)}) %collective-permute-start.18) | collective-permute-done | bytes 524320 | tf_op jit(solution)/shard_map/ppermute | solution.py:461
  40.7 2.2 %collective-permute-start.19 = (f32[2,2,2,32,128]{4,3,2,1,0:T(8,128)S(1)}, f32[2,2,2,32,128]{4,3,2,1,0:T(8,128)S(1)}, u32[]{:S(2)}, u32[]{:S(2)}) collective-permute-start(f32[2,2,2,32,128]{4,3,2,1,0:T(8,128)S(1)} %get-tuple-element.38), channel_id=1, source_target_pairs={{0,4},{2,6},{4,8},{6,10},{8,12},{10,14},{12,0},{14,2},{1,5},{3,7},... | collective-permute-start | bytes 393224 | tf_op jit(solution)/shard_map/ppermute | solution.py:384
  42.9 3.3 %collective-permute-start.20 = (f32[2,2,2,32,128]{4,3,2,1,0:T(8,128)S(1)}, f32[2,2,2,32,128]{4,3,2,1,0:T(8,128)S(1)}, u32[]{:S(2)}, u32[]{:S(2)}) collective-permute-start(f32[2,2,2,32,128]{4,3,2,1,0:T(8,128)S(1)} %get-tuple-element.37), channel_id=1, source_target_pairs={{0,8},{2,10},{4,12},{6,14},{8,0},{10,2},{12,4},{14,6},{1,9},{3,11}... | collective-permute-start | bytes 393224 | tf_op jit(solution)/shard_map/ppermute | solution.py:384
  46.2 2.8 %collective-permute-start.21 = (f32[2,2,2,32,128]{4,3,2,1,0:T(8,128)S(1)}, f32[2,2,2,32,128]{4,3,2,1,0:T(8,128)S(1)}, u32[]{:S(2)}, u32[]{:S(2)}) collective-permute-start(f32[2,2,2,32,128]{4,3,2,1,0:T(8,128)S(1)} %get-tuple-element.36), channel_id=1, source_target_pairs={{0,12},{2,14},{4,0},{6,2},{8,4},{10,6},{12,8},{14,10},{1,13},{3,15... | collective-permute-start | bytes 393224 | tf_op jit(solution)/shard_map/ppermute | solution.py:384
  49.1 2.2 %copy-done = bf16[2,2048,512]{2,1,0:T(8,128)(2,1)S(1)} copy-done((bf16[2,2048,512]{2,1,0:T(8,128)(2,1)S(1)}, bf16[2,2048,512]{2,1,0:T(8,128)(2,1)}, u32[]{:S(2)}) %copy-start) | copy-done | bytes 4194328
  51.3 13.1 %values.1 = (f32[2,2,1536,128]{3,2,1,0:T(8,128)}, f32[2,2,1536,128]{3,2,1,0:T(8,128)}) custom-call(s32[2,6,16]{2,1,0:T(8,128)S(1)} %copy-done.1, bf16[2,1536,6144]{2,1,0:T(8,128)(2,1)} %a_ref.3, bf16[2,2048,512]{2,1,0:T(8,128)(2,1)S(1)} %copy-done), custom_call_target="tpu_custom_call" | custom-call | flops 6442450944 | bytes 16777216 | tf_op jit(solution)/shard_map/values/pallas_call | solution.py:319
  64.5 4.3 %collective-permute-done.22 = f32[2,2,32,128]{3,2,1,0:T(8,128)S(1)} collective-permute-done((f32[2,2,32,128]{3,2,1,0:T(8,128)S(1)}, f32[2,2,32,128]{3,2,1,0:T(8,128)S(1)}, u32[]{:S(2)}, u32[]{:S(2)}) %collective-permute-start.22) | collective-permute-done | bytes 65568 | tf_op jit(solution)/shard_map/ppermute | solution.py:391
  69.5 3.3 %collective-permute-start.25 = (f32[2,2,32,128]{3,2,1,0:T(8,128)S(1)}, f32[2,2,32,128]{3,2,1,0:T(8,128)S(1)}, u32[]{:S(2)}, u32[]{:S(2)}) collective-permute-start(f32[2,2,32,128]{3,2,1,0:T(8,128)S(1)} %bitcast_add_fusion.1.refs_0_), channel_id=1, source_target_pairs={{0,12},{2,14},{4,0},{6,2},{8,4},{10,6},{12,8},{14,10},{1,13},{3,15... | collective-permute-start | bytes 196616 | tf_op jit(solution)/shard_map/ppermute | solution.py:412
  72.7 3.0 %collective-permute-done.23.refs_1_ = f32[2,2,32,128]{3,2,1,0:T(8,128)S(1)} collective-permute-done((f32[2,2,32,128]{3,2,1,0:T(8,128)S(1)}, f32[2,2,32,128]{3,2,1,0:T(8,128)S(1)}, u32[]{:S(2)}, u32[]{:S(2)}) %collective-permute-start.23) | collective-permute-done | bytes 65568 | tf_op jit(solution)/shard_map/ppermute | solution.py:412
  75.7 1.9 %collective-permute-done.24.refs_2_ = f32[2,2,32,128]{3,2,1,0:T(8,128)S(1)} collective-permute-done((f32[2,2,32,128]{3,2,1,0:T(8,128)S(1)}, f32[2,2,32,128]{3,2,1,0:T(8,128)S(1)}, u32[]{:S(2)}, u32[]{:S(2)}) %collective-permute-start.24) | collective-permute-done | bytes 65568 | tf_op jit(solution)/shard_map/ppermute | solution.py:412
  78.3 3.9 %add.80 = f32[2,2,1536,128]{3,2,1,0:T(8,128)} add(f32[2,2,1536,128]{3,2,1,0:T(8,128)} %get-tuple-element.32, f32[2,2,1536,128]{3,2,1,0:T(8,128)S(1)} %collective-permute-done.27) | non-fusion elementwise | flops 786432 | bytes 9437184 | tf_op jit(solution)/shard_map/add | solution.py:465
  82.2 3.6 %collective-permute-done.26.refs_4_ = f32[4,2,2,32,128]{4,3,2,1,0:T(8,128)S(1)} collective-permute-done((f32[4,2,2,32,128]{4,3,2,1,0:T(8,128)S(1)}, f32[4,2,2,32,128]{4,3,2,1,0:T(8,128)S(1)}, u32[]{:S(2)}, u32[]{:S(2)}) %collective-permute-start.26) | collective-permute-done | bytes 262176 | tf_op jit(solution)/shard_map/ppermute | solution.py:413
  86.5 2.1 %place.1 = f32[2,2,256,128]{3,2,1,0:T(8,128)} custom-call(bf16[2,2,256,128]{3,2,1,0:T(8,128)(2,1)} %diag_ref.1, f32[2,2,32,128]{3,2,1,0:T(8,128)} %copy-done.2, f32[2,2,32,128]{3,2,1,0:T(8,128)} %copy-done.4, f32[2,2,32,128]{3,2,1,0:T(8,128)} %copy-done.5, f32[2,2,32,128]{3,2,1,0:T(8,128)} %copy-done.6, f32[4,2,2,32,128]{4,3,2,1,0:T(8,128)} %copy-done.3), custom_call_target="tpu_custom_call" | custom-call | tf_op jit(solution)/shard_map/place/pallas_call | solution.py:416
  (76 shorter events, 12.6 us)
Async XLA Ops:
  1.7 7.5 %collective-permute-start = (bf16[2,256,128]{2,1,0:T(8,128)(2,1)S(1)}, bf16[2,256,128]{2,1,0:T(8,128)(2,1)S(1)}, u32[]{:S(2)}, u32[]{:S(2)}) collective-permute-start(bf16[2,256,128]{2,1,0:T(8,128)(2,1)S(1)} %get-tuple-element.42), channel_id=1, source_target_pairs={{0,4},{4,8},{8,12},{12,14},{14,10},{10,6},{6,2},{2,0},{1,5},{5,9},... | collective-permute-start | bytes 393224 | tf_op jit(solution)/shard_map/ppermute | solution.py:445
  4.7 6.5 %collective-permute-start.1 = (bf16[2,256,128]{2,1,0:T(8,128)(2,1)S(1)}, bf16[2,256,128]{2,1,0:T(8,128)(2,1)S(1)}, u32[]{:S(2)}, u32[]{:S(2)}) collective-permute-start(bf16[2,256,128]{2,1,0:T(8,128)(2,1)S(1)} %get-tuple-element.42), channel_id=1, source_target_pairs={{4,0},{8,4},{12,8},{14,12},{10,14},{6,10},{2,6},{0,2},{5,1},{9,5},... | collective-permute-start | bytes 393224 | tf_op jit(solution)/shard_map/ppermute | solution.py:446
  4.8 6.5 %collective-permute-start.4 = (bf16[2,256,128]{2,1,0:T(8,128)(2,1)S(1)}, bf16[2,256,128]{2,1,0:T(8,128)(2,1)S(1)}, u32[]{:S(2)}, u32[]{:S(2)}) collective-permute-start(bf16[2,256,128]{2,1,0:T(8,128)(2,1)S(1)} %get-tuple-element.41), channel_id=1, source_target_pairs={{0,4},{4,8},{8,12},{12,14},{14,10},{10,6},{6,2},{2,0},{1,5},{5,9},... | collective-permute-start | bytes 393224 | tf_op jit(solution)/shard_map/ppermute | solution.py:445
  6.8 6.5 %collective-permute-start.5 = (bf16[2,256,128]{2,1,0:T(8,128)(2,1)S(1)}, bf16[2,256,128]{2,1,0:T(8,128)(2,1)S(1)}, u32[]{:S(2)}, u32[]{:S(2)}) collective-permute-start(bf16[2,256,128]{2,1,0:T(8,128)(2,1)S(1)} %get-tuple-element.41), channel_id=1, source_target_pairs={{4,0},{8,4},{12,8},{14,12},{10,14},{6,10},{2,6},{0,2},{5,1},{9,5},... | collective-permute-start | bytes 393224 | tf_op jit(solution)/shard_map/ppermute | solution.py:446
  9.2 6.3 %collective-permute-start.2 = (bf16[2,256,128]{2,1,0:T(8,128)(2,1)S(1)}, bf16[2,256,128]{2,1,0:T(8,128)(2,1)S(1)}, u32[]{:S(2)}, u32[]{:S(2)}) collective-permute-start(bf16[2,256,128]{2,1,0:T(8,128)(2,1)S(1)} %collective-permute-done), channel_id=1, source_target_pairs={{0,4},{4,8},{8,12},{12,14},{14,10},{10,6},{6,2},{2,0},{1,5},{5,9},... | collective-permute-start | bytes 393224 | tf_op jit(solution)/shard_map/ppermute | solution.py:445
  11.2 6.1 %collective-permute-start.3 = (bf16[2,256,128]{2,1,0:T(8,128)(2,1)S(1)}, bf16[2,256,128]{2,1,0:T(8,128)(2,1)S(1)}, u32[]{:S(2)}, u32[]{:S(2)}) collective-permute-start(bf16[2,256,128]{2,1,0:T(8,128)(2,1)S(1)} %collective-permute-done.1), channel_id=1, source_target_pairs={{4,0},{8,4},{12,8},{14,12},{10,14},{6,10},{2,6},{0,2},{5,1},{9,5},... | collective-permute-start | bytes 393224 | tf_op jit(solution)/shard_map/ppermute | solution.py:446
  11.3 7.1 %collective-permute-start.6 = (bf16[2,256,128]{2,1,0:T(8,128)(2,1)S(1)}, bf16[2,256,128]{2,1,0:T(8,128)(2,1)S(1)}, u32[]{:S(2)}, u32[]{:S(2)}) collective-permute-start(bf16[2,256,128]{2,1,0:T(8,128)(2,1)S(1)} %collective-permute-done.4), channel_id=1, source_target_pairs={{0,4},{4,8},{8,12},{12,14},{14,10},{10,6},{6,2},{2,0},{1,5},{5,9},... | collective-permute-start | bytes 393224 | tf_op jit(solution)/shard_map/ppermute | solution.py:445
  13.3 6.9 %collective-permute-start.7 = (bf16[2,256,128]{2,1,0:T(8,128)(2,1)S(1)}, bf16[2,256,128]{2,1,0:T(8,128)(2,1)S(1)}, u32[]{:S(2)}, u32[]{:S(2)}) collective-permute-start(bf16[2,256,128]{2,1,0:T(8,128)(2,1)S(1)} %collective-permute-done.5), channel_id=1, source_target_pairs={{4,0},{8,4},{12,8},{14,12},{10,14},{6,10},{2,6},{0,2},{5,1},{9,5},... | collective-permute-start | bytes 393224 | tf_op jit(solution)/shard_map/ppermute | solution.py:446
  15.5 5.7 %collective-permute-start.8 = (bf16[2,256,128]{2,1,0:T(8,128)(2,1)S(1)}, bf16[2,256,128]{2,1,0:T(8,128)(2,1)S(1)}, u32[]{:S(2)}, u32[]{:S(2)}) collective-permute-start(bf16[2,256,128]{2,1,0:T(8,128)(2,1)S(1)} %collective-permute-done.2), channel_id=1, source_target_pairs={{0,4},{4,8},{8,12},{12,14},{14,10},{10,6},{6,2},{2,0},{1,5},{5,9},... | collective-permute-start | bytes 393224 | tf_op jit(solution)/shard_map/ppermute | solution.py:445
  17.3 5.7 %collective-permute-start.9 = (bf16[2,256,128]{2,1,0:T(8,128)(2,1)S(1)}, bf16[2,256,128]{2,1,0:T(8,128)(2,1)S(1)}, u32[]{:S(2)}, u32[]{:S(2)}) collective-permute-start(bf16[2,256,128]{2,1,0:T(8,128)(2,1)S(1)} %collective-permute-done.3), channel_id=1, source_target_pairs={{4,0},{8,4},{12,8},{14,12},{10,14},{6,10},{2,6},{0,2},{5,1},{9,5},... | collective-permute-start | bytes 393224 | tf_op jit(solution)/shard_map/ppermute | solution.py:446
  18.3 5.2 %collective-permute-start.12 = (bf16[2,256,128]{2,1,0:T(8,128)(2,1)S(1)}, bf16[2,256,128]{2,1,0:T(8,128)(2,1)S(1)}, u32[]{:S(2)}, u32[]{:S(2)}) collective-permute-start(bf16[2,256,128]{2,1,0:T(8,128)(2,1)S(1)} %collective-permute-done.6), channel_id=1, source_target_pairs={{0,4},{4,8},{8,12},{12,14},{14,10},{10,6},{6,2},{2,0},{1,5},{5,9},... | collective-permute-start | bytes 393224 | tf_op jit(solution)/shard_map/ppermute | solution.py:445
  20.2 5.2 %collective-permute-start.13 = (bf16[2,256,128]{2,1,0:T(8,128)(2,1)S(1)}, bf16[2,256,128]{2,1,0:T(8,128)(2,1)S(1)}, u32[]{:S(2)}, u32[]{:S(2)}) collective-permute-start(bf16[2,256,128]{2,1,0:T(8,128)(2,1)S(1)} %collective-permute-done.7), channel_id=1, source_target_pairs={{4,0},{8,4},{12,8},{14,12},{10,14},{6,10},{2,6},{0,2},{5,1},{9,5},... | collective-permute-start | bytes 393224 | tf_op jit(solution)/shard_map/ppermute | solution.py:446
  21.3 4.5 %collective-permute-start.10 = (bf16[1,256,128]{2,1,0:T(8,128)(2,1)S(1)}, bf16[1,256,128]{2,1,0:T(8,128)(2,1)S(1)}, u32[]{:S(2)}, u32[]{:S(2)}) collective-permute-start(bf16[1,256,128]{2,1,0:T(8,128)(2,1)S(1)} %slice.26), channel_id=1, source_target_pairs={{0,4},{4,8},{8,12},{12,14},{14,10},{10,6},{6,2},{2,0},{1,5},{5,9},... | collective-permute-start | bytes 196616 | tf_op jit(solution)/shard_map/ppermute | solution.py:451
  23.5 8.8 %collective-permute-start.16 = (bf16[2,5,2,256,128]{4,3,2,1,0:T(8,128)(2,1)S(1)}, bf16[2,5,2,256,128]{4,3,2,1,0:T(8,128)(2,1)S(1)}, u32[]{:S(2)}, u32[]{:S(2)}) collective-permute-start(bf16[2,5,2,256,128]{4,3,2,1,0:T(8,128)(2,1)S(1)} %pad_maximum_fusion.own0), channel_id=1, source_target_pairs={{0,1},{1,0},{2,3},{3,2},{4,5},{5,4},{6,7},{7,6},{8,9},{9,8},{10,11... | collective-permute-start | bytes 3932168 | tf_op jit(solution)/shard_map/ppermute | solution.py:458
  23.6 4.7 %collective-permute-start.14 = (bf16[1,256,128]{2,1,0:T(8,128)(2,1)S(1)}, bf16[1,256,128]{2,1,0:T(8,128)(2,1)S(1)}, u32[]{:S(2)}, u32[]{:S(2)}) collective-permute-start(bf16[1,256,128]{2,1,0:T(8,128)(2,1)S(1)} %slice.28), channel_id=1, source_target_pairs={{0,4},{4,8},{8,12},{12,14},{14,10},{10,6},{6,2},{2,0},{1,5},{5,9},... | collective-permute-start | bytes 196616 | tf_op jit(solution)/shard_map/ppermute | solution.py:451
  40.7 23.6 %collective-permute-start.19 = (f32[2,2,2,32,128]{4,3,2,1,0:T(8,128)S(1)}, f32[2,2,2,32,128]{4,3,2,1,0:T(8,128)S(1)}, u32[]{:S(2)}, u32[]{:S(2)}) collective-permute-start(f32[2,2,2,32,128]{4,3,2,1,0:T(8,128)S(1)} %get-tuple-element.38), channel_id=1, source_target_pairs={{0,4},{2,6},{4,8},{6,10},{8,12},{10,14},{12,0},{14,2},{1,5},{3,7},... | collective-permute-start | bytes 393224 | tf_op jit(solution)/shard_map/ppermute | solution.py:384
  42.9 21.5 %collective-permute-start.20 = (f32[2,2,2,32,128]{4,3,2,1,0:T(8,128)S(1)}, f32[2,2,2,32,128]{4,3,2,1,0:T(8,128)S(1)}, u32[]{:S(2)}, u32[]{:S(2)}) collective-permute-start(f32[2,2,2,32,128]{4,3,2,1,0:T(8,128)S(1)} %get-tuple-element.37), channel_id=1, source_target_pairs={{0,8},{2,10},{4,12},{6,14},{8,0},{10,2},{12,4},{14,6},{1,9},{3,11}... | collective-permute-start | bytes 393224 | tf_op jit(solution)/shard_map/ppermute | solution.py:384
  46.2 18.2 %collective-permute-start.21 = (f32[2,2,2,32,128]{4,3,2,1,0:T(8,128)S(1)}, f32[2,2,2,32,128]{4,3,2,1,0:T(8,128)S(1)}, u32[]{:S(2)}, u32[]{:S(2)}) collective-permute-start(f32[2,2,2,32,128]{4,3,2,1,0:T(8,128)S(1)} %get-tuple-element.36), channel_id=1, source_target_pairs={{0,12},{2,14},{4,0},{6,2},{8,4},{10,6},{12,8},{14,10},{1,13},{3,15... | collective-permute-start | bytes 393224 | tf_op jit(solution)/shard_map/ppermute | solution.py:384
  64.5 4.3 %collective-permute-start.22 = (f32[2,2,32,128]{3,2,1,0:T(8,128)S(1)}, f32[2,2,32,128]{3,2,1,0:T(8,128)S(1)}, u32[]{:S(2)}, u32[]{:S(2)}) collective-permute-start(f32[2,2,32,128]{3,2,1,0:T(8,128)S(1)} %dynamic-slice_bitcast_fusion.3), channel_id=1, source_target_pairs={{0,2},{2,0},{4,6},{6,4},{8,10},{10,8},{12,14},{14,12},{1,3},{3,1},... | collective-permute-start | bytes 196616 | tf_op jit(solution)/shard_map/ppermute | solution.py:391
  68.8 9.5 %collective-permute-start.27 = (f32[2,2,1536,128]{3,2,1,0:T(8,128)}, f32[2,2,1536,128]{3,2,1,0:T(8,128)S(1)}, u32[]{:S(2)}, u32[]{:S(2)}) collective-permute-start(f32[2,2,1536,128]{3,2,1,0:T(8,128)} %get-tuple-element.33), channel_id=1, source_target_pairs={{0,1},{1,0},{2,3},{3,2},{4,5},{5,4},{6,7},{7,6},{8,9},{9,8},{10,11... | collective-permute-start | bytes 9437192 | tf_op jit(solution)/shard_map/ppermute | solution.py:465
  68.8 6.8 %collective-permute-start.23 = (f32[2,2,32,128]{3,2,1,0:T(8,128)S(1)}, f32[2,2,32,128]{3,2,1,0:T(8,128)S(1)}, u32[]{:S(2)}, u32[]{:S(2)}) collective-permute-start(f32[2,2,32,128]{3,2,1,0:T(8,128)S(1)} %bitcast_add_fusion.1.refs_0_), channel_id=1, source_target_pairs={{0,4},{2,6},{4,8},{6,10},{8,12},{10,14},{12,0},{14,2},{1,5},{3,7},... | collective-permute-start | bytes 196616 | tf_op jit(solution)/shard_map/ppermute | solution.py:412
  68.9 8.7 %collective-permute-start.24 = (f32[2,2,32,128]{3,2,1,0:T(8,128)S(1)}, f32[2,2,32,128]{3,2,1,0:T(8,128)S(1)}, u32[]{:S(2)}, u32[]{:S(2)}) collective-permute-start(f32[2,2,32,128]{3,2,1,0:T(8,128)S(1)} %bitcast_add_fusion.1.refs_0_), channel_id=1, source_target_pairs={{0,8},{2,10},{4,12},{6,14},{8,0},{10,2},{12,4},{14,6},{1,9},{3,11}... | collective-permute-start | bytes 196616 | tf_op jit(solution)/shard_map/ppermute | solution.py:412
  69.5 8.1 %collective-permute-start.25 = (f32[2,2,32,128]{3,2,1,0:T(8,128)S(1)}, f32[2,2,32,128]{3,2,1,0:T(8,128)S(1)}, u32[]{:S(2)}, u32[]{:S(2)}) collective-permute-start(f32[2,2,32,128]{3,2,1,0:T(8,128)S(1)} %bitcast_add_fusion.1.refs_0_), channel_id=1, source_target_pairs={{0,12},{2,14},{4,0},{6,2},{8,4},{10,6},{12,8},{14,10},{1,13},{3,15... | collective-permute-start | bytes 196616 | tf_op jit(solution)/shard_map/ppermute | solution.py:412
  78.2 7.6 %collective-permute-start.26 = (f32[4,2,2,32,128]{4,3,2,1,0:T(8,128)S(1)}, f32[4,2,2,32,128]{4,3,2,1,0:T(8,128)S(1)}, u32[]{:S(2)}, u32[]{:S(2)}) collective-permute-start(f32[4,2,2,32,128]{4,3,2,1,0:T(8,128)S(1)} %pad_maximum_fusion.2), channel_id=1, source_target_pairs={{0,2},{2,0},{4,6},{6,4},{8,10},{10,8},{12,14},{14,12},{1,3},{3,1},... | collective-permute-start | bytes 786440 | tf_op jit(solution)/shard_map/ppermute | solution.py:413
  (11 other events, 45.9 us)

commit v4 on v3

--- a/solution.py
+++ b/solution.py
@@ -326,7 +326,7 @@
             out_specs=(out_spec, out_spec),
             scratch_shapes=scratch,
         ),
-        compiler_params=pltpu.CompilerParams(vmem_limit_bytes=vmem_limit(scratch, [(2, tile, width)] * 2)),
+        compiler_params=pltpu.CompilerParams(vmem_limit_bytes=60 * 2**20),
         cost_estimate=pl.CostEstimate(
             flops=2 * supernodes * rows * slots * BLK * 4 * width, bytes_accessed=16 * 2**20, transcendentals=0
         ),
@@ -418,6 +418,7 @@
         out_shape=jax.ShapeDtypeStruct(diag_blocks.shape, jnp.float32),
         in_specs=[vmem] * (half + 2),
         out_specs=vmem,
+        compiler_params=pltpu.CompilerParams(vmem_limit_bytes=6 * 2**20),
         name="place",
     )(diag_blocks, *own, other)
     return schur, beside

time: 90.2 us -> 86.6 us (0.960); the launches traced: 88.6 us -> 86.3 us
  starting transfers between devices: 30.2 us -> 34.7 us
  local copies, waits for them, and re-layouts: 4.81 us -> 1.28 us
  Pallas kernels: 23.9 us -> 22.2 us
  waiting for transfers between devices: 24.3 us -> 22.8 us
    unnamed x21 -> x11, local copies, waits for them, and re-layouts: 4.7 us -> 1.17 us
    ppermute x1, starting transfers between devices: 0.01 us -> 2.98 us  [local(): values = mine + lax.ppermute(theirs, 'col', swap)]
    ppermute x1, starting transfers between devices: 0.07 us -> 2.52 us  [local(): total = mine + lax.ppermute(theirs, 'col', swap)]
    pallas_call x1, Pallas kernels: 13.1 us -> 11.3 us  [make_values(): pl.pallas_call(functools.partial(values_kernel, tile), out_shape=(out, ou...]
    pallas_call x1, Pallas kernels: 6.35 us -> 7.64 us  [make_gram(): pl.pallas_call(functools.partial(gram_kernel, entries, early_count, sub),...]
    pallas_call x1, Pallas kernels: 2.05 us -> 0.88 us  [gather_shares(): pl.pallas_call(functools.partial(place_kernel, n_row), out_shape=jax.Shap...]
    ppermute x3, starting transfers between devices: 8.35 us -> 7.18 us  [scatter_sum(): came.append(lax.ppermute(sent, 'row', route))]
    ppermute x1, waiting for transfers between devices: 3.62 us -> 2.5 us  [gather_shares(): lax.ppermute(jnp.stack(own), 'row', [(i, i ^ 1) for i in range(n_row)])]
  transfers between devices with their start and end apart: 28 -> 28, of which waited for: 12 -> 12; matrix products, arithmetic and copies ran while one was open for 5% -> 5% of each run, Pallas kernels for 17% -> 16%
where the time goes in v4:
time: 86.6 us; the launch traced here: 86.3 us
  starting transfers between devices  34.7 us (40%)
  waiting for transfers between devices  22.8 us (26%)
  Pallas kernels  22.2 us (26%)
  other arithmetic  4.38 us (5%)
  local copies, waits for them, and re-layouts  1.28 us (1%)
  between operations  0.89 us (1%)
    ppermute x6, starting transfers between devices, local(): up[k] = lax.ppermute(up[k], 'row', ahead)  12.8 us
    pallas_call x1, Pallas kernels, make_values(): pl.pallas_call(functools.partial(values_kernel, tile), out_shape=(out, ou...  11.3 us
    pallas_call x1, Pallas kernels, make_gram(): pl.pallas_call(functools.partial(gram_kernel, entries, early_count, sub),...  7.64 us
    ppermute x3, starting transfers between devices, scatter_sum(): came.append(lax.ppermute(sent, 'row', route))  7.18 us
    ppermute x3, waiting for transfers between devices, gather_shares(): lax.ppermute(share, 'row', [(i, (i + 2 * d) % n_row) for i in range(n_row)])  4.68 us
    ppermute x1, waiting for transfers between devices, scatter_sum(): lax.ppermute(sent, 'row', route)  4.25 us
    add x1, other arithmetic, local(): values = mine + lax.ppermute(theirs, 'col', swap)  3.9 us
    ppermute x3, starting transfers between devices, gather_shares(): lax.ppermute(share, 'row', [(i, (i + 2 * d) % n_row) for i in range(n_row)])  3.87 us
  transfers between devices with their start and end apart: 28, of which 12 were waited for; matrix products, arithmetic and copies ran while one was open for 5% of the time, Pallas kernels for 16%

profile of v4, /device:TPU:0, one launch (start us, length us, event | category | flops | bytes accessed | tf_op | source)
XLA Modules:
  0.0 86.3 jit_solution(5703571698200217895)
XLA Ops:
  1.7 3.1 %collective-permute-start = (bf16[2,256,128]{2,1,0:T(8,128)(2,1)S(1)}, bf16[2,256,128]{2,1,0:T(8,128)(2,1)S(1)}, u32[]{:S(2)}, u32[]{:S(2)}) collective-permute-start(bf16[2,256,128]{2,1,0:T(8,128)(2,1)S(1)} %get-tuple-element.42), channel_id=1, source_target_pairs={{0,4},{4,8},{8,12},{12,14},{14,10},{10,6},{6,2},{2,0},{1,5},{5,9},... | collective-permute-start | bytes 393224 | tf_op jit(solution)/shard_map/ppermute | solution.py:446
  4.8 2.0 %collective-permute-start.4 = (bf16[2,256,128]{2,1,0:T(8,128)(2,1)S(1)}, bf16[2,256,128]{2,1,0:T(8,128)(2,1)S(1)}, u32[]{:S(2)}, u32[]{:S(2)}) collective-permute-start(bf16[2,256,128]{2,1,0:T(8,128)(2,1)S(1)} %get-tuple-element.41), channel_id=1, source_target_pairs={{0,4},{4,8},{8,12},{12,14},{14,10},{10,6},{6,2},{2,0},{1,5},{5,9},... | collective-permute-start | bytes 393224 | tf_op jit(solution)/shard_map/ppermute | solution.py:446
  6.8 2.4 %table.1.tab_ref = s32[2,6,16]{2,1,0:T(8,128)} custom-call(s32[2,16]{1,0:T(2,128)} %lists_ref.1, s32[96]{0:T(128)} %order_ref.1), custom_call_target="tpu_custom_call" | custom-call | tf_op jit(solution)/shard_map/table/pallas_call | solution.py:67
  9.2 2.1 %collective-permute-start.2 = (bf16[2,256,128]{2,1,0:T(8,128)(2,1)S(1)}, bf16[2,256,128]{2,1,0:T(8,128)(2,1)S(1)}, u32[]{:S(2)}, u32[]{:S(2)}) collective-permute-start(bf16[2,256,128]{2,1,0:T(8,128)(2,1)S(1)} %collective-permute-done), channel_id=1, source_target_pairs={{0,4},{4,8},{8,12},{12,14},{14,10},{10,6},{6,2},{2,0},{1,5},{5,9},... | collective-permute-start | bytes 393224 | tf_op jit(solution)/shard_map/ppermute | solution.py:446
  11.3 2.0 %collective-permute-start.6 = (bf16[2,256,128]{2,1,0:T(8,128)(2,1)S(1)}, bf16[2,256,128]{2,1,0:T(8,128)(2,1)S(1)}, u32[]{:S(2)}, u32[]{:S(2)}) collective-permute-start(bf16[2,256,128]{2,1,0:T(8,128)(2,1)S(1)} %collective-permute-done.4), channel_id=1, source_target_pairs={{0,4},{4,8},{8,12},{12,14},{14,10},{10,6},{6,2},{2,0},{1,5},{5,9},... | collective-permute-start | bytes 393224 | tf_op jit(solution)/shard_map/ppermute | solution.py:446
  13.4 2.1 %collective-permute-done.2 = bf16[2,256,128]{2,1,0:T(8,128)(2,1)S(1)} collective-permute-done((bf16[2,256,128]{2,1,0:T(8,128)(2,1)S(1)}, bf16[2,256,128]{2,1,0:T(8,128)(2,1)S(1)}, u32[]{:S(2)}, u32[]{:S(2)}) %collective-permute-start.2) | collective-permute-done | bytes 131104 | tf_op jit(solution)/shard_map/ppermute | solution.py:446
  15.5 1.8 %collective-permute-start.8 = (bf16[2,256,128]{2,1,0:T(8,128)(2,1)S(1)}, bf16[2,256,128]{2,1,0:T(8,128)(2,1)S(1)}, u32[]{:S(2)}, u32[]{:S(2)}) collective-permute-start(bf16[2,256,128]{2,1,0:T(8,128)(2,1)S(1)} %collective-permute-done.2), channel_id=1, source_target_pairs={{0,4},{4,8},{8,12},{12,14},{14,10},{10,6},{6,2},{2,0},{1,5},{5,9},... | collective-permute-start | bytes 393224 | tf_op jit(solution)/shard_map/ppermute | solution.py:446
  18.3 1.8 %collective-permute-start.12 = (bf16[2,256,128]{2,1,0:T(8,128)(2,1)S(1)}, bf16[2,256,128]{2,1,0:T(8,128)(2,1)S(1)}, u32[]{:S(2)}, u32[]{:S(2)}) collective-permute-start(bf16[2,256,128]{2,1,0:T(8,128)(2,1)S(1)} %collective-permute-done.6), channel_id=1, source_target_pairs={{0,4},{4,8},{8,12},{12,14},{14,10},{10,6},{6,2},{2,0},{1,5},{5,9},... | collective-permute-start | bytes 393224 | tf_op jit(solution)/shard_map/ppermute | solution.py:446
  21.3 1.7 %collective-permute-start.10 = (bf16[1,256,128]{2,1,0:T(8,128)(2,1)S(1)}, bf16[1,256,128]{2,1,0:T(8,128)(2,1)S(1)}, u32[]{:S(2)}, u32[]{:S(2)}) collective-permute-start(bf16[1,256,128]{2,1,0:T(8,128)(2,1)S(1)} %slice.26), channel_id=1, source_target_pairs={{0,4},{4,8},{8,12},{12,14},{14,10},{10,6},{6,2},{2,0},{1,5},{5,9},... | collective-permute-start | bytes 196616 | tf_op jit(solution)/shard_map/ppermute | solution.py:452
  23.6 1.8 %collective-permute-start.14 = (bf16[1,256,128]{2,1,0:T(8,128)(2,1)S(1)}, bf16[1,256,128]{2,1,0:T(8,128)(2,1)S(1)}, u32[]{:S(2)}, u32[]{:S(2)}) collective-permute-start(bf16[1,256,128]{2,1,0:T(8,128)(2,1)S(1)} %slice.28), channel_id=1, source_target_pairs={{0,4},{4,8},{8,12},{12,14},{14,10},{10,6},{6,2},{2,0},{1,5},{5,9},... | collective-permute-start | bytes 196616 | tf_op jit(solution)/shard_map/ppermute | solution.py:452
  25.7 1.6 %collective-permute-done.11 = bf16[1,256,128]{2,1,0:T(8,128)(2,1)S(1)} collective-permute-done((bf16[1,256,128]{2,1,0:T(8,128)(2,1)S(1)}, bf16[1,256,128]{2,1,0:T(8,128)(2,1)S(1)}, u32[]{:S(2)}, u32[]{:S(2)}) %collective-permute-start.11) | collective-permute-done | bytes 65568 | tf_op jit(solution)/shard_map/ppermute | solution.py:452
  30.0 2.3 %collective-permute-done.17.sib1 = bf16[2,3,2,256,128]{4,3,2,1,0:T(8,128)(2,1)S(1)} collective-permute-done((bf16[2,3,2,256,128]{4,3,2,1,0:T(8,128)(2,1)S(1)}, bf16[2,3,2,256,128]{4,3,2,1,0:T(8,128)(2,1)S(1)}, u32[]{:S(2)}, u32[]{:S(2)}) %collective-permute-start.17) | collective-permute-done | bytes 786464 | tf_op jit(solution)/shard_map/ppermute | solution.py:459
  32.3 7.6 %gram.1 = (f32[8,2,2,32,128]{4,3,2,1,0:T(8,128)S(1)}, f32[8,2,2,32,128]{4,3,2,1,0:T(8,128)S(1)}, bf16[2,2048,512]{2,1,0:T(8,128)(2,1)}) custom-call(s32[2,6,16]{2,1,0:T(8,128)S(1)} %copy-done.1, bf16[2,1536,6144]{2,1,0:T(8,128)(2,1)} %a_ref.3, bf16[2,5,2,256,128]{4,3,2,1,0:T(8,128)(2,1)S(1)} %pad_maximum_fusion.own0, ...), custom_call_target="tpu_custom_call" | custom-call | flops 1073741824 | bytes 8388608 | tf_op jit(solution)/shard_map/gram/pallas_call | solution.py:357
  39.9 2.5 %collective-permute-start.18 = (f32[8,2,2,32,128]{4,3,2,1,0:T(8,128)S(1)}, f32[8,2,2,32,128]{4,3,2,1,0:T(8,128)S(1)}, u32[]{:S(2)}, u32[]{:S(2)}) collective-permute-start(f32[8,2,2,32,128]{4,3,2,1,0:T(8,128)S(1)} %get-tuple-element.22), channel_id=1, source_target_pairs={{0,1},{1,0},{2,3},{3,2},{4,5},{5,4},{6,7},{7,6},{8,9},{9,8},{10,11... | collective-permute-start | bytes 1572872 | tf_op jit(solution)/shard_map/ppermute | solution.py:462
  44.2 4.3 %collective-permute-start.20 = (f32[2,2,2,32,128]{4,3,2,1,0:T(8,128)S(1)}, f32[2,2,2,32,128]{4,3,2,1,0:T(8,128)S(1)}, u32[]{:S(2)}, u32[]{:S(2)}) collective-permute-start(f32[2,2,2,32,128]{4,3,2,1,0:T(8,128)S(1)} %get-tuple-element.37), channel_id=1, source_target_pairs={{0,8},{2,10},{4,12},{6,14},{8,0},{10,2},{12,4},{14,6},{1,9},{3,11}... | collective-permute-start | bytes 393224 | tf_op jit(solution)/shard_map/ppermute | solution.py:384
  48.5 2.8 %collective-permute-start.21 = (f32[2,2,2,32,128]{4,3,2,1,0:T(8,128)S(1)}, f32[2,2,2,32,128]{4,3,2,1,0:T(8,128)S(1)}, u32[]{:S(2)}, u32[]{:S(2)}) collective-permute-start(f32[2,2,2,32,128]{4,3,2,1,0:T(8,128)S(1)} %get-tuple-element.36), channel_id=1, source_target_pairs={{0,12},{2,14},{4,0},{6,2},{8,4},{10,6},{12,8},{14,10},{1,13},{3,15... | collective-permute-start | bytes 393224 | tf_op jit(solution)/shard_map/ppermute | solution.py:384
  51.3 11.3 %values.1 = (f32[2,2,1536,128]{3,2,1,0:T(8,128)}, f32[2,2,1536,128]{3,2,1,0:T(8,128)}) custom-call(s32[2,6,16]{2,1,0:T(8,128)} %table.1.tab_ref, bf16[2,1536,6144]{2,1,0:T(8,128)(2,1)} %a_ref.3, bf16[2,2048,512]{2,1,0:T(8,128)(2,1)} %get-tuple-element.25.rows_ref), custom_call_target="tpu_custom_call" | custom-call | flops 6442450944 | bytes 16777216 | tf_op jit(solution)/shard_map/values/pallas_call | solution.py:319
  62.8 4.3 %collective-permute-done.22 = f32[2,2,32,128]{3,2,1,0:T(8,128)S(1)} collective-permute-done((f32[2,2,32,128]{3,2,1,0:T(8,128)S(1)}, f32[2,2,32,128]{3,2,1,0:T(8,128)S(1)}, u32[]{:S(2)}, u32[]{:S(2)}) %collective-permute-start.22) | collective-permute-done | bytes 65568 | tf_op jit(solution)/shard_map/ppermute | solution.py:391
  67.1 3.0 %collective-permute-start.27 = (f32[2,2,1536,128]{3,2,1,0:T(8,128)}, f32[2,2,1536,128]{3,2,1,0:T(8,128)S(1)}, u32[]{:S(2)}, u32[]{:S(2)}) collective-permute-start(f32[2,2,1536,128]{3,2,1,0:T(8,128)} %get-tuple-element.33), channel_id=1, source_target_pairs={{0,1},{1,0},{2,3},{3,2},{4,5},{5,4},{6,7},{7,6},{8,9},{9,8},{10,11... | collective-permute-start | bytes 9437192 | tf_op jit(solution)/shard_map/ppermute | solution.py:466
  70.9 3.0 %collective-permute-start.25 = (f32[2,2,32,128]{3,2,1,0:T(8,128)S(1)}, f32[2,2,32,128]{3,2,1,0:T(8,128)S(1)}, u32[]{:S(2)}, u32[]{:S(2)}) collective-permute-start(f32[2,2,32,128]{3,2,1,0:T(8,128)S(1)} %bitcast_add_fusion.1.refs_0_), channel_id=1, source_target_pairs={{0,12},{2,14},{4,0},{6,2},{8,4},{10,6},{12,8},{14,10},{1,13},{3,15... | collective-permute-start | bytes 196616 | tf_op jit(solution)/shard_map/ppermute | solution.py:412
  73.9 3.0 %collective-permute-done.23.refs_1_ = f32[2,2,32,128]{3,2,1,0:T(8,128)S(1)} collective-permute-done((f32[2,2,32,128]{3,2,1,0:T(8,128)S(1)}, f32[2,2,32,128]{3,2,1,0:T(8,128)S(1)}, u32[]{:S(2)}, u32[]{:S(2)}) %collective-permute-start.23) | collective-permute-done | bytes 65568 | tf_op jit(solution)/shard_map/ppermute | solution.py:412
  76.9 1.7 %collective-permute-done.24.refs_2_ = f32[2,2,32,128]{3,2,1,0:T(8,128)S(1)} collective-permute-done((f32[2,2,32,128]{3,2,1,0:T(8,128)S(1)}, f32[2,2,32,128]{3,2,1,0:T(8,128)S(1)}, u32[]{:S(2)}, u32[]{:S(2)}) %collective-permute-start.24) | collective-permute-done | bytes 65568 | tf_op jit(solution)/shard_map/ppermute | solution.py:412
  79.0 3.9 %add.80 = f32[2,2,1536,128]{3,2,1,0:T(8,128)} add(f32[2,2,1536,128]{3,2,1,0:T(8,128)} %get-tuple-element.32, f32[2,2,1536,128]{3,2,1,0:T(8,128)S(1)} %collective-permute-done.27) | non-fusion elementwise | flops 786432 | bytes 9437184 | tf_op jit(solution)/shard_map/add | solution.py:466
  82.9 2.5 %collective-permute-done.26.refs_4_ = f32[4,2,2,32,128]{4,3,2,1,0:T(8,128)S(1)} collective-permute-done((f32[4,2,2,32,128]{4,3,2,1,0:T(8,128)S(1)}, f32[4,2,2,32,128]{4,3,2,1,0:T(8,128)S(1)}, u32[]{:S(2)}, u32[]{:S(2)}) %collective-permute-start.26) | collective-permute-done | bytes 262176 | tf_op jit(solution)/shard_map/ppermute | solution.py:413
  (66 shorter events, 10.8 us)
Async XLA Ops:
  1.7 7.5 %collective-permute-start = (bf16[2,256,128]{2,1,0:T(8,128)(2,1)S(1)}, bf16[2,256,128]{2,1,0:T(8,128)(2,1)S(1)}, u32[]{:S(2)}, u32[]{:S(2)}) collective-permute-start(bf16[2,256,128]{2,1,0:T(8,128)(2,1)S(1)} %get-tuple-element.42), channel_id=1, source_target_pairs={{0,4},{4,8},{8,12},{12,14},{14,10},{10,6},{6,2},{2,0},{1,5},{5,9},... | collective-permute-start | bytes 393224 | tf_op jit(solution)/shard_map/ppermute | solution.py:446
  4.7 6.5 %collective-permute-start.1 = (bf16[2,256,128]{2,1,0:T(8,128)(2,1)S(1)}, bf16[2,256,128]{2,1,0:T(8,128)(2,1)S(1)}, u32[]{:S(2)}, u32[]{:S(2)}) collective-permute-start(bf16[2,256,128]{2,1,0:T(8,128)(2,1)S(1)} %get-tuple-element.42), channel_id=1, source_target_pairs={{4,0},{8,4},{12,8},{14,12},{10,14},{6,10},{2,6},{0,2},{5,1},{9,5},... | collective-permute-start | bytes 393224 | tf_op jit(solution)/shard_map/ppermute | solution.py:447
  4.8 6.5 %collective-permute-start.4 = (bf16[2,256,128]{2,1,0:T(8,128)(2,1)S(1)}, bf16[2,256,128]{2,1,0:T(8,128)(2,1)S(1)}, u32[]{:S(2)}, u32[]{:S(2)}) collective-permute-start(bf16[2,256,128]{2,1,0:T(8,128)(2,1)S(1)} %get-tuple-element.41), channel_id=1, source_target_pairs={{0,4},{4,8},{8,12},{12,14},{14,10},{10,6},{6,2},{2,0},{1,5},{5,9},... | collective-permute-start | bytes 393224 | tf_op jit(solution)/shard_map/ppermute | solution.py:446
  6.8 6.5 %collective-permute-start.5 = (bf16[2,256,128]{2,1,0:T(8,128)(2,1)S(1)}, bf16[2,256,128]{2,1,0:T(8,128)(2,1)S(1)}, u32[]{:S(2)}, u32[]{:S(2)}) collective-permute-start(bf16[2,256,128]{2,1,0:T(8,128)(2,1)S(1)} %get-tuple-element.41), channel_id=1, source_target_pairs={{4,0},{8,4},{12,8},{14,12},{10,14},{6,10},{2,6},{0,2},{5,1},{9,5},... | collective-permute-start | bytes 393224 | tf_op jit(solution)/shard_map/ppermute | solution.py:447
  9.2 6.3 %collective-permute-start.2 = (bf16[2,256,128]{2,1,0:T(8,128)(2,1)S(1)}, bf16[2,256,128]{2,1,0:T(8,128)(2,1)S(1)}, u32[]{:S(2)}, u32[]{:S(2)}) collective-permute-start(bf16[2,256,128]{2,1,0:T(8,128)(2,1)S(1)} %collective-permute-done), channel_id=1, source_target_pairs={{0,4},{4,8},{8,12},{12,14},{14,10},{10,6},{6,2},{2,0},{1,5},{5,9},... | collective-permute-start | bytes 393224 | tf_op jit(solution)/shard_map/ppermute | solution.py:446
  11.2 6.1 %collective-permute-start.3 = (bf16[2,256,128]{2,1,0:T(8,128)(2,1)S(1)}, bf16[2,256,128]{2,1,0:T(8,128)(2,1)S(1)}, u32[]{:S(2)}, u32[]{:S(2)}) collective-permute-start(bf16[2,256,128]{2,1,0:T(8,128)(2,1)S(1)} %collective-permute-done.1), channel_id=1, source_target_pairs={{4,0},{8,4},{12,8},{14,12},{10,14},{6,10},{2,6},{0,2},{5,1},{9,5},... | collective-permute-start | bytes 393224 | tf_op jit(solution)/shard_map/ppermute | solution.py:447
  11.3 7.1 %collective-permute-start.6 = (bf16[2,256,128]{2,1,0:T(8,128)(2,1)S(1)}, bf16[2,256,128]{2,1,0:T(8,128)(2,1)S(1)}, u32[]{:S(2)}, u32[]{:S(2)}) collective-permute-start(bf16[2,256,128]{2,1,0:T(8,128)(2,1)S(1)} %collective-permute-done.4), channel_id=1, source_target_pairs={{0,4},{4,8},{8,12},{12,14},{14,10},{10,6},{6,2},{2,0},{1,5},{5,9},... | collective-permute-start | bytes 393224 | tf_op jit(solution)/shard_map/ppermute | solution.py:446
  13.3 6.9 %collective-permute-start.7 = (bf16[2,256,128]{2,1,0:T(8,128)(2,1)S(1)}, bf16[2,256,128]{2,1,0:T(8,128)(2,1)S(1)}, u32[]{:S(2)}, u32[]{:S(2)}) collective-permute-start(bf16[2,256,128]{2,1,0:T(8,128)(2,1)S(1)} %collective-permute-done.5), channel_id=1, source_target_pairs={{4,0},{8,4},{12,8},{14,12},{10,14},{6,10},{2,6},{0,2},{5,1},{9,5},... | collective-permute-start | bytes 393224 | tf_op jit(solution)/shard_map/ppermute | solution.py:447
  15.5 5.7 %collective-permute-start.8 = (bf16[2,256,128]{2,1,0:T(8,128)(2,1)S(1)}, bf16[2,256,128]{2,1,0:T(8,128)(2,1)S(1)}, u32[]{:S(2)}, u32[]{:S(2)}) collective-permute-start(bf16[2,256,128]{2,1,0:T(8,128)(2,1)S(1)} %collective-permute-done.2), channel_id=1, source_target_pairs={{0,4},{4,8},{8,12},{12,14},{14,10},{10,6},{6,2},{2,0},{1,5},{5,9},... | collective-permute-start | bytes 393224 | tf_op jit(solution)/shard_map/ppermute | solution.py:446
  17.3 5.7 %collective-permute-start.9 = (bf16[2,256,128]{2,1,0:T(8,128)(2,1)S(1)}, bf16[2,256,128]{2,1,0:T(8,128)(2,1)S(1)}, u32[]{:S(2)}, u32[]{:S(2)}) collective-permute-start(bf16[2,256,128]{2,1,0:T(8,128)(2,1)S(1)} %collective-permute-done.3), channel_id=1, source_target_pairs={{4,0},{8,4},{12,8},{14,12},{10,14},{6,10},{2,6},{0,2},{5,1},{9,5},... | collective-permute-start | bytes 393224 | tf_op jit(solution)/shard_map/ppermute | solution.py:447
  18.3 5.2 %collective-permute-start.12 = (bf16[2,256,128]{2,1,0:T(8,128)(2,1)S(1)}, bf16[2,256,128]{2,1,0:T(8,128)(2,1)S(1)}, u32[]{:S(2)}, u32[]{:S(2)}) collective-permute-start(bf16[2,256,128]{2,1,0:T(8,128)(2,1)S(1)} %collective-permute-done.6), channel_id=1, source_target_pairs={{0,4},{4,8},{8,12},{12,14},{14,10},{10,6},{6,2},{2,0},{1,5},{5,9},... | collective-permute-start | bytes 393224 | tf_op jit(solution)/shard_map/ppermute | solution.py:446
  20.2 5.2 %collective-permute-start.13 = (bf16[2,256,128]{2,1,0:T(8,128)(2,1)S(1)}, bf16[2,256,128]{2,1,0:T(8,128)(2,1)S(1)}, u32[]{:S(2)}, u32[]{:S(2)}) collective-permute-start(bf16[2,256,128]{2,1,0:T(8,128)(2,1)S(1)} %collective-permute-done.7), channel_id=1, source_target_pairs={{4,0},{8,4},{12,8},{14,12},{10,14},{6,10},{2,6},{0,2},{5,1},{9,5},... | collective-permute-start | bytes 393224 | tf_op jit(solution)/shard_map/ppermute | solution.py:447
  21.3 4.5 %collective-permute-start.10 = (bf16[1,256,128]{2,1,0:T(8,128)(2,1)S(1)}, bf16[1,256,128]{2,1,0:T(8,128)(2,1)S(1)}, u32[]{:S(2)}, u32[]{:S(2)}) collective-permute-start(bf16[1,256,128]{2,1,0:T(8,128)(2,1)S(1)} %slice.26), channel_id=1, source_target_pairs={{0,4},{4,8},{8,12},{12,14},{14,10},{10,6},{6,2},{2,0},{1,5},{5,9},... | collective-permute-start | bytes 196616 | tf_op jit(solution)/shard_map/ppermute | solution.py:452
  23.5 8.8 %collective-permute-start.16 = (bf16[2,5,2,256,128]{4,3,2,1,0:T(8,128)(2,1)S(1)}, bf16[2,5,2,256,128]{4,3,2,1,0:T(8,128)(2,1)S(1)}, u32[]{:S(2)}, u32[]{:S(2)}) collective-permute-start(bf16[2,5,2,256,128]{4,3,2,1,0:T(8,128)(2,1)S(1)} %pad_maximum_fusion.own0), channel_id=1, source_target_pairs={{0,1},{1,0},{2,3},{3,2},{4,5},{5,4},{6,7},{7,6},{8,9},{9,8},{10,11... | collective-permute-start | bytes 3932168 | tf_op jit(solution)/shard_map/ppermute | solution.py:459
  23.6 4.7 %collective-permute-start.14 = (bf16[1,256,128]{2,1,0:T(8,128)(2,1)S(1)}, bf16[1,256,128]{2,1,0:T(8,128)(2,1)S(1)}, u32[]{:S(2)}, u32[]{:S(2)}) collective-permute-start(bf16[1,256,128]{2,1,0:T(8,128)(2,1)S(1)} %slice.28), channel_id=1, source_target_pairs={{0,4},{4,8},{8,12},{12,14},{14,10},{10,6},{6,2},{2,0},{1,5},{5,9},... | collective-permute-start | bytes 196616 | tf_op jit(solution)/shard_map/ppermute | solution.py:452
  44.1 18.5 %collective-permute-start.19 = (f32[2,2,2,32,128]{4,3,2,1,0:T(8,128)S(1)}, f32[2,2,2,32,128]{4,3,2,1,0:T(8,128)S(1)}, u32[]{:S(2)}, u32[]{:S(2)}) collective-permute-start(f32[2,2,2,32,128]{4,3,2,1,0:T(8,128)S(1)} %get-tuple-element.38), channel_id=1, source_target_pairs={{0,4},{2,6},{4,8},{6,10},{8,12},{10,14},{12,0},{14,2},{1,5},{3,7},... | collective-permute-start | bytes 393224 | tf_op jit(solution)/shard_map/ppermute | solution.py:384
  44.2 18.5 %collective-permute-start.20 = (f32[2,2,2,32,128]{4,3,2,1,0:T(8,128)S(1)}, f32[2,2,2,32,128]{4,3,2,1,0:T(8,128)S(1)}, u32[]{:S(2)}, u32[]{:S(2)}) collective-permute-start(f32[2,2,2,32,128]{4,3,2,1,0:T(8,128)S(1)} %get-tuple-element.37), channel_id=1, source_target_pairs={{0,8},{2,10},{4,12},{6,14},{8,0},{10,2},{12,4},{14,6},{1,9},{3,11}... | collective-permute-start | bytes 393224 | tf_op jit(solution)/shard_map/ppermute | solution.py:384
  48.5 14.2 %collective-permute-start.21 = (f32[2,2,2,32,128]{4,3,2,1,0:T(8,128)S(1)}, f32[2,2,2,32,128]{4,3,2,1,0:T(8,128)S(1)}, u32[]{:S(2)}, u32[]{:S(2)}) collective-permute-start(f32[2,2,2,32,128]{4,3,2,1,0:T(8,128)S(1)} %get-tuple-element.36), channel_id=1, source_target_pairs={{0,12},{2,14},{4,0},{6,2},{8,4},{10,6},{12,8},{14,10},{1,13},{3,15... | collective-permute-start | bytes 393224 | tf_op jit(solution)/shard_map/ppermute | solution.py:384
  62.7 4.3 %collective-permute-start.22 = (f32[2,2,32,128]{3,2,1,0:T(8,128)S(1)}, f32[2,2,32,128]{3,2,1,0:T(8,128)S(1)}, u32[]{:S(2)}, u32[]{:S(2)}) collective-permute-start(f32[2,2,32,128]{3,2,1,0:T(8,128)S(1)} %dynamic-slice_bitcast_fusion.3), channel_id=1, source_target_pairs={{0,2},{2,0},{4,6},{6,4},{8,10},{10,8},{12,14},{14,12},{1,3},{3,1},... | collective-permute-start | bytes 196616 | tf_op jit(solution)/shard_map/ppermute | solution.py:391
  67.1 11.9 %collective-permute-start.27 = (f32[2,2,1536,128]{3,2,1,0:T(8,128)}, f32[2,2,1536,128]{3,2,1,0:T(8,128)S(1)}, u32[]{:S(2)}, u32[]{:S(2)}) collective-permute-start(f32[2,2,1536,128]{3,2,1,0:T(8,128)} %get-tuple-element.33), channel_id=1, source_target_pairs={{0,1},{1,0},{2,3},{3,2},{4,5},{5,4},{6,7},{7,6},{8,9},{9,8},{10,11... | collective-permute-start | bytes 9437192 | tf_op jit(solution)/shard_map/ppermute | solution.py:466
  70.0 6.8 %collective-permute-start.23 = (f32[2,2,32,128]{3,2,1,0:T(8,128)S(1)}, f32[2,2,32,128]{3,2,1,0:T(8,128)S(1)}, u32[]{:S(2)}, u32[]{:S(2)}) collective-permute-start(f32[2,2,32,128]{3,2,1,0:T(8,128)S(1)} %bitcast_add_fusion.1.refs_0_), channel_id=1, source_target_pairs={{0,4},{2,6},{4,8},{6,10},{8,12},{10,14},{12,0},{14,2},{1,5},{3,7},... | collective-permute-start | bytes 196616 | tf_op jit(solution)/shard_map/ppermute | solution.py:412
  70.1 8.5 %collective-permute-start.24 = (f32[2,2,32,128]{3,2,1,0:T(8,128)S(1)}, f32[2,2,32,128]{3,2,1,0:T(8,128)S(1)}, u32[]{:S(2)}, u32[]{:S(2)}) collective-permute-start(f32[2,2,32,128]{3,2,1,0:T(8,128)S(1)} %bitcast_add_fusion.1.refs_0_), channel_id=1, source_target_pairs={{0,8},{2,10},{4,12},{6,14},{8,0},{10,2},{12,4},{14,6},{1,9},{3,11}... | collective-permute-start | bytes 196616 | tf_op jit(solution)/shard_map/ppermute | solution.py:412
  70.9 7.7 %collective-permute-start.25 = (f32[2,2,32,128]{3,2,1,0:T(8,128)S(1)}, f32[2,2,32,128]{3,2,1,0:T(8,128)S(1)}, u32[]{:S(2)}, u32[]{:S(2)}) collective-permute-start(f32[2,2,32,128]{3,2,1,0:T(8,128)S(1)} %bitcast_add_fusion.1.refs_0_), channel_id=1, source_target_pairs={{0,12},{2,14},{4,0},{6,2},{8,4},{10,6},{12,8},{14,10},{1,13},{3,15... | collective-permute-start | bytes 196616 | tf_op jit(solution)/shard_map/ppermute | solution.py:412
  78.6 6.8 %collective-permute-start.26 = (f32[4,2,2,32,128]{4,3,2,1,0:T(8,128)S(1)}, f32[4,2,2,32,128]{4,3,2,1,0:T(8,128)S(1)}, u32[]{:S(2)}, u32[]{:S(2)}) collective-permute-start(f32[4,2,2,32,128]{4,3,2,1,0:T(8,128)S(1)} %pad_maximum_fusion.2), channel_id=1, source_target_pairs={{0,2},{2,0},{4,6},{6,4},{8,10},{10,8},{12,14},{14,12},{1,3},{3,1},... | collective-permute-start | bytes 786440 | tf_op jit(solution)/shard_map/ppermute | solution.py:413
  (6 other events, 30.4 us)
